TPU v7x, 512 devices: a whole 4x4x16 slice. The times are simulated.
512 devices in a mesh: dom: 64 (over x_lo, z, core), cls: 8 (over x_hi, y).
Axes of the slice: x: 4 (x_hi: 2, x_lo: 2; x = x_hi * 2 + x_lo), y: 4, z: 16, core: 2. Of those that a mesh axis runs over, the one named last changes fastest.
Arguments:
- particles: bfloat16 [1024, 64, 288], P(('dom', 'cls')), may hold values from -200 to 200
- group_ids: int32 [1024], P(('dom', 'cls')), may hold values from 0 to 31
- ctf_table: float32 [32, 64], replicated, may hold values from 0.1 to 1
- references: bfloat16 [400, 64, 288], P('cls'), may hold values from -4 to 4
Outputs:
- new_references: bfloat16 [400, 64, 288], P('cls')
All inputs are finite; a program needn't handle non-finite values.
Results may differ from a plain program's by a relative error of at most 0.0075.
The roundings to bfloat16 on the way count: a program that leaves them out, or rounds other values in their place, can miss the bound.
Values may be sent and summed in bfloat16 or wider, within the bound.
No kernel may reach another device: no remote copies, remote signals or barrier semaphores. Data moves between devices by JAX's collectives and lax.ppermute only.
A program may use at most 128 MiB of HBM per device.

v0:
```python
import math

import jax
import jax.numpy as jnp
from jax import lax
from jax.sharding import PartitionSpec as P

CYCLES = 64
ANG = 288
ROT = 72
GROUPS = 32


PRIOR_WEIGHT = 1.0


def joined(value, axis, join):
    pieces = jax.tree.map(lambda part: lax.all_gather(part, axis), value)
    head = jax.tree.map(lambda part: part[0], pieces)
    tail = jax.tree.map(lambda part: part[1:], pieces)
    total, _ = lax.scan(lambda total, slab: (join(total, slab), None), head, tail)
    return total


def rounded(values):
    return lax.optimization_barrier(values.astype(jnp.bfloat16)).astype(jnp.float32)


def phase_table(rows, cols, factor):
    index = (
        jnp.arange(rows, dtype=jnp.int32)[:, None]
        * factor
        * jnp.arange(cols, dtype=jnp.int32)[None, :]
        % ANG
    )
    return 2.0 * math.pi * index.astype(jnp.float32) / ANG


def combine_parts(first, second):
    top = jnp.maximum(first[0], second[0])
    return (top, first[1] * jnp.exp(first[0] - top) + second[1] * jnp.exp(second[0] - top))


def body(particles, group_ids, ctf_table, references):
    highest = lax.Precision.HIGHEST
    freqs = ANG // 2 + 1
    kd = references.shape[0]
    cycles = CYCLES
    forward_phase = phase_table(ANG, freqs, 1)
    forward = jnp.concatenate([jnp.cos(forward_phase), jnp.sin(forward_phase)], axis=1)
    rot_phase = phase_table(freqs, ROT, ANG // ROT)
    cos_rot = jnp.cos(rot_phase)
    sin_rot = jnp.sin(rot_phase)
    freq = jnp.arange(freqs, dtype=jnp.int32)
    scale = jnp.where((freq == 0) | (freq == ANG // 2), 1.0, 2.0).astype(jnp.float32) / ANG
    cos_weighted = cos_rot * scale[:, None]
    sin_weighted = sin_rot * scale[:, None]
    ref_float = references.astype(jnp.float32)
    ref_spec = jnp.dot(ref_float.reshape(kd * cycles, ANG), forward, precision=highest)
    ref_spec = ref_spec.reshape(kd, cycles, 2 * freqs).astype(jnp.bfloat16)
    ref_ct = ref_spec[:, :, :freqs].transpose(2, 1, 0)
    ref_st = ref_spec[:, :, freqs:].transpose(2, 1, 0)
    ref_matrix = jnp.concatenate(
        [jnp.concatenate([ref_ct, ref_st], axis=2), jnp.concatenate([ref_st, -ref_ct], axis=2)],
        axis=1,
    )
    power = jnp.sum(ref_float * ref_float, axis=-1)
    raw, ids = (
        lax.all_gather(particles, "cls", axis=0, tiled=True),
        lax.all_gather(group_ids, "cls", axis=0, tiled=True),
    )
    onehot = (ids[:, None] == jnp.arange(GROUPS, dtype=jnp.int32)[None, :]).astype(jnp.float32)
    ctf = jnp.dot(onehot, ctf_table, precision=highest)
    count = raw.shape[0]
    block = math.gcd(count, 16)

    def one_block(inputs):
        rows, factors = inputs
        spec = jnp.dot(
            rows.astype(jnp.float32).reshape(block * cycles, ANG), forward, precision=highest
        )
        spec = spec.reshape(block, cycles, 2, freqs) * factors[:, :, None, None]
        return spec.astype(jnp.bfloat16)

    spec = lax.map(
        one_block,
        (
            raw.reshape(count // block, block, cycles, ANG),
            ctf.reshape(count // block, block, cycles),
        ),
    )
    spec = spec.reshape(count, cycles, 2, freqs)
    ydata = spec.transpose(3, 0, 2, 1).reshape(freqs, count, 2 * cycles)
    paired = jnp.einsum("mpj,mjn->mpn", ydata, ref_matrix, preferred_element_type=jnp.float32)
    cross = jnp.einsum("mpk,mr->pkr", paired[:, :, :kd], cos_weighted, precision=highest)
    cross = cross - jnp.einsum("mpk,mr->pkr", paired[:, :, kd:], sin_weighted, precision=highest)
    ctf_square = ctf * ctf
    energy = jnp.dot(ctf_square, power.T, precision=highest)
    score = 4.0 / math.sqrt(CYCLES * ANG) * (cross - 0.5 * energy[:, :, None])
    top_local = jnp.max(score, axis=(1, 2))
    total_local = jnp.sum(jnp.exp(score - top_local[:, None, None]), axis=(1, 2))
    top_all, total_all = joined((top_local, total_local), "cls", combine_parts)
    post = jnp.exp(score - top_all[:, None, None]) / total_all[:, None, None]
    q_both = jnp.concatenate(
        [
            jnp.einsum("pkr,mr->mpk", post, cos_rot, precision=highest),
            jnp.einsum("pkr,mr->mpk", post, sin_rot, precision=highest),
        ],
        axis=2,
    ).astype(jnp.bfloat16)
    grams = jnp.einsum("mpi,mpj->mij", q_both, ydata, preferred_element_type=jnp.float32)
    sum_c = grams[:, :kd, :cycles] + grams[:, kd:, cycles:]
    sum_s = grams[:, :kd, cycles:] - grams[:, kd:, :cycles]
    totals = jnp.stack([sum_c, sum_s])
    weight = jnp.einsum("pk,pr->kr", jnp.sum(post, axis=2), ctf_square, precision=highest)
    totals, weight = lax.psum((totals, weight), "dom")
    hat = rounded(totals / (weight[None, None, :, :] + PRIOR_WEIGHT))
    inverse_phase = phase_table(freqs, ANG, 1)
    inv_cos = jnp.cos(inverse_phase) * scale[:, None]
    inv_sin = jnp.sin(inverse_phase) * scale[:, None]
    result = jnp.einsum("mkr,ma->kra", hat[0], inv_cos, precision=highest) + jnp.einsum(
        "mkr,ma->kra", hat[1], inv_sin, precision=highest
    )
    return result.astype(jnp.bfloat16)


def solution(mesh):
    in_specs = (P(("dom", "cls"), None, None), P(("dom", "cls")), P(), P("cls", None, None))
    out_specs = P("cls", None, None)
    return jax.shard_map(body, mesh=mesh, in_specs=in_specs, out_specs=out_specs, check_vma=False)
```

profile of v0, /device:TPU:1, one launch (start us, length us, event | category | flops | bytes accessed | tf_op | source)
XLA Modules:
  0.0 627.7 jit_solution(13764335772919790876)
XLA Ops:
  7.5 1.3 dynamic-slice.2
  11.0 11.6 %all-reduce = s32[16]{0:T(128)S(1)} all-reduce(s32[16]{0:T(128)S(1)} %dynamic-update-slice), channel_id=1, replica_groups=mesh['dom'=64,'cls'=8] {'cls'}, use_global_device_ids=true, to_apply=%add | all-reduce | flops 16 | bytes 128
  22.6 2.3 multiply_reduce_fusion
  25.0 30.1 %all_gather.18 = bf16[16,64,288]{2,1,0:T(8,128)(2,1)S(1)} all-gather(bf16[2,64,288]{2,1,0:T(8,128)(2,1)S(1)} %copy-done.3), channel_id=1, replica_groups=mesh['dom'=64,'cls'=8] {'cls'}, dimensions={0}, use_global_device_ids=true | all-gather | bytes 663552 | tf_op jit(solution)/shard_map/all_gather | solution.py:69
  55.4 1.9 fusion.19
  57.3 1.3 copy.17
  59.2 7.5 %fusion.5 = bf16[3200,290]{0,1:T(8,128)(2,1)} fusion(bf16[3200,288]{1,0:T(8,128)(2,1)} %bitcast.73, f32[288,145]{0,1:T(8,128)S(1)} %get-tuple-element.74, f32[288,145]{0,1:T(8,128)S(1)} %get-tuple-element.75), kind=kOutput, calls=%fused_computation.10 | convolution fusion | flops 3208179456 | bytes 4033280 | tf_op jit(solution)/shard_map/dot_general | solution.py:59
  66.6 3.6 copy.18
  70.3 2.6 fusion.127
  72.8 4.6 copy.28
  77.5 4.2 copy.27
  83.2 2.9 fusion.8
  86.5 2.8 fusion.20
  89.4 3.0 fusion.129
  93.2 15.7 %all-reduce.3 = (f32[128]{0:T(128)S(1)}, f32[128]{0:T(128)S(1)}) all-reduce(f32[128]{0:T(128)S(1)} %dynamic-update-slice.1, f32[128]{0:T(128)S(1)} %dynamic-update-slice.2), channel_id=2, replica_groups=mesh['dom'=64,'cls'=8] {'cls'}, use_global_device_ids=true, to_apply=%add.1 | all-reduce | flops 256 | bytes 2048
  109.4 1.2 convolution_convert_fusion.2
  112.7 5.3 fusion.130
  118.0 10.0 %fusion.7 = (f32[1,145,50,64]{3,2,1,0:T(8,128)S(1)}, f32[1,145,50,64]{3,2,1,0:T(8,128)}) fusion(f32[145,100,128]{2,1,0:T(8,128)} %fusion.130), kind=kLoop, calls=%fused_computation.16 | loop fusion | flops 928000 | bytes 11136000 | tf_op jit(solution)/shard_map/stack | solution.py:114
  128.0 5.9 pad_maximum_fusion
  134.4 223.9 %psum.15 = f32[50,64]{1,0:T(8,128)S(1)} all-reduce(f32[50,64]{1,0:T(8,128)S(1)} %fusion.100), channel_id=1, replica_groups=mesh['dom'=64,'cls'=8] {'dom'}, use_global_device_ids=true, to_apply=%region_7.8 | all-reduce | flops 3200 | bytes 25600 | tf_op jit(solution)/shard_map/psum | solution.py:116
  358.4 247.1 %all-reduce.6.cloned.1.call-done = f32[2,145,50,64]{3,2,1,0:T(8,128)} async-done(((f32[2,145,50,64]{3,2,1,0:T(8,128)}), f32[2,145,50,64]{3,2,1,0:T(8,128)}) %all-reduce.6.cloned.1.call-update) | async-done | bytes 3712016 | tf_op jit(solution)/shard_map/psum | solution.py:116
  605.4 4.0 divide_convert_fusion
  610.2 4.3 fusion.17
  614.5 5.9 add_convert_fusion
  (46 shorter events, 9.6 us)
Async XLA Ops:
  6.5 48.6 %copy-start = (f32[32,64]{1,0:T(8,128)S(1)}, f32[32,64]{1,0:T(8,128)}, u32[]{:S(2)}) copy-start(f32[32,64]{1,0:T(8,128)} %param.8) | copy-start | bytes 24580
  6.5 18.4 %copy-start.3 = (bf16[2,64,288]{2,1,0:T(8,128)(2,1)S(1)}, bf16[2,64,288]{2,1,0:T(8,128)(2,1)}, u32[]{:S(2)}) copy-start(bf16[2,64,288]{2,1,0:T(8,128)(2,1)} %param.6) | copy-start | bytes 221188
  6.5 598.9 %all-reduce.6.cloned.1.call-start = ((), (), s32[]{:S(2)}) async-start(), calls=%async_computation | async-start | bytes 16629760 | tf_op jit(solution)/shard_map/psum | solution.py:116
  81.7 1.6 copy-start.2
  614.5 6.0 copy-start.1
Sparse Core Ops, SparseCore 0:
  134.0 471.3 all-reduce.5
where the time goes:
time: 635 us; the launch traced here: 628 us
  blocking collectives  281 us (44%)
  waiting for transfers between devices  247 us (39%)
  matrix products  36.5 us (6%)
  other arithmetic  24.7 us (4%)
  local copies, waits for them, and re-layouts  22.6 us (4%)
  between operations  15.3 us (2%)
    psum x1, waiting for transfers between devices, body(): totals, weight = lax.psum((totals, weight), 'dom')  247 us
    psum x1, blocking collectives, body(): totals, weight = lax.psum((totals, weight), 'dom')  224 us
    all_gather x1, blocking collectives, body(): lax.all_gather(particles, 'cls', axis=0, tiled=True)  30.1 us
    unnamed x2, blocking collectives  27.3 us
    another operation x2, other arithmetic, body(): totals = jnp.stack([sum_c, sum_s])  15.9 us
  transfers between devices with their start and end apart: 1, of which 1 were waited for; matrix products, arithmetic and copies ran while one was open for 0% of the time, Pallas kernels for 0%

commit v1 on v0

v1 whole, which is shorter than its diff:
```python
import math

import jax
import jax.numpy as jnp
from jax import lax
from jax.sharding import Mesh
from jax.sharding import PartitionSpec as P

CYCLES = 64
ANG = 288
ROT = 72
GROUPS = 32
HALF = ANG // 2
LANES = 2 * CYCLES
PRIOR_WEIGHT = 1.0

X, Z, CORE = 2, 16, 2
CHUNK = 113
SLOT = 128

DOM = ("x_lo", "z", "core")
CLS = ("x_hi", "y")
SHARE = ("core", "x_hi", "y")


def phase(rows, cols, factor):
    index = jnp.arange(rows, dtype=jnp.int32)[:, None] * factor * jnp.arange(cols, dtype=jnp.int32)[None, :]
    return 2.0 * math.pi * (index % ANG).astype(jnp.float32) / ANG


def forward_table():
    angle = phase(ANG, HALF + 1, 1)
    cos, sin = jnp.cos(angle), jnp.sin(angle)
    return jnp.concatenate([cos[:, :HALF], cos[:, HALF:], sin[:, 1:HALF]], axis=1)


def inverse_table():
    angle = phase(HALF + 1, ANG, 1)
    cos, sin = jnp.cos(angle), jnp.sin(angle)
    real = jnp.concatenate([cos[:1], 2.0 * cos[1:HALF]], axis=0) / ANG
    imag = jnp.concatenate([cos[HALF:], 2.0 * sin[1:HALF]], axis=0) / ANG
    return real, imag


def narrow(values):
    return lax.optimization_barrier(values.astype(jnp.bfloat16))


def parts(values):
    high = narrow(values)
    low = (values - high.astype(jnp.float32)).astype(jnp.bfloat16)
    return jnp.concatenate([high, low], axis=-1)


def spectra(images):
    rows = images.astype(jnp.float32).reshape(-1, ANG)
    spec = jnp.dot(rows, forward_table(), precision=lax.Precision.HIGHEST)
    return spec.reshape(images.shape[0], CYCLES, 2, HALF)


def swap(axis, value):
    return lax.ppermute(value, axis, [(0, 1), (1, 0)])


def both(axis, mine):
    other = swap(axis, mine)
    first = lax.axis_index(axis) == 0
    return jnp.stack([jnp.where(first, mine, other), jnp.where(first, other, mine)])


def body(particles, group_ids, ctf_table, references):
    highest = lax.Precision.HIGHEST
    core, x_lo, z = (lax.axis_index(name) for name in ("core", "x_lo", "z"))
    kd = references.shape[0] // CORE
    mine = particles.shape[0]

    def factors(ids):
        onehot = (ids[:, None] == jnp.arange(GROUPS, dtype=jnp.int32)[None, :]).astype(jnp.float32)
        return jnp.dot(onehot, ctf_table, precision=highest)

    own = spectra(particles) * factors(group_ids)[:, :, None, None]
    own = own.astype(jnp.bfloat16).transpose(0, 3, 2, 1).reshape(mine * HALF, LANES)
    tags = jnp.broadcast_to(group_ids.astype(jnp.bfloat16)[:, None], (mine, LANES))
    tags = jnp.pad(tags, ((0, 16 - mine), (0, 0)))
    message = jnp.concatenate([own, tags], axis=0)
    shares = CORE * 8
    gathered = lax.all_to_all(
        jnp.broadcast_to(message[None], (shares,) + message.shape), SHARE, 0, 0, tiled=True
    )
    ydata = gathered[:, : mine * HALF].reshape(shares * mine, HALF, LANES).transpose(1, 0, 2)
    ids = gathered[:, mine * HALF : mine * HALF + mine, 0].reshape(-1).astype(jnp.int32)
    ctf_square = factors(ids) ** 2

    refs = lax.dynamic_slice_in_dim(references, core * kd, kd, 0)
    ref_float = refs.astype(jnp.float32)
    power = jnp.sum(ref_float * ref_float, axis=-1)
    ref_spec = spectra(refs).astype(jnp.bfloat16).transpose(3, 0, 2, 1)
    straight = ref_spec.reshape(HALF, kd, LANES)
    turned = jnp.concatenate([ref_spec[:, :, 1], -ref_spec[:, :, 0]], axis=2)
    paired = jnp.einsum(
        "jpl,jkl->jpk",
        ydata,
        jnp.concatenate([straight, turned], axis=1),
        preferred_element_type=jnp.float32,
    )
    angle = phase(HALF, ROT, ANG // ROT)
    cos_rot, sin_rot = jnp.cos(angle), jnp.sin(angle)
    scale = jnp.where(jnp.arange(HALF) == 0, 1.0, 2.0).astype(jnp.float32)[:, None] / ANG
    cross = jnp.einsum("jpk,jr->pkr", paired[:, :, :kd], cos_rot * scale, precision=highest)
    cross = cross - jnp.einsum("jpk,jr->pkr", paired[:, :, kd:], sin_rot * scale, precision=highest)
    energy = jnp.dot(ctf_square, power.T, precision=highest)
    score = 4.0 / math.sqrt(CYCLES * ANG) * (cross - 0.5 * energy[:, :, None])
    top = jnp.max(score, axis=(1, 2))
    expo = jnp.exp(score - top[:, None, None])
    by_class = jnp.sum(expo, axis=2)
    total = jnp.sum(by_class, axis=1)
    stats = jnp.concatenate([top[None], total[None]], axis=0)
    stats = lax.all_to_all(
        jnp.broadcast_to(stats[None], (shares,) + stats.shape), SHARE, 0, 0, tiled=True
    )
    top_all = jnp.max(stats[:, 0], axis=0)
    total_all = jnp.sum(stats[:, 1] * jnp.exp(stats[:, 0] - top_all[None]), axis=0)
    share = jnp.exp(top - top_all) / total_all
    post = expo * share[:, None, None]
    q_cos = jnp.einsum("pkr,jr->jpk", post, cos_rot, precision=highest).astype(jnp.bfloat16)
    q_sin = jnp.einsum("pkr,jr->jpk", post, sin_rot, precision=highest).astype(jnp.bfloat16)
    yturned = jnp.concatenate([ydata[:, :, CYCLES:], -ydata[:, :, :CYCLES]], axis=2)
    sums = jnp.einsum(
        "jpk,jpl->kjl",
        jnp.concatenate([q_cos, q_sin], axis=1),
        jnp.concatenate([ydata, yturned], axis=1),
        preferred_element_type=jnp.float32,
    )
    weight = jnp.einsum("pk,pr->kr", by_class * share[:, None], ctf_square, precision=highest)

    chunks = X * Z
    sums = jnp.pad(sums.reshape(kd * HALF, LANES), ((0, chunks * CHUNK - kd * HALF), (0, 0)))
    sums = sums.reshape(X, Z, CHUNK, LANES)
    first = jnp.minimum(jnp.arange(chunks, dtype=jnp.int32) * CHUNK // HALF, kd - 1)
    second = jnp.minimum(first + 1, kd - 1)
    weights = jnp.stack([weight[first], weight[second]], axis=1).reshape(X, Z, 2, CYCLES)

    def packed(values, scales):
        rows = jnp.concatenate([values.astype(jnp.bfloat16), parts(scales)], axis=-2)
        return jnp.pad(rows, ((0, 0),) * (rows.ndim - 2) + ((0, SLOT - CHUNK - 2), (0, 0)))

    def unpacked(rows):
        rows = rows.astype(jnp.float32)
        scales = rows[..., CHUNK : CHUNK + 2, :]
        return rows[..., :CHUNK, :], scales[..., :CYCLES] + scales[..., CYCLES:]

    def half(values, index):
        return lax.dynamic_index_in_dim(values, index, 0, keepdims=False)

    got, got_scale = unpacked(swap("x_lo", packed(half(sums, 1 - x_lo), half(weights, 1 - x_lo))))
    sent = packed(half(sums, x_lo) + got, half(weights, x_lo) + got_scale)
    got, got_scale = unpacked(lax.all_to_all(sent, "z", 0, 0, tiled=True))
    got, got_scale = jnp.sum(got, axis=0), jnp.sum(got_scale, axis=0) + PRIOR_WEIGHT
    chunk = x_lo * Z + z
    row_class = (chunk * CHUNK + jnp.arange(CHUNK, dtype=jnp.int32)) // HALF
    lead = (row_class == jnp.minimum(chunk * CHUNK // HALF, kd - 1))[:, None]
    scale_rows = jnp.where(lead, got_scale[:1], got_scale[1:])
    hat = (got / jnp.concatenate([scale_rows, scale_rows], axis=1)).astype(jnp.bfloat16)
    hat = jnp.pad(hat, ((0, SLOT - CHUNK), (0, 0)))

    hats = lax.all_to_all(jnp.broadcast_to(hat[None], (Z,) + hat.shape), "z", 0, 0, tiled=True)
    hats = both("core", both("x_lo", hats))
    hats = hats[..., :CHUNK, :].reshape(CORE, chunks * CHUNK, LANES)[:, : kd * HALF]
    hats = hats.reshape(CORE * kd, HALF, LANES).astype(jnp.float32)
    real, imag = inverse_table()
    result = jnp.einsum("kjc,ja->kca", hats[..., :CYCLES], real, precision=highest)
    result = result + jnp.einsum("kjc,ja->kca", hats[..., CYCLES:], imag, precision=highest)
    return result.astype(jnp.bfloat16)


def solution(mesh):
    fine = Mesh(mesh.devices.reshape(X, Z, CORE, 2, 4), DOM + CLS)
    in_specs = (P(DOM + CLS, None, None), P(DOM + CLS), P(), P(CLS, None, None))
    return jax.shard_map(body, mesh=fine, in_specs=in_specs, out_specs=P(CLS, None, None), check_vma=False)
```

time: 635 us -> 199 us (0.31); the launches traced: 628 us -> 199 us
  blocking collectives: 281 us -> 34.8 us
  waiting for transfers between devices: 247 us -> 55.1 us
  starting transfers between devices: 0.01 us -> 41.5 us
  between operations: 15.3 us -> 0.57 us
  matrix products: 36.5 us -> 23.6 us
  other arithmetic: 24.7 us -> 13.4 us
  local copies, waits for them, and re-layouts: 22.6 us -> 29.6 us
    psum x1 -> x0, waiting for transfers between devices: 247 us -> none  [body(): totals, weight = lax.psum((totals, weight), 'dom')]
    psum x1 -> x0, blocking collectives: 224 us -> none  [body(): totals, weight = lax.psum((totals, weight), 'dom')]
    all_to_all x0 -> x1, blocking collectives: none -> 34.8 us  [body(): lax.all_to_all(jnp.broadcast_to(hat[None], (Z,) + hat.shape), 'z', 0, 0,...]
    all_to_all x0 -> x3, waiting for transfers between devices: none -> 34.1 us  [the longest x1 22.8 us: body(): got, got_scale = unpacked(lax.all_to_all(sent, 'z', 0, 0, tiled=True))]
    all_gather x1 -> x0, blocking collectives: 30.1 us -> none  [body(): lax.all_gather(particles, 'cls', axis=0, tiled=True)]
    unnamed x2 -> x0, blocking collectives: 27.3 us -> none
    all_to_all x0 -> x3, starting transfers between devices: none -> 27.1 us  [the longest x1 12.3 us: body(): got, got_scale = unpacked(lax.all_to_all(sent, 'z', 0, 0, tiled=True))]
    ppermute x0 -> x3, waiting for transfers between devices: none -> 20.9 us  [swap(): return lax.ppermute(value, axis, [(0, 1), (1, 0)])]
  transfers between devices with their start and end apart: 1 -> 6, of which waited for: 1 -> 6; matrix products, arithmetic and copies ran while one was open for 0% -> 9% of each run, Pallas kernels for 0% -> 0%
where the time goes in v1:
time: 199 us
  waiting for transfers between devices  55.1 us (28%)
  starting transfers between devices  41.5 us (21%)
  blocking collectives  34.8 us (17%)
  local copies, waits for them, and re-layouts  29.6 us (15%)
  matrix products  23.6 us (12%)
  other arithmetic  13.4 us (7%)
    all_to_all x1, blocking collectives, body(): lax.all_to_all(jnp.broadcast_to(hat[None], (Z,) + hat.shape), 'z', 0, 0,...  34.8 us
    all_to_all x1, waiting for transfers between devices, body(): got, got_scale = unpacked(lax.all_to_all(sent, 'z', 0, 0, tiled=True))  22.8 us
    ppermute x3, waiting for transfers between devices, swap(): return lax.ppermute(value, axis, [(0, 1), (1, 0)])  20.9 us
    ppermute x3, starting transfers between devices, swap(): return lax.ppermute(value, axis, [(0, 1), (1, 0)])  14.4 us
    all_to_all x1, starting transfers between devices, body(): got, got_scale = unpacked(lax.all_to_all(sent, 'z', 0, 0, tiled=True))  12.3 us
    all_to_all x1, starting transfers between devices, body(): lax.all_to_all(jnp.broadcast_to(message[None], (shares,) + message.shape)...  11 us
    dot_general x1, matrix products, body(): jnp.einsum('kjc,ja->kca', hats[..., CYCLES:], imag, precision=highest)  6.26 us
    concatenate x1, local copies, waits for them, and re-layouts, body(): jnp.concatenate([straight, turned], axis=1)  6 us
  transfers between devices with their start and end apart: 6, of which 6 were waited for; matrix products, arithmetic and copies ran while one was open for 9% of the time, Pallas kernels for 0%

profile of v1, /device:TPU:1, one launch (start us, length us, event | category | flops | bytes accessed | tf_op | source)
XLA Modules:
  0.0 198.5 jit_solution(12102613945792725350)
XLA Ops:
  5.7 11.0 %all-to-all-start = ((bf16[16,304,128]{2,1,0:T(8,128)(2,1)}), bf16[16,304,128]{2,1,0:T(8,128)(2,1)}, u32[]{:S(2)}, u32[]{:S(2)}) async-start(bf16[16,304,128]{2,1,0:T(8,128)(2,1)} %broadcast_in_dim.37), calls=%async_computation | async-start | bytes 2490368 | tf_op jit(solution)/shard_map/all_to_all | solution.py:87
  16.8 4.0 %convolution_convert_fusion = bf16[25,64,2,144]{3,1,2,0:T(8,128)(2,1)S(1)} fusion(f32[2,144,288,1]{2,1,0,3:T(8,128)S(1)} %bitcast.116, bf16[50,64,288]{2,1,0:T(8,128)(2,1)} %param.7, s32[]{:T(128)S(6)} %select_n.141), kind=kOutput, calls=%fused_computation.15 | convolution fusion | flops 1592985600 | bytes 2482180 | tf_op jit(solution)/shard_map/dot_general | solution.py:57
  20.9 2.2 %maximum_maximum_fusion = bf16[144,50,128]{0,2,1:T(8,128)(2,1)} fusion(bf16[144,25,64]{0,2,1:T(8,128)(2,1)S(1)} %get-tuple-element.14, bf16[144,25,64]{0,2,1:T(8,128)(2,1)S(1)} %get-tuple-element.13, bf16[144,25,128]{0,2,1:T(8,128)(2,1)S(1)} %bitcast.109), kind=kLoop, calls=%fused_computation.3 | loop fusion | flops 5529600 | bytes 3686400 | tf_op jit(solution)/shard_map/concatenate | solution.py:103
  23.2 6.0 %copy.76 = bf16[144,50,128]{2,1,0:T(8,128)(2,1)S(1)} copy(bf16[144,50,128]{0,2,1:T(8,128)(2,1)} %maximum_maximum_fusion) | data formatting | bytes 3686400 | tf_op jit(solution)/shard_map/concatenate | solution.py:103
  29.2 1.6 multiply_reduce_fusion
  30.9 5.8 %all-to-all-done = bf16[16,304,128]{2,1,0:T(8,128)(2,1)} async-done(((bf16[16,304,128]{2,1,0:T(8,128)(2,1)}), bf16[16,304,128]{2,1,0:T(8,128)(2,1)}, u32[]{:S(2)}, u32[]{:S(2)}) %all-to-all-start) | async-done | bytes 1245216 | tf_op jit(solution)/shard_map/all_to_all | solution.py:87
  41.2 3.0 %fusion.138 = (f32[144,32,25]{2,1,0:T(8,128)}, f32[144,32,25]{2,1,0:T(8,128)}) fusion(f32[144,32,50]{2,1,0:T(8,128)S(1)} %fusion.135), kind=kLoop, calls=%fused_computation.195 | loop fusion | bytes 1843200 | tf_op jit(solution)/shard_map/slice | solution.py:110
  44.2 2.8 %copy.78 = f32[144,32,25]{0,1,2:T(8,128)S(1)} copy(f32[144,32,25]{2,1,0:T(8,128)} %get-tuple-element.9) | data formatting | bytes 921600 | tf_op jit(solution)/shard_map/slice | solution.py:110
  47.1 2.9 %copy.77 = f32[144,32,25]{0,1,2:T(8,128)S(1)} copy(f32[144,32,25]{2,1,0:T(8,128)} %get-tuple-element.10) | data formatting | bytes 921600 | tf_op jit(solution)/shard_map/slice | solution.py:109
  53.3 3.8 %all-to-all-start.1 = ((f32[16,2,32]{2,1,0:T(2,128)}), f32[16,2,32]{2,1,0:T(2,128)S(1)}, u32[]{:S(2)}, u32[]{:S(2)}) async-start(f32[16,2,32]{2,1,0:T(2,128)} %broadcast_in_dim.42), calls=%async_computation.1 | async-start | bytes 32768 | tf_op jit(solution)/shard_map/all_to_all | solution.py:118
  57.1 1.8 fusion.139
  58.8 5.5 %all-to-all-done.1 = f32[16,2,32]{2,1,0:T(2,128)S(1)} async-done(((f32[16,2,32]{2,1,0:T(2,128)}), f32[16,2,32]{2,1,0:T(2,128)S(1)}, u32[]{:S(2)}, u32[]{:S(2)}) %all-to-all-start.1) | async-done | bytes 4128 | tf_op jit(solution)/shard_map/all_to_all | solution.py:118
  69.5 2.5 %fusion.9 = f32[25,144,128]{2,0,1:T(8,128)S(1)} fusion(bf16[144,64,25]{1,2,0:T(8,128)(2,1)S(1)} %copy.81, bf16[144,32,64]{2,1,0:T(8,128)(2,1)} %get-tuple-element.16, bf16[144,32,64]{2,1,0:T(8,128)(2,1)} %get-tuple-element.15, bf16[144,32,128]{2,1,0:T(8,128)(2,1)S(1)} %bitcast.111), kind=kOutput, calls=%fused_computation.16 | convolution fusion | flops 66060288 | bytes 4663296 | tf_op jit(solution)/shard_map/jpk,jpl->kjl/dot_general | solution.py:128
  76.1 1.9 collective-permute-start
  78.0 13.1 %collective-permute-done = bf16[16,128,128]{2,1,0:T(8,128)(2,1)S(1)} collective-permute-done((bf16[16,128,128]{2,1,0:T(8,128)(2,1)S(1)}, bf16[16,128,128]{2,1,0:T(8,128)(2,1)S(1)}, u32[]{:S(2)}, u32[]{:S(2)}) %collective-permute-start) | collective-permute-done | bytes 524320 | tf_op jit(solution)/shard_map/ppermute | solution.py:62
  92.3 12.3 %all-to-all-start.2 = ((bf16[16,128,128]{2,1,0:T(8,128)(2,1)}), bf16[16,128,128]{2,1,0:T(8,128)(2,1)S(1)}, u32[]{:S(2)}, u32[]{:S(2)}) async-start(bf16[16,128,128]{2,1,0:T(8,128)(2,1)} %fusion.24), calls=%async_computation.2 | async-start | bytes 1048576 | tf_op jit(solution)/shard_map/all_to_all | solution.py:157
  104.7 22.8 %all-to-all-done.2 = bf16[16,128,128]{2,1,0:T(8,128)(2,1)S(1)} async-done(((bf16[16,128,128]{2,1,0:T(8,128)(2,1)}), bf16[16,128,128]{2,1,0:T(8,128)(2,1)S(1)}, u32[]{:S(2)}, u32[]{:S(2)}) %all-to-all-start.2) | async-done | bytes 524320 | tf_op jit(solution)/shard_map/all_to_all | solution.py:157
  128.0 34.8 %all_to_all.20 = bf16[16,128,128]{2,1,0:T(8,128)(2,1)S(1)} all-to-all(bf16[16,128,128]{2,1,0:T(8,128)(2,1)S(1)} %broadcast_in_dim.57), channel_id=1, replica_groups=mesh['x_lo'=2,'z'=16,'core'=2,'x_hi'=2,'y'=4] {'z'}, dimensions={0} | all-to-all | bytes 1048576 | tf_op jit(solution)/shard_map/all_to_all | solution.py:166
  162.8 2.2 %collective-permute-start.1 = (bf16[16,128,128]{2,1,0:T(8,128)(2,1)S(1)}, bf16[16,128,128]{2,1,0:T(8,128)(2,1)S(1)}, u32[]{:S(2)}, u32[]{:S(2)}) collective-permute-start(bf16[16,128,128]{2,1,0:T(8,128)(2,1)S(1)} %all_to_all.20), channel_id=1, source_target_pairs={{0,256},{256,0},{1,257},{257,1},{2,258},{258,2},{3,259},{259,3},{4... | collective-permute-start | bytes 1572872 | tf_op jit(solution)/shard_map/ppermute | solution.py:62
  165.0 7.7 %collective-permute-done.1 = bf16[16,128,128]{2,1,0:T(8,128)(2,1)S(1)} collective-permute-done((bf16[16,128,128]{2,1,0:T(8,128)(2,1)S(1)}, bf16[16,128,128]{2,1,0:T(8,128)(2,1)S(1)}, u32[]{:S(2)}, u32[]{:S(2)}) %collective-permute-start.1) | collective-permute-done | bytes 524320 | tf_op jit(solution)/shard_map/ppermute | solution.py:62
  172.9 10.2 %collective-permute-start.2 = (bf16[2,16,128,128]{3,2,1,0:T(8,128)(2,1)S(1)}, bf16[2,16,128,128]{3,2,1,0:T(8,128)(2,1)S(1)}, u32[]{:S(2)}, u32[]{:S(2)}) collective-permute-start(bf16[2,16,128,128]{3,2,1,0:T(8,128)(2,1)S(1)} %pad_maximum_fusion.1), channel_id=1, source_target_pairs={{0,8},{8,0},{1,9},{9,1},{2,10},{10,2},{3,11},{11,3},{4,12},{12,4},... | collective-permute-start | bytes 3145736 | tf_op jit(solution)/shard_map/ppermute | solution.py:62
  185.5 1.9 copy.85
  189.0 3.2 %fusion.7 = f32[50,64,288]{2,1,0:T(8,128)S(1)} fusion(bf16[50,144,128]{2,1,0:T(8,128)(2,1)S(1)} %bitcast.106, f32[143,288]{1,0:T(8,128)S(1)} %slice_multiply_fusion, f32[1,288]{1,0:T(1,128)S(1)} %get-tuple-element.20), kind=kOutput, calls=%fused_computation.13 | convolution fusion | flops 1592607744 | bytes 5695488 | tf_op jit(solution)/shard_map/kjc,ja->kca/dot_general | solution.py:171
  192.2 6.3 %add_convert_fusion = bf16[50,64,288]{2,1,0:T(8,128)(2,1)} fusion(f32[50,64,288]{2,1,0:T(8,128)S(1)} %fusion.7, bf16[50,144,128]{2,1,0:T(8,128)(2,1)S(1)} %bitcast.107, f32[143,288]{1,0:T(8,128)S(1)} %fusion.43, f32[1,288]{1,0:T(1,128)S(1)} %get-tuple-element.19), kind=kOutput, calls=%fused_computation.2 | convolution fusion | flops 1594450944 | bytes 7538688 | tf_op jit(solution)/shard_map/kjc,ja->kca/dot_general | solution.py:172
  (87 shorter events, 28.6 us)
Async XLA Ops:
  0.0 3.5 %copy-start = (bf16[2,64,288]{2,1,0:T(8,128)(2,1)S(1)}, bf16[2,64,288]{2,1,0:T(8,128)(2,1)}, u32[]{:S(2)}) copy-start(bf16[2,64,288]{2,1,0:T(8,128)(2,1)} %param.4) | copy-start | bytes 221188
  5.7 30.9 %all-to-all-start = ((bf16[16,304,128]{2,1,0:T(8,128)(2,1)}), bf16[16,304,128]{2,1,0:T(8,128)(2,1)}, u32[]{:S(2)}, u32[]{:S(2)}) async-start(bf16[16,304,128]{2,1,0:T(8,128)(2,1)} %broadcast_in_dim.37), calls=%async_computation | async-start | bytes 2490368 | tf_op jit(solution)/shard_map/all_to_all | solution.py:87
  23.1 14.7 %copy-start.3 = (f32[32,64]{1,0:T(8,128)S(1)}, f32[32,64]{1,0:T(8,128)}, u32[]{:S(2)}) copy-start(f32[32,64]{1,0:T(8,128)} %param.6) | copy-start | bytes 24580
  53.3 11.1 %all-to-all-start.1 = ((f32[16,2,32]{2,1,0:T(2,128)}), f32[16,2,32]{2,1,0:T(2,128)S(1)}, u32[]{:S(2)}, u32[]{:S(2)}) async-start(f32[16,2,32]{2,1,0:T(2,128)} %broadcast_in_dim.42), calls=%async_computation.1 | async-start | bytes 32768 | tf_op jit(solution)/shard_map/all_to_all | solution.py:118
  74.6 16.6 %copy-start.2 = (f32[2,16,113,128]{3,2,1,0:T(8,128)S(1)}, f32[2,16,113,128]{3,2,1,0:T(8,128)}, u32[]{:S(2)}) copy-start(f32[2,16,113,128]{3,2,1,0:T(8,128)} %reshape.164) | copy-start | bytes 5554180
  76.1 15.0 %collective-permute-start = (bf16[16,128,128]{2,1,0:T(8,128)(2,1)S(1)}, bf16[16,128,128]{2,1,0:T(8,128)(2,1)S(1)}, u32[]{:S(2)}, u32[]{:S(2)}) collective-permute-start(bf16[16,128,128]{2,1,0:T(8,128)(2,1)S(1)} %fusion.25), channel_id=1, source_target_pairs={{0,256},{256,0},{1,257},{257,1},{2,258},{258,2},{3,259},{259,3},{4... | collective-permute-start | bytes 1572872 | tf_op jit(solution)/shard_map/ppermute | solution.py:62
  92.3 35.1 %all-to-all-start.2 = ((bf16[16,128,128]{2,1,0:T(8,128)(2,1)}), bf16[16,128,128]{2,1,0:T(8,128)(2,1)S(1)}, u32[]{:S(2)}, u32[]{:S(2)}) async-start(bf16[16,128,128]{2,1,0:T(8,128)(2,1)} %fusion.24), calls=%async_computation.2 | async-start | bytes 1048576 | tf_op jit(solution)/shard_map/all_to_all | solution.py:157
  162.8 9.9 %collective-permute-start.1 = (bf16[16,128,128]{2,1,0:T(8,128)(2,1)S(1)}, bf16[16,128,128]{2,1,0:T(8,128)(2,1)S(1)}, u32[]{:S(2)}, u32[]{:S(2)}) collective-permute-start(bf16[16,128,128]{2,1,0:T(8,128)(2,1)S(1)} %all_to_all.20), channel_id=1, source_target_pairs={{0,256},{256,0},{1,257},{257,1},{2,258},{258,2},{3,259},{259,3},{4... | collective-permute-start | bytes 1572872 | tf_op jit(solution)/shard_map/ppermute | solution.py:62
  172.9 12.3 %collective-permute-start.2 = (bf16[2,16,128,128]{3,2,1,0:T(8,128)(2,1)S(1)}, bf16[2,16,128,128]{3,2,1,0:T(8,128)(2,1)S(1)}, u32[]{:S(2)}, u32[]{:S(2)}) collective-permute-start(bf16[2,16,128,128]{3,2,1,0:T(8,128)(2,1)S(1)} %pad_maximum_fusion.1), channel_id=1, source_target_pairs={{0,8},{8,0},{1,9},{9,1},{2,10},{10,2},{3,11},{11,3},{4,12},{12,4},... | collective-permute-start | bytes 3145736 | tf_op jit(solution)/shard_map/ppermute | solution.py:62
  192.2 6.3 %copy-start.1 = (bf16[2,64,288]{2,1,0:T(8,128)(2,1)S(1)}, bf16[2,64,288]{2,1,0:T(8,128)(2,1)}, u32[]{:S(2)}) copy-start(bf16[2,64,288]{2,1,0:T(8,128)(2,1)} %param.4) | copy-start | bytes 221188

commit v2 on v0

v2 whole, which is shorter than its diff:
```python
import functools
import math

import jax
import jax.numpy as jnp
import ml_dtypes
import numpy as np
from jax import lax
from jax.experimental import pallas as pl
from jax.experimental.pallas import tpu as pltpu
from jax.sharding import Mesh
from jax.sharding import PartitionSpec as P

CYCLES = 64
ANG = 288
ROT = 72
HALF = ANG // 2
LANES = 2 * CYCLES
PRIOR_WEIGHT = 1.0
SCORE_SCALE = 4.0 / math.sqrt(CYCLES * ANG)

X, Z, CORE, SIDE = 2, 16, 2, 8
MINE = 2
PER_CORE = 25
KD = 13
KPAD = 16
KROWS = KPAD // 2
SOURCES = X * SIDE
COUNT = MINE * CORE * SOURCES
MSG = MINE * HALF + 16
CHUNK = KD * HALF // Z
SLOT = 128

DOM = ("x_lo", "z", "core")
CLS = ("x_hi", "y")

NT = (((1,), (1,)), ((), ()))
NN = (((1,), (0,)), ((), ()))
f32 = jnp.float32
bf16 = jnp.bfloat16


def angles(rows, cols, factor):
    index = np.arange(rows)[:, None] * factor * np.arange(cols)[None, :] % ANG
    return 2.0 * math.pi * index / ANG


def split(table):
    table = table.astype(np.float32)
    high = table.astype(ml_dtypes.bfloat16)
    low = (table - high.astype(np.float32)).astype(ml_dtypes.bfloat16)
    return np.stack([high, low])


def forward_table():
    angle = angles(HALF + 1, ANG, 1)
    real = np.cos(angle[:HALF])
    imag = np.concatenate([np.cos(angle[HALF:]), np.sin(angle[1:HALF])])
    return split(np.concatenate([real, imag]))


def weights_of_rows():
    return np.where(np.arange(HALF) == 0, 1.0, 2.0)[:, None] / ANG


def search_table():
    angle = angles(HALF, ROT, ANG // ROT)
    scale = weights_of_rows()
    return split(np.concatenate([np.cos(angle) * scale, -np.sin(angle) * scale]).T)


def post_table():
    angle = angles(HALF, ROT, ANG // ROT)
    return split(np.concatenate([np.cos(angle), np.sin(angle)]))


def inverse_table():
    angle = angles(HALF + 1, ANG, 1)
    scale = weights_of_rows()
    real = np.cos(angle[:HALF]) * scale
    imag = np.concatenate([np.cos(angle[HALF:]), np.sin(angle[1:HALF])]) * scale
    return np.concatenate([split(real), split(imag)])


def dot(a, b, dims=NN):
    return lax.dot_general(a, b, dims, preferred_element_type=f32)


def halves(values):
    high = values.astype(bf16)
    return high, (values - high.astype(f32)).astype(bf16)


def dot3(table, values):
    high, low = halves(values)
    return dot(table[0], high) + (dot(table[0], low) + dot(table[1], high))


def turn(values):
    return pltpu.roll(values, CYCLES, 1)


def left(shape):
    return lax.broadcasted_iota(jnp.int32, shape, len(shape) - 1) < CYCLES


def fold(spec):
    real, imag = spec[:HALF], spec[HALF:]
    side = left(real.shape)
    return jnp.where(side, real, turn(imag)), jnp.where(side, turn(real), imag)


def share_kernel(ids, x, ctf, table, out):
    images = x[...].reshape(MINE * CYCLES, ANG)
    factor = jnp.concatenate([ctf[pl.ds(ids[0], 1), :], ctf[pl.ds(ids[1], 1), :]], axis=1)
    spec = (dot(table[0], images, NT) + dot(table[1], images, NT)) * factor
    first, second = fold(spec)
    out[0:HALF] = first.astype(bf16)
    out[HALF : 2 * HALF] = second.astype(bf16)
    high, rest = halves(factor)
    rest = factor - high.astype(f32)
    mid = rest.astype(bf16)
    low = rest - mid.astype(f32)
    row = lax.broadcasted_iota(jnp.int32, (16, LANES), 0)
    tags = jnp.where(row == 0, high.astype(f32), jnp.where(row == 1, mid.astype(f32), jnp.where(row == 2, low, 0.0)))
    out[2 * HALF : MSG] = tags.astype(bf16)


def class_kernel(start, refs, table, out, power, images, rows, sem):
    copy = pltpu.make_async_copy(refs.at[pl.ds(start[0], KD)], images.at[pl.ds(0, KD)], sem)
    copy.start()
    images[KD:] = jnp.zeros((KPAD - KD, CYCLES, ANG), bf16)
    ones = jnp.ones((8, ANG), bf16)
    copy.wait()
    for step in range(KPAD // 4):
        block = images[4 * step : 4 * step + 4].reshape(4 * CYCLES, ANG)
        spec = dot(table[0], block, NT) + dot(table[1], block, NT)
        wide = block.astype(f32)
        high, low = halves(wide * wide)
        energy = dot(ones, high, NT) + dot(ones, low, NT)
        for pair in range(2):
            k = 4 * step + 2 * pair
            lanes = slice(pair * LANES, (pair + 1) * LANES)
            first, second = fold(spec[:, lanes])
            rows[k * HALF : (k + 1) * HALF] = first.astype(bf16).astype(f32)
            rows[(k + 1) * HALF : (k + 2) * HALF] = second.astype(bf16).astype(f32)
            part = energy[:, lanes]
            side = left(part.shape)
            power[k : k + 1] = jnp.where(side, part, 0.0)[0:1]
            power[k + 1 : k + 2] = jnp.where(side, turn(part), 0.0)[0:1]

    def step(j, carry):
        plain = rows[pl.ds(j, KPAD, stride=HALF), :]
        other = turn(plain)
        other = jnp.where(left(other.shape), other, -other)
        out[j] = jnp.concatenate([plain, other], axis=0).astype(bf16)
        return carry

    lax.fori_loop(0, HALF, step, 0, unroll=8)


def score_kernel(place, own, other, rmat, power, table, expo, stats, by_class, ydata, csq, wide, pairs):
    core, x_lo = place[0], place[1]

    def widen(s, carry):
        mine = pl.multiple_of((core * SOURCES + s) * MSG, 8)
        theirs = pl.multiple_of(((1 - core) * SOURCES + s) * MSG, 8)
        wide[pl.ds(mine, MSG), :] = own[s].astype(f32)
        wide[pl.ds(theirs, MSG), :] = other[s].astype(f32)
        return carry

    lax.fori_loop(0, SOURCES, widen, 0)
    many = CORE * SOURCES
    factor = wide[pl.ds(2 * HALF, many, stride=MSG), :] + wide[pl.ds(2 * HALF + 1, many, stride=MSG), :]
    factor = factor + wide[pl.ds(2 * HALF + 2, many, stride=MSG), :]
    square = factor * factor
    side = left(square.shape)
    square = jnp.concatenate([jnp.where(side, square, 0.0), jnp.where(side, turn(square), 0.0)], axis=0)
    csq[...] = square
    energy = lax.dot_general(
        power[...],
        jnp.concatenate([square, square], axis=0),
        NT,
        precision=lax.Precision.HIGHEST,
        preferred_element_type=f32,
    )
    side = left((KROWS, LANES))
    energy = jnp.where(side, energy[:KROWS], energy[KROWS:])

    def step(j, carry):
        rows = jnp.concatenate([wide[pl.ds(j, many, stride=MSG), :], wide[pl.ds(HALF + j, many, stride=MSG), :]], axis=0)
        rows = rows.astype(bf16)
        ydata[j] = rows
        both = dot(rmat[j], jnp.concatenate([rows, rows], axis=0), NT)
        side = left((KROWS, LANES))
        straight = jnp.where(side, both[:KROWS], both[KROWS : 2 * KROWS])
        crossed = jnp.where(side, both[2 * KROWS : 3 * KROWS], both[3 * KROWS :])
        pairs[pl.ds(j, KROWS, stride=ANG), :] = straight
        pairs[pl.ds(HALF + j, KROWS, stride=ANG), :] = crossed
        return carry

    lax.fori_loop(0, HALF, step, 0, unroll=8)
    top = jnp.full((1, LANES), -3.0e38, f32)
    lane_side = left((ROT, LANES))
    for kk in range(KROWS):
        cross = dot3(table, pairs[kk * ANG : (kk + 1) * ANG])
        score = SCORE_SCALE * (cross - 0.5 * energy[kk : kk + 1])
        if kk + KROWS >= KD:
            score = jnp.where(lane_side, score, -3.0e38)
        if kk == 0:
            score = jnp.where(jnp.logical_and(lane_side, x_lo == 1), -3.0e38, score)
        expo[:, kk * LANES : (kk + 1) * LANES] = score
        top = jnp.maximum(top, jnp.max(score, axis=0, keepdims=True))
    top = jnp.maximum(top, turn(top))
    total = jnp.zeros((1, LANES), f32)
    for kk in range(KROWS):
        value = jnp.exp(expo[:, kk * LANES : (kk + 1) * LANES] - top)
        expo[:, kk * LANES : (kk + 1) * LANES] = value
        part = jnp.sum(value, axis=0, keepdims=True)
        by_class[kk : kk + 1] = part
        total = total + part
    total = total + turn(total)
    stats[...] = jnp.where(lax.broadcasted_iota(jnp.int32, (8, LANES), 0) == 0, top, total)


def post_kernel(expo, table, out, rows):
    for kk in range(KROWS):
        rows[kk * ANG : (kk + 1) * ANG] = dot3(table, expo[:, kk * LANES : (kk + 1) * LANES])

    def step(j, carry):
        real = rows[pl.ds(j, KROWS, stride=ANG), :]
        imag = rows[pl.ds(HALF + j, KROWS, stride=ANG), :]
        out[j] = jnp.concatenate([real, turn(real), imag, turn(imag)], axis=0)
        return carry

    lax.fori_loop(0, HALF, step, 0, unroll=8)


def sum_kernel(all_stats, stats, post, ydata, by_class, csq, out, rows, slots):
    tops, totals = all_stats[:, 0, :], all_stats[:, 1, :]
    top = jnp.max(tops, axis=0, keepdims=True)
    total = jnp.sum(totals * jnp.exp(tops - top), axis=0, keepdims=True)
    share = jnp.exp(stats[0:1] - top) / total

    def step(j, carry):
        weights = (post[j] * share)[:, :CYCLES].astype(bf16)
        both = dot(weights, ydata[j])
        other = turn(both[KPAD:])
        other = jnp.where(left(other.shape), other, -other)
        rows[pl.ds(j, KPAD, stride=HALF), :] = both[:KPAD] + other
        return carry

    lax.fori_loop(0, HALF, step, 0, unroll=8)
    mass = by_class[...] * share
    mass = jnp.concatenate([mass, turn(mass)], axis=0)[:, :CYCLES]
    weight = lax.dot_general(mass, csq[...], NN, precision=lax.Precision.HIGHEST, preferred_element_type=f32)
    high, low = halves(weight)
    scales = jnp.where(left(weight.shape), high.astype(f32), turn(low.astype(f32)))
    for z in range(Z):
        first = z * CHUNK // HALF
        second = min(first + 1, KD - 1)
        base = z * SLOT
        slots[base + SLOT - 16 : base + SLOT] = jnp.zeros((16, LANES), f32)
        slots[base : base + CHUNK] = rows[z * CHUNK : (z + 1) * CHUNK]
        slots[base + CHUNK : base + CHUNK + 1] = scales[first : first + 1]
        slots[base + CHUNK + 1 : base + CHUNK + 2] = scales[second : second + 1]
        out[z] = slots[base : base + SLOT].astype(bf16)


def image_kernel(place, hats, table, *rest):
    out, flat, real, imag, stage, sem = rest[-6:]
    core, x_lo = place[0], place[1]
    for z in range(Z):
        flat[z * CHUNK : (z + 1) * CHUNK] = hats[z].astype(f32)[:CHUNK]
    for k in range(KD):
        rows = flat[k * HALF : (k + 1) * HALF].T.astype(bf16)
        real[k * CYCLES : (k + 1) * CYCLES] = rows[:CYCLES]
        imag[k * CYCLES : (k + 1) * CYCLES] = rows[CYCLES:]
    for k in range(KD):
        lines = slice(k * CYCLES, (k + 1) * CYCLES)
        image = dot(real[lines], table[0]) + dot(imag[lines], table[2])
        image = image + (dot(real[lines], table[1]) + dot(imag[lines], table[3]))
        stage[k] = image.astype(bf16)
    base = core * PER_CORE + x_lo * (KD - 1)
    copy = pltpu.make_async_copy(stage.at[pl.ds(x_lo, KD - 1)], out.at[pl.ds(base + x_lo, KD - 1)], sem.at[0])
    copy.start()

    @pl.when(x_lo == 0)
    def _():
        last = pltpu.make_async_copy(stage.at[pl.ds(KD - 1, 1)], out.at[pl.ds(base + KD - 1, 1)], sem.at[1])
        last.start()
        last.wait()

    copy.wait()


VMEM = pl.BlockSpec(memory_space=pltpu.VMEM)
SMEM = pl.BlockSpec(memory_space=pltpu.SMEM)
ANYWHERE = pl.BlockSpec(memory_space=pl.ANY)


def call(kernel, ins, outs, scratch, flops, nbytes, aliases=None, out_specs=None):
    out_shape = [jax.ShapeDtypeStruct(shape, dtype) for shape, dtype in outs]
    single = len(out_shape) == 1
    specs = out_specs or [VMEM] * len(out_shape)
    return pl.pallas_call(
        kernel,
        out_shape=out_shape[0] if single else out_shape,
        in_specs=ins,
        out_specs=specs[0] if single else specs,
        scratch_shapes=scratch,
        input_output_aliases=aliases or {},
        compiler_params=pltpu.CompilerParams(vmem_limit_bytes=48 * 2**20),
        cost_estimate=pl.CostEstimate(flops=flops, bytes_accessed=nbytes, transcendentals=0),
    )


def swap(axis, value):
    return lax.ppermute(value, axis, [(0, 1), (1, 0)])


def spread(value, axes, count):
    return lax.all_to_all(jnp.broadcast_to(value[None], (count,) + value.shape), axes, 0, 0, tiled=True)


def body(particles, group_ids, ctf_table, references):
    core, x_lo, z = (lax.axis_index(name) for name in ("core", "x_lo", "z"))
    forward = jnp.asarray(forward_table())
    place = jnp.stack([core, x_lo])

    message = call(
        share_kernel, [SMEM, VMEM, VMEM, VMEM], [((MSG, LANES), bf16)], [], 10**7, 10**6
    )(group_ids, particles, ctf_table, forward)
    own = spread(message, ("x_lo", "x_hi", "y"), SOURCES)
    other = swap("core", own)

    start = (core * PER_CORE + x_lo * (KD - 1)).reshape(1)
    rmat, power = call(
        class_kernel,
        [SMEM, ANYWHERE, VMEM],
        [((HALF, 2 * KPAD, LANES), bf16), ((KPAD, LANES), f32)],
        [
            pltpu.VMEM((KPAD, CYCLES, ANG), bf16),
            pltpu.VMEM((KPAD * HALF, LANES), f32),
            pltpu.SemaphoreType.DMA,
        ],
        10**9,
        4 * 10**6,
    )(start, references, forward)

    expo, stats, by_class, ydata, csq = call(
        score_kernel,
        [SMEM] + [VMEM] * 5,
        [
            ((ROT, KROWS * LANES), f32),
            ((8, LANES), f32),
            ((KROWS, LANES), f32),
            ((HALF, COUNT, LANES), bf16),
            ((COUNT, LANES), f32),
        ],
        [
            pltpu.VMEM((CORE * SOURCES * MSG, LANES), f32),
            pltpu.VMEM((KROWS * ANG, LANES), f32),
        ],
        10**9,
        8 * 10**6,
    )(place, own, other, rmat, power, jnp.asarray(search_table()))
    all_stats = spread(stats, ("core", "x_lo", "x_hi", "y"), CORE * SOURCES)
    post = call(
        post_kernel,
        [VMEM, VMEM],
        [((HALF, 2 * KPAD, LANES), f32)],
        [pltpu.VMEM((KROWS * ANG, LANES), f32)],
        10**9,
        3 * 10**6,
    )(expo, jnp.asarray(post_table()))
    sums = call(
        sum_kernel,
        [VMEM] * 6,
        [((Z, SLOT, LANES), bf16)],
        [pltpu.VMEM((KPAD * HALF, LANES), f32), pltpu.VMEM((Z * SLOT, LANES), f32)],
        10**9,
        8 * 10**6,
    )(all_stats, stats, post, ydata, by_class, csq)

    got = jnp.sum(lax.all_to_all(sums, "z", 0, 0, tiled=True).astype(f32), axis=0)
    scales = got[CHUNK : CHUNK + 2]
    scales = scales[:, :CYCLES] + scales[:, CYCLES:] + PRIOR_WEIGHT
    scales = jnp.concatenate([scales, scales], axis=1)
    row = lax.broadcasted_iota(jnp.int32, (SLOT, LANES), 0)
    edge = (z * CHUNK // HALF + 1) * HALF - z * CHUNK
    hat = (got / jnp.where(row < edge, scales[:1], scales[1:])).astype(bf16)

    near = lax.all_gather(hat, "z")
    far = swap("x_lo", near)
    inverse = jnp.asarray(inverse_table())
    result = None
    for hats, which in (
        (near, (core, x_lo)),
        (swap("core", near), (1 - core, x_lo)),
        (far, (core, 1 - x_lo)),
        (swap("core", far), (1 - core, 1 - x_lo)),
    ):
        extra = [] if result is None else [result]
        result = call(
            image_kernel,
            [SMEM, VMEM, VMEM] + [ANYWHERE] * len(extra),
            [((CORE * PER_CORE, CYCLES, ANG), bf16)],
            [
                pltpu.VMEM((KD * HALF, LANES), f32),
                pltpu.VMEM((KD * CYCLES, HALF), bf16),
                pltpu.VMEM((KD * CYCLES, HALF), bf16),
                pltpu.VMEM((KD, CYCLES, ANG), bf16),
                pltpu.SemaphoreType.DMA((2,)),
            ],
            10**9,
            2 * 10**6,
            {3: 0} if extra else None,
            [ANYWHERE],
        )(jnp.stack(which), hats, inverse, *extra)
    return result


def solution(mesh):
    fine = Mesh(mesh.devices.reshape(X, Z, CORE, 2, 4), DOM + CLS)
    in_specs = (P(DOM + CLS, None, None), P(DOM + CLS), P(), P(CLS, None, None))
    return jax.shard_map(body, mesh=fine, in_specs=in_specs, out_specs=P(CLS, None, None), check_vma=False)
```

time: 635 us -> 168 us (0.26); the launches traced: 628 us -> 168 us
  blocking collectives: 281 us -> 52.3 us
  waiting for transfers between devices: 247 us -> 26.4 us
  starting transfers between devices: 0.01 us -> 49.2 us
  matrix products: 36.5 us -> 0 us
  Pallas kernels: 0 us -> 30.2 us
  other arithmetic: 24.7 us -> 0.55 us
  between operations: 15.3 us -> 0.23 us
  local copies, waits for them, and re-layouts: 22.6 us -> 8.91 us
    psum x1 -> x0, waiting for transfers between devices: 247 us -> none  [body(): totals, weight = lax.psum((totals, weight), 'dom')]
    psum x1 -> x0, blocking collectives: 224 us -> none  [body(): totals, weight = lax.psum((totals, weight), 'dom')]
    dot_general x13 -> x0, matrix products: 36.5 us -> none  [the longest x1 7.48 us: body(): jnp.dot(ref_float.reshape(kd * cycles, ANG), forward, precision=highest)]
    ppermute x0 -> x4, starting transfers between devices: none -> 30.4 us  [swap(): return lax.ppermute(value, axis, [(0, 1), (1, 0)])]
    pallas_call x0 -> x9, Pallas kernels: none -> 30.2 us  [the longest x4 10.9 us: body(): call(image_kernel, [SMEM, VMEM, VMEM] + [ANYWHERE] * len(extra), [((CORE...]
    unnamed x2 -> x0, blocking collectives: 27.3 us -> none
    all_to_all x0 -> x2, waiting for transfers between devices: none -> 26.4 us  [the longest x1 22.9 us: body(): lax.all_to_all(sums, 'z', 0, 0, tiled=True).astype(f32)]
    all_to_all x0 -> x1, blocking collectives: none -> 24.3 us  [spread(): lax.all_to_all(jnp.broadcast_to(value[None], (count,) + value.shape), axe...]
  transfers between devices with their start and end apart: 1 -> 6, of which waited for: 1 -> 2; matrix products, arithmetic and copies ran while one was open for 0% -> 0% of each run, Pallas kernels for 0% -> 8%
where the time goes in v2:
time: 168 us
  blocking collectives  52.3 us (31%)
  starting transfers between devices  49.2 us (29%)
  Pallas kernels  30.2 us (18%)
  waiting for transfers between devices  26.4 us (16%)
  local copies, waits for them, and re-layouts  8.91 us (5%)
    ppermute x4, starting transfers between devices, swap(): return lax.ppermute(value, axis, [(0, 1), (1, 0)])  30.4 us
    all_gather x1, blocking collectives, body(): near = lax.all_gather(hat, 'z')  28 us
    all_to_all x1, blocking collectives, spread(): lax.all_to_all(jnp.broadcast_to(value[None], (count,) + value.shape), axe...  24.3 us
    all_to_all x1, waiting for transfers between devices, body(): lax.all_to_all(sums, 'z', 0, 0, tiled=True).astype(f32)  22.9 us
    all_to_all x1, starting transfers between devices, body(): lax.all_to_all(sums, 'z', 0, 0, tiled=True).astype(f32)  15.1 us
    pallas_call x4, Pallas kernels, body(): call(image_kernel, [SMEM, VMEM, VMEM] + [ANYWHERE] * len(extra), [((CORE...  10.9 us
    unnamed x24, local copies, waits for them, and re-layouts  8.08 us
    pallas_call x1, Pallas kernels, body(): call(score_kernel, [SMEM] + [VMEM] * 5, [((ROT, KROWS * LANES), f32), ((8...  7.32 us
  transfers between devices with their start and end apart: 6, of which 2 were waited for; matrix products, arithmetic and copies ran while one was open for 0% of the time, Pallas kernels for 8%

profile of v2, /device:TPU:1, one launch (start us, length us, event | category | flops | bytes accessed | tf_op | source)
XLA Modules:
  0.0 167.8 jit_solution(10093946736102374848)
XLA Ops:
  0.0 1.0 copy-done.4
  1.0 0.9 copy-done.7
  3.3 0.9 shard_map.82
  4.3 24.3 %all_to_all.15.own = bf16[16,304,128]{2,1,0:T(8,128)(2,1)S(1)} all-to-all(bf16[16,304,128]{2,1,0:T(8,128)(2,1)S(1)} %broadcast_in_dim.32), channel_id=1, replica_groups=mesh['x_lo'=2,'z'=16,'core'=2,'x_hi'=2,'y'=4] {'x_lo','x_hi','y'}, dimensions={0} | all-to-all | bytes 2490368 | tf_op jit(solution)/shard_map/all_to_all | solution.py:323
  28.7 5.1 %collective-permute-start = (bf16[16,304,128]{2,1,0:T(8,128)(2,1)S(1)}, bf16[16,304,128]{2,1,0:T(8,128)(2,1)S(1)}, u32[]{:S(2)}, u32[]{:S(2)}) collective-permute-start(bf16[16,304,128]{2,1,0:T(8,128)(2,1)S(1)} %all_to_all.15.own), channel_id=1, source_target_pairs={{0,8},{8,0},{1,9},{9,1},{2,10},{10,2},{3,11},{11,3},{4,12},{12,4},... | collective-permute-start | bytes 3735560 | tf_op jit(solution)/shard_map/ppermute | solution.py:319
  33.8 1.7 %copy-done.10 = bf16[50,64,288]{2,1,0:T(8,128)(2,1)S(1)} copy-done((bf16[50,64,288]{2,1,0:T(8,128)(2,1)S(1)}, bf16[50,64,288]{2,1,0:T(8,128)(2,1)}, u32[]{:S(2)}) %copy-start.10) | copy-done | bytes 1843224
  35.5 3.1 %shard_map.83 = (bf16[144,32,128]{2,1,0:T(8,128)(2,1)S(1)}, f32[16,128]{1,0:T(8,128)S(1)}) custom-call(s32[1]{0:T(128)} %bitcast.4.start, bf16[50,64,288]{2,1,0:T(8,128)(2,1)S(1)} %copy-done.10, bf16[2,288,288]{2,1,0:T(8,128)(2,1)S(1)} %copy-done.5), custom_call_target="tpu_custom_call" | custom-call | flops 1000000000 | bytes 4000000 | tf_op jit(solution)/shard_map/pallas_call | solution.py:338
  38.8 7.3 %shard_map.84 = (f32[72,1024]{1,0:T(8,128)S(1)}, f32[8,128]{1,0:T(8,128)S(1)}, f32[8,128]{1,0:T(8,128)S(1)}, bf16[144,64,128]{2,1,0:T(8,128)(2,1)}, f32[64,128]{1,0:T(8,128)S(1)}) custom-call(s32[2]{0:T(128)S(1)} %pad_add_fusion.3.place, bf16[16,304,128]{2,1,0:T(8,128)(2,1)S(1)} %all_to_all.15.own, bf16[16,304,128]{2,1,0:T(8,128)(2,1)S(1)} %collective-permute-done.other, ...), custom_call_target="tpu_custom_call" | custom-call | flops 1000000000 | bytes 8000000 | tf_op jit(solution)/shard_map/pallas_call | solution.py:351
  46.7 3.8 %all-to-all-start.1 = ((f32[32,8,128]{2,1,0:T(8,128)}), f32[32,8,128]{2,1,0:T(8,128)S(1)}, u32[]{:S(2)}, u32[]{:S(2)}) async-start(f32[32,8,128]{2,1,0:T(8,128)} %broadcast_in_dim.33), calls=%async_computation.1 | async-start | bytes 262144 | tf_op jit(solution)/shard_map/all_to_all | solution.py:323
  50.5 2.6 %shard_map.85.post = f32[144,32,128]{2,1,0:T(8,128)S(1)} custom-call(f32[72,1024]{1,0:T(8,128)S(1)} %get-tuple-element.15.expo, bf16[2,288,72]{2,1,0:T(8,128)(2,1)S(1)} %copy-done.11), custom_call_target="tpu_custom_call" | custom-call | flops 1000000000 | bytes 3000000 | tf_op jit(solution)/shard_map/pallas_call | solution.py:369
  53.1 1.4 copy-done.2
  54.5 3.5 %all-to-all-done.1.all_stats = f32[32,8,128]{2,1,0:T(8,128)S(1)} async-done(((f32[32,8,128]{2,1,0:T(8,128)}), f32[32,8,128]{2,1,0:T(8,128)S(1)}, u32[]{:S(2)}, u32[]{:S(2)}) %all-to-all-start.1) | async-done | bytes 131104 | tf_op jit(solution)/shard_map/all_to_all | solution.py:323
  58.1 1.7 copy-done.3
  59.7 5.4 %shard_map.86 = bf16[16,128,128]{2,1,0:T(8,128)(2,1)} custom-call(f32[32,8,128]{2,1,0:T(8,128)S(1)} %all-to-all-done.1.all_stats, f32[8,128]{1,0:T(8,128)S(1)} %get-tuple-element.14.stats, f32[144,32,128]{2,1,0:T(8,128)S(1)} %copy-done.3, bf16[144,64,128]{2,1,0:T(8,128)(2,1)S(1)} %copy-done.1, f32[8,128]{1,0:T(8,128)S(1)} %get-tuple-element.17.by_class, ...), custom_call_target="tpu_custom_call" | custom-call | flops 1000000000 | bytes 8000000 | tf_op jit(solution)/shard_map/pallas_call | solution.py:377
  65.1 15.1 %all-to-all-start.2 = ((bf16[16,128,128]{2,1,0:T(8,128)(2,1)}), bf16[16,128,128]{2,1,0:T(8,128)(2,1)S(1)}, u32[]{:S(2)}, u32[]{:S(2)}) async-start(bf16[16,128,128]{2,1,0:T(8,128)(2,1)} %shard_map.86), calls=%async_computation.2 | async-start | bytes 1048576 | tf_op jit(solution)/shard_map/all_to_all | solution.py:386
  80.2 22.9 %all-to-all-done.2 = bf16[16,128,128]{2,1,0:T(8,128)(2,1)S(1)} async-done(((bf16[16,128,128]{2,1,0:T(8,128)(2,1)}), bf16[16,128,128]{2,1,0:T(8,128)(2,1)S(1)}, u32[]{:S(2)}, u32[]{:S(2)}) %all-to-all-start.2) | async-done | bytes 524320 | tf_op jit(solution)/shard_map/all_to_all | solution.py:386
  103.5 28.0 %all_gather.4.hats = bf16[16,128,128]{2,1,0:T(8,128)(2,1)S(1)} all-gather(bf16[1,128,128]{2,1,0:T(8,128)(2,1)S(1)} %fusion), channel_id=1, replica_groups=mesh['x_lo'=2,'z'=16,'core'=2,'x_hi'=2,'y'=4] {'z'}, dimensions={0}, use_global_device_ids=true | all-gather | bytes 557056 | tf_op jit(solution)/shard_map/all_gather | solution.py:394
  131.4 2.2 %collective-permute-start.1 = (bf16[16,128,128]{2,1,0:T(8,128)(2,1)S(1)}, bf16[16,128,128]{2,1,0:T(8,128)(2,1)S(1)}, u32[]{:S(2)}, u32[]{:S(2)}) collective-permute-start(bf16[16,128,128]{2,1,0:T(8,128)(2,1)S(1)} %all_gather.4.hats), channel_id=1, source_target_pairs={{0,256},{256,0},{1,257},{257,1},{2,258},{258,2},{3,259},{259,3},{4... | collective-permute-start | bytes 1572872 | tf_op jit(solution)/shard_map/ppermute | solution.py:319
  133.7 14.5 %collective-permute-start.3 = (bf16[16,128,128]{2,1,0:T(8,128)(2,1)S(1)}, bf16[16,128,128]{2,1,0:T(8,128)(2,1)S(1)}, u32[]{:S(2)}, u32[]{:S(2)}) collective-permute-start(bf16[16,128,128]{2,1,0:T(8,128)(2,1)S(1)} %all_gather.4.hats), channel_id=1, source_target_pairs={{0,8},{8,0},{1,9},{9,1},{2,10},{10,2},{3,11},{11,3},{4,12},{12,4},... | collective-permute-start | bytes 1572872 | tf_op jit(solution)/shard_map/ppermute | solution.py:319
  148.2 8.5 %collective-permute-start.2 = (bf16[16,128,128]{2,1,0:T(8,128)(2,1)S(1)}, bf16[16,128,128]{2,1,0:T(8,128)(2,1)S(1)}, u32[]{:S(2)}, u32[]{:S(2)}) collective-permute-start(bf16[16,128,128]{2,1,0:T(8,128)(2,1)S(1)} %collective-permute-done.1.hats), channel_id=1, source_target_pairs={{0,8},{8,0},{1,9},{9,1},{2,10},{10,2},{3,11},{11,3},{4,12},{12,4},... | collective-permute-start | bytes 1572872 | tf_op jit(solution)/shard_map/ppermute | solution.py:319
  156.9 2.7 %shard_map.87.rest_0_ = bf16[50,64,288]{2,1,0:T(8,128)(2,1)} custom-call(s32[2]{0:T(128)S(1)} %pad_add_fusion.3.place, bf16[16,128,128]{2,1,0:T(8,128)(2,1)S(1)} %all_gather.4.hats, bf16[4,144,288]{2,1,0:T(8,128)(2,1)S(1)} %copy-done), custom_call_target="tpu_custom_call" | custom-call | flops 1000000000 | bytes 2000000 | tf_op jit(solution)/shard_map/pallas_call | solution.py:405
  159.6 2.7 %shard_map.88.rest_0_ = bf16[50,64,288]{2,1,0:T(8,128)(2,1)} custom-call(s32[2]{0:T(128)S(1)} %pad_add_fusion.2.place, bf16[16,128,128]{2,1,0:T(8,128)(2,1)S(1)} %collective-permute-done.3.hats, bf16[4,144,288]{2,1,0:T(8,128)(2,1)S(1)} %copy-done, bf16[50,64,288]{2,1,0:T(8,128)(2,1)} %shard_map.87.rest_0_), custom_call_target="tpu_custom_call", output_to_operand_aliasing={{}: (3, {})} | custom-call | flops 1000000000 | bytes 2000000 | tf_op jit(solution)/shard_map/pallas_call | solution.py:405
  162.3 2.7 %shard_map.89.rest_0_ = bf16[50,64,288]{2,1,0:T(8,128)(2,1)} custom-call(s32[2]{0:T(128)S(1)} %get-tuple-element.21.place, bf16[16,128,128]{2,1,0:T(8,128)(2,1)S(1)} %collective-permute-done.1.hats, bf16[4,144,288]{2,1,0:T(8,128)(2,1)S(1)} %copy-done, bf16[50,64,288]{2,1,0:T(8,128)(2,1)} %shard_map.88.rest_0_), custom_call_target="tpu_custom_call", output_to_operand_aliasing={{}: (3, {})} | custom-call | flops 1000000000 | bytes 2000000 | tf_op jit(solution)/shard_map/pallas_call | solution.py:405
  165.1 2.7 %shard_map.90 = bf16[50,64,288]{2,1,0:T(8,128)(2,1)} custom-call(s32[2]{0:T(128)S(1)} %get-tuple-element.22.place, bf16[16,128,128]{2,1,0:T(8,128)(2,1)S(1)} %collective-permute-done.2.hats, bf16[4,144,288]{2,1,0:T(8,128)(2,1)S(1)} %copy-done, bf16[50,64,288]{2,1,0:T(8,128)(2,1)} %shard_map.89.rest_0_), custom_call_target="tpu_custom_call", output_to_operand_aliasing={{}: (3, {})} | custom-call | flops 1000000000 | bytes 2000000 | tf_op jit(solution)/shard_map/pallas_call | solution.py:405
  (34 shorter events, 2.8 us)
Async XLA Ops:
  0.0 1.0 copy-start.4
  1.0 0.9 copy-start.7
  1.9 0.7 copy-start.8
  2.6 0.7 copy-start.9
  3.3 30.5 %copy-start.5 = (bf16[2,288,288]{2,1,0:T(8,128)(2,1)S(1)}, bf16[2,288,288]{2,1,0:T(8,128)(2,1)}, u32[]{:S(2)}) copy-start(bf16[2,288,288]{2,1,0:T(8,128)(2,1)} %constant.45.clone.table) | copy-start | bytes 995332
  28.7 10.1 %copy-start.6 = (bf16[2,72,288]{2,1,0:T(8,128)(2,1)S(1)}, bf16[2,72,288]{2,1,0:T(8,128)(2,1)}, u32[]{:S(2)}) copy-start(bf16[2,72,288]{2,1,0:T(8,128)(2,1)} %constant.46.clone.table) | copy-start | bytes 248836
  28.7 10.1 %collective-permute-start = (bf16[16,304,128]{2,1,0:T(8,128)(2,1)S(1)}, bf16[16,304,128]{2,1,0:T(8,128)(2,1)S(1)}, u32[]{:S(2)}, u32[]{:S(2)}) collective-permute-start(bf16[16,304,128]{2,1,0:T(8,128)(2,1)S(1)} %all_to_all.15.own), channel_id=1, source_target_pairs={{0,8},{8,0},{1,9},{9,1},{2,10},{10,2},{3,11},{11,3},{4,12},{12,4},... | collective-permute-start | bytes 3735560 | tf_op jit(solution)/shard_map/ppermute | solution.py:319
  33.8 1.7 %copy-start.10 = (bf16[50,64,288]{2,1,0:T(8,128)(2,1)S(1)}, bf16[50,64,288]{2,1,0:T(8,128)(2,1)}, u32[]{:S(2)}) copy-start(bf16[50,64,288]{2,1,0:T(8,128)(2,1)} %refs.1) | copy-start | bytes 5529604
  38.7 11.9 %copy-start.11 = (bf16[2,288,72]{2,1,0:T(8,128)(2,1)S(1)}, bf16[2,288,72]{2,1,0:T(8,128)(2,1)}, u32[]{:S(2)}) copy-start(bf16[2,288,72]{2,1,0:T(8,128)(2,1)} %constant.47.clone.table) | copy-start | bytes 248836
  46.1 12.0 %copy-start.1 = (bf16[144,64,128]{2,1,0:T(8,128)(2,1)S(1)}, bf16[144,64,128]{2,1,0:T(8,128)(2,1)}, u32[]{:S(2)}) copy-start(bf16[144,64,128]{2,1,0:T(8,128)(2,1)} %get-tuple-element.16.ydata) | copy-start | bytes 7077892
  46.7 11.3 %all-to-all-start.1 = ((f32[32,8,128]{2,1,0:T(8,128)}), f32[32,8,128]{2,1,0:T(8,128)S(1)}, u32[]{:S(2)}, u32[]{:S(2)}) async-start(f32[32,8,128]{2,1,0:T(8,128)} %broadcast_in_dim.33), calls=%async_computation.1 | async-start | bytes 262144 | tf_op jit(solution)/shard_map/all_to_all | solution.py:323
  53.1 1.4 copy-start.2
  58.1 1.7 copy-start.3
  59.7 97.1 %copy-start = (bf16[4,144,288]{2,1,0:T(8,128)(2,1)S(1)}, bf16[4,144,288]{2,1,0:T(8,128)(2,1)}, u32[]{:S(2)}) copy-start(bf16[4,144,288]{2,1,0:T(8,128)(2,1)} %constant.48.clone.table) | copy-start | bytes 995332
  65.1 38.0 %all-to-all-start.2 = ((bf16[16,128,128]{2,1,0:T(8,128)(2,1)}), bf16[16,128,128]{2,1,0:T(8,128)(2,1)S(1)}, u32[]{:S(2)}, u32[]{:S(2)}) async-start(bf16[16,128,128]{2,1,0:T(8,128)(2,1)} %shard_map.86), calls=%async_computation.2 | async-start | bytes 1048576 | tf_op jit(solution)/shard_map/all_to_all | solution.py:386
  131.4 16.8 %collective-permute-start.1 = (bf16[16,128,128]{2,1,0:T(8,128)(2,1)S(1)}, bf16[16,128,128]{2,1,0:T(8,128)(2,1)S(1)}, u32[]{:S(2)}, u32[]{:S(2)}) collective-permute-start(bf16[16,128,128]{2,1,0:T(8,128)(2,1)S(1)} %all_gather.4.hats), channel_id=1, source_target_pairs={{0,256},{256,0},{1,257},{257,1},{2,258},{258,2},{3,259},{259,3},{4... | collective-permute-start | bytes 1572872 | tf_op jit(solution)/shard_map/ppermute | solution.py:319
  133.7 25.9 %collective-permute-start.3 = (bf16[16,128,128]{2,1,0:T(8,128)(2,1)S(1)}, bf16[16,128,128]{2,1,0:T(8,128)(2,1)S(1)}, u32[]{:S(2)}, u32[]{:S(2)}) collective-permute-start(bf16[16,128,128]{2,1,0:T(8,128)(2,1)S(1)} %all_gather.4.hats), channel_id=1, source_target_pairs={{0,8},{8,0},{1,9},{9,1},{2,10},{10,2},{3,11},{11,3},{4,12},{12,4},... | collective-permute-start | bytes 1572872 | tf_op jit(solution)/shard_map/ppermute | solution.py:319
  148.2 16.9 %collective-permute-start.2 = (bf16[16,128,128]{2,1,0:T(8,128)(2,1)S(1)}, bf16[16,128,128]{2,1,0:T(8,128)(2,1)S(1)}, u32[]{:S(2)}, u32[]{:S(2)}) collective-permute-start(bf16[16,128,128]{2,1,0:T(8,128)(2,1)S(1)} %collective-permute-done.1.hats), channel_id=1, source_target_pairs={{0,8},{8,0},{1,9},{9,1},{2,10},{10,2},{3,11},{11,3},{4,12},{12,4},... | collective-permute-start | bytes 1572872 | tf_op jit(solution)/shard_map/ppermute | solution.py:319

commit v3 on v2

--- a/solution.py
+++ b/solution.py
@@ -1,4 +1,3 @@
-import functools
 import math
 
 import jax
@@ -20,18 +19,20 @@
 SCORE_SCALE = 4.0 / math.sqrt(CYCLES * ANG)
 
 X, Z, CORE, SIDE = 2, 16, 2, 8
+ZH, ZL = 4, 4
 MINE = 2
 PER_CORE = 25
 KD = 13
 KPAD = 16
 KROWS = KPAD // 2
+PARTS = 2
 SOURCES = X * SIDE
 COUNT = MINE * CORE * SOURCES
 MSG = MINE * HALF + 16
 CHUNK = KD * HALF // Z
-SLOT = 128
-
-DOM = ("x_lo", "z", "core")
+SLOT = 120
+
+DOM = ("x_lo", "z_hi", "z_lo", "core")
 CLS = ("x_hi", "y")
 
 NT = (((1,), (1,)), ((), ()))
@@ -93,7 +94,9 @@
 
 def dot3(table, values):
     high, low = halves(values)
-    return dot(table[0], high) + (dot(table[0], low) + dot(table[1], high))
+    rows = table.shape[0] // 2
+    both = dot(table[...], high)
+    return both[:rows] + (both[rows:] + dot(table[:rows], low))
 
 
 def turn(values):
@@ -110,7 +113,7 @@
     return jnp.where(side, real, turn(imag)), jnp.where(side, turn(real), imag)
 
 
-def share_kernel(ids, x, ctf, table, out):
+def share_kernel(ids, x, ctf, table, outs, out, sem):
     images = x[...].reshape(MINE * CYCLES, ANG)
     factor = jnp.concatenate([ctf[pl.ds(ids[0], 1), :], ctf[pl.ds(ids[1], 1), :]], axis=1)
     spec = (dot(table[0], images, NT) + dot(table[1], images, NT)) * factor
@@ -124,6 +127,11 @@
     row = lax.broadcasted_iota(jnp.int32, (16, LANES), 0)
     tags = jnp.where(row == 0, high.astype(f32), jnp.where(row == 1, mid.astype(f32), jnp.where(row == 2, low, 0.0)))
     out[2 * HALF : MSG] = tags.astype(bf16)
+    copies = [pltpu.make_async_copy(out, outs.at[s], sem.at[s]) for s in range(SOURCES)]
+    for copy in copies:
+        copy.start()
+    for copy in copies:
+        copy.wait()
 
 
 def class_kernel(start, refs, table, out, power, images, rows, sem):
@@ -156,10 +164,10 @@
         out[j] = jnp.concatenate([plain, other], axis=0).astype(bf16)
         return carry
 
-    lax.fori_loop(0, HALF, step, 0, unroll=8)
-
-
-def score_kernel(place, own, other, rmat, power, table, expo, stats, by_class, ydata, csq, wide, pairs):
+    lax.fori_loop(0, HALF, step, 0, unroll=36)
+
+
+def score_kernel(place, own, other, rmat, power, table, expo, stats, by_class, csq, far, wide, pairs, ydata, sem):
     core, x_lo = place[0], place[1]
 
     def widen(s, carry):
@@ -191,15 +199,16 @@
         rows = jnp.concatenate([wide[pl.ds(j, many, stride=MSG), :], wide[pl.ds(HALF + j, many, stride=MSG), :]], axis=0)
         rows = rows.astype(bf16)
         ydata[j] = rows
-        both = dot(rmat[j], jnp.concatenate([rows, rows], axis=0), NT)
-        side = left((KROWS, LANES))
-        straight = jnp.where(side, both[:KROWS], both[KROWS : 2 * KROWS])
-        crossed = jnp.where(side, both[2 * KROWS : 3 * KROWS], both[3 * KROWS :])
+        both = dot(rmat[j], rows, NT)
+        straight = jnp.concatenate([both[:KROWS], both[KROWS : 2 * KROWS]], axis=1)
+        crossed = jnp.concatenate([both[2 * KROWS : 3 * KROWS], both[3 * KROWS :]], axis=1)
         pairs[pl.ds(j, KROWS, stride=ANG), :] = straight
         pairs[pl.ds(HALF + j, KROWS, stride=ANG), :] = crossed
         return carry
 
-    lax.fori_loop(0, HALF, step, 0, unroll=8)
+    lax.fori_loop(0, HALF, step, 0, unroll=48)
+    keep = pltpu.make_async_copy(ydata, far, sem)
+    keep.start()
     top = jnp.full((1, LANES), -3.0e38, f32)
     lane_side = left((ROT, LANES))
     for kk in range(KROWS):
@@ -220,37 +229,55 @@
         by_class[kk : kk + 1] = part
         total = total + part
     total = total + turn(total)
-    stats[...] = jnp.where(lax.broadcasted_iota(jnp.int32, (8, LANES), 0) == 0, top, total)
-
-
-def post_kernel(expo, table, out, rows):
+    pair = jnp.where(lax.broadcasted_iota(jnp.int32, (8, LANES), 0) == 0, top, total)
+    for s in range(CORE * SOURCES):
+        stats[s] = pair
+    keep.wait()
+
+
+def post_kernel(expo, table, far, rows, out, sem):
     for kk in range(KROWS):
         rows[kk * ANG : (kk + 1) * ANG] = dot3(table, expo[:, kk * LANES : (kk + 1) * LANES])
 
     def step(j, carry):
         real = rows[pl.ds(j, KROWS, stride=ANG), :]
         imag = rows[pl.ds(HALF + j, KROWS, stride=ANG), :]
-        out[j] = jnp.concatenate([real, turn(real), imag, turn(imag)], axis=0)
+        out[j] = jnp.concatenate([real, imag], axis=0)
         return carry
 
-    lax.fori_loop(0, HALF, step, 0, unroll=8)
-
-
-def sum_kernel(all_stats, stats, post, ydata, by_class, csq, out, rows, slots):
+    lax.fori_loop(0, HALF, step, 0, unroll=36)
+    keep = pltpu.make_async_copy(out, far, sem)
+    keep.start()
+    keep.wait()
+
+
+def sum_kernel(all_stats, stats, by_class, csq, far_post, far_ydata, out, rows, slots, post, ydata, sem):
+    copies = []
+    for part in range(PARTS):
+        lines = pl.ds(part * HALF // PARTS, HALF // PARTS)
+        copies.append(pltpu.make_async_copy(far_post.at[lines], post.at[lines], sem.at[0, part]))
+        copies.append(pltpu.make_async_copy(far_ydata.at[lines], ydata.at[lines], sem.at[1, part]))
+    for copy in copies:
+        copy.start()
     tops, totals = all_stats[:, 0, :], all_stats[:, 1, :]
     top = jnp.max(tops, axis=0, keepdims=True)
     total = jnp.sum(totals * jnp.exp(tops - top), axis=0, keepdims=True)
-    share = jnp.exp(stats[0:1] - top) / total
+    share = jnp.exp(stats[0, 0:1] - top) / total
 
     def step(j, carry):
-        weights = (post[j] * share)[:, :CYCLES].astype(bf16)
-        both = dot(weights, ydata[j])
+        wide = post[j] * share
+        real, imag = wide[:KROWS], wide[KROWS:]
+        weights = jnp.concatenate([real, turn(real), imag, turn(imag)], axis=0)[:, :CYCLES]
+        both = dot(weights.astype(bf16), ydata[j])
         other = turn(both[KPAD:])
         other = jnp.where(left(other.shape), other, -other)
         rows[pl.ds(j, KPAD, stride=HALF), :] = both[:KPAD] + other
         return carry
 
-    lax.fori_loop(0, HALF, step, 0, unroll=8)
+    for part in range(PARTS):
+        copies[2 * part].wait()
+        copies[2 * part + 1].wait()
+        lax.fori_loop(part * HALF // PARTS, (part + 1) * HALF // PARTS, step, 0, unroll=HALF // PARTS)
     mass = by_class[...] * share
     mass = jnp.concatenate([mass, turn(mass)], axis=0)[:, :CYCLES]
     weight = lax.dot_general(mass, csq[...], NN, precision=lax.Precision.HIGHEST, preferred_element_type=f32)
@@ -260,11 +287,26 @@
         first = z * CHUNK // HALF
         second = min(first + 1, KD - 1)
         base = z * SLOT
-        slots[base + SLOT - 16 : base + SLOT] = jnp.zeros((16, LANES), f32)
+        slots[base + SLOT - 8 : base + SLOT] = jnp.zeros((8, LANES), f32)
         slots[base : base + CHUNK] = rows[z * CHUNK : (z + 1) * CHUNK]
         slots[base + CHUNK : base + CHUNK + 1] = scales[first : first + 1]
         slots[base + CHUNK + 1 : base + CHUNK + 2] = scales[second : second + 1]
-        out[z] = slots[base : base + SLOT].astype(bf16)
+        out[z % ZL, z // ZL] = slots[base : base + SLOT].astype(bf16)
+
+
+def fold_kernel(pieces, out):
+    total = pieces[0].astype(f32)
+    for s in range(1, ZL):
+        total = total + pieces[s].astype(f32)
+    last = SLOT - 8
+    row = lax.broadcasted_iota(jnp.int32, (8, LANES), 0)
+    for h in range(ZH):
+        rows = total[h, last:]
+        scales = rows + turn(rows)
+        high = scales.astype(bf16).astype(f32)
+        scales = jnp.where(left(scales.shape), high, scales - high)
+        rows = jnp.where(row < CHUNK - last, rows, scales)
+        out[h] = jnp.concatenate([total[h, :last], rows], axis=0).astype(bf16)
 
 
 def image_kernel(place, hats, table, *rest):
@@ -276,11 +318,9 @@
         rows = flat[k * HALF : (k + 1) * HALF].T.astype(bf16)
         real[k * CYCLES : (k + 1) * CYCLES] = rows[:CYCLES]
         imag[k * CYCLES : (k + 1) * CYCLES] = rows[CYCLES:]
-    for k in range(KD):
-        lines = slice(k * CYCLES, (k + 1) * CYCLES)
-        image = dot(real[lines], table[0]) + dot(imag[lines], table[2])
-        image = image + (dot(real[lines], table[1]) + dot(imag[lines], table[3]))
-        stage[k] = image.astype(bf16)
+    image = dot(real[...], table[0]) + dot(imag[...], table[2])
+    image = image + (dot(real[...], table[1]) + dot(imag[...], table[3]))
+    stage[...] = image.astype(bf16).reshape(KD, CYCLES, ANG)
     base = core * PER_CORE + x_lo * (KD - 1)
     copy = pltpu.make_async_copy(stage.at[pl.ds(x_lo, KD - 1)], out.at[pl.ds(base + x_lo, KD - 1)], sem.at[0])
     copy.start()
@@ -296,10 +336,10 @@
 
 VMEM = pl.BlockSpec(memory_space=pltpu.VMEM)
 SMEM = pl.BlockSpec(memory_space=pltpu.SMEM)
-ANYWHERE = pl.BlockSpec(memory_space=pl.ANY)
-
-
-def call(kernel, ins, outs, scratch, flops, nbytes, aliases=None, out_specs=None):
+HBM = pl.BlockSpec(memory_space=pltpu.HBM)
+
+
+def call(kernel, ins, outs, scratch, flops, nbytes, aliases=None, out_specs=None, limit=48):
     out_shape = [jax.ShapeDtypeStruct(shape, dtype) for shape, dtype in outs]
     single = len(out_shape) == 1
     specs = out_specs or [VMEM] * len(out_shape)
@@ -310,7 +350,7 @@
         out_specs=specs[0] if single else specs,
         scratch_shapes=scratch,
         input_output_aliases=aliases or {},
-        compiler_params=pltpu.CompilerParams(vmem_limit_bytes=48 * 2**20),
+        compiler_params=pltpu.CompilerParams(vmem_limit_bytes=limit * 2**20),
         cost_estimate=pl.CostEstimate(flops=flops, bytes_accessed=nbytes, transcendentals=0),
     )
 
@@ -319,25 +359,23 @@
     return lax.ppermute(value, axis, [(0, 1), (1, 0)])
 
 
-def spread(value, axes, count):
-    return lax.all_to_all(jnp.broadcast_to(value[None], (count,) + value.shape), axes, 0, 0, tiled=True)
-
-
-def body(particles, group_ids, ctf_table, references):
-    core, x_lo, z = (lax.axis_index(name) for name in ("core", "x_lo", "z"))
-    forward = jnp.asarray(forward_table())
-    place = jnp.stack([core, x_lo])
-
-    message = call(
-        share_kernel, [SMEM, VMEM, VMEM, VMEM], [((MSG, LANES), bf16)], [], 10**7, 10**6
+def share(group_ids, particles, ctf_table, forward):
+    return call(
+        share_kernel,
+        [SMEM, VMEM, VMEM, VMEM],
+        [((SOURCES, MSG, LANES), bf16)],
+        [pltpu.VMEM((MSG, LANES), bf16), pltpu.SemaphoreType.DMA((SOURCES,))],
+        10**7,
+        10**6,
+        out_specs=[HBM],
+        limit=64,
     )(group_ids, particles, ctf_table, forward)
-    own = spread(message, ("x_lo", "x_hi", "y"), SOURCES)
-    other = swap("core", own)
-
-    start = (core * PER_CORE + x_lo * (KD - 1)).reshape(1)
-    rmat, power = call(
+
+
+def classes(start, references, forward):
+    return call(
         class_kernel,
-        [SMEM, ANYWHERE, VMEM],
+        [SMEM, HBM, VMEM],
         [((HALF, 2 * KPAD, LANES), bf16), ((KPAD, LANES), f32)],
         [
             pltpu.VMEM((KPAD, CYCLES, ANG), bf16),
@@ -346,82 +384,132 @@
         ],
         10**9,
         4 * 10**6,
+        limit=64,
     )(start, references, forward)
 
-    expo, stats, by_class, ydata, csq = call(
+
+def scores(place, own, other, rmat, power, table):
+    return call(
         score_kernel,
         [SMEM] + [VMEM] * 5,
         [
             ((ROT, KROWS * LANES), f32),
-            ((8, LANES), f32),
+            ((CORE * SOURCES, 8, LANES), f32),
             ((KROWS, LANES), f32),
+            ((COUNT, LANES), f32),
             ((HALF, COUNT, LANES), bf16),
-            ((COUNT, LANES), f32),
         ],
         [
             pltpu.VMEM((CORE * SOURCES * MSG, LANES), f32),
             pltpu.VMEM((KROWS * ANG, LANES), f32),
+            pltpu.VMEM((HALF, COUNT, LANES), bf16),
+            pltpu.SemaphoreType.DMA,
         ],
         10**9,
         8 * 10**6,
-    )(place, own, other, rmat, power, jnp.asarray(search_table()))
-    all_stats = spread(stats, ("core", "x_lo", "x_hi", "y"), CORE * SOURCES)
-    post = call(
+        limit=64,
+        out_specs=[VMEM] * 4 + [HBM],
+    )(place, own, other, rmat, power, table)
+
+
+def posts(expo, table):
+    return call(
         post_kernel,
         [VMEM, VMEM],
-        [((HALF, 2 * KPAD, LANES), f32)],
-        [pltpu.VMEM((KROWS * ANG, LANES), f32)],
+        [((HALF, KPAD, LANES), f32)],
+        [
+            pltpu.VMEM((KROWS * ANG, LANES), f32),
+            pltpu.VMEM((HALF, KPAD, LANES), f32),
+            pltpu.SemaphoreType.DMA,
+        ],
         10**9,
         3 * 10**6,
-    )(expo, jnp.asarray(post_table()))
-    sums = call(
+        limit=64,
+        out_specs=[HBM],
+    )(expo, table)
+
+
+def sums_of(all_stats, stats, by_class, csq, post, ydata):
+    return call(
         sum_kernel,
-        [VMEM] * 6,
-        [((Z, SLOT, LANES), bf16)],
-        [pltpu.VMEM((KPAD * HALF, LANES), f32), pltpu.VMEM((Z * SLOT, LANES), f32)],
+        [VMEM] * 4 + [HBM] * 2,
+        [((ZL, ZH, SLOT, LANES), bf16)],
+        [
+            pltpu.VMEM((KPAD * HALF, LANES), f32),
+            pltpu.VMEM((Z * SLOT, LANES), f32),
+            pltpu.VMEM((HALF, KPAD, LANES), f32),
+            pltpu.VMEM((HALF, COUNT, LANES), bf16),
+            pltpu.SemaphoreType.DMA((2, PARTS)),
+        ],
         10**9,
         8 * 10**6,
-    )(all_stats, stats, post, ydata, by_class, csq)
-
-    got = jnp.sum(lax.all_to_all(sums, "z", 0, 0, tiled=True).astype(f32), axis=0)
+        limit=64,
+    )(all_stats, stats, by_class, csq, post, ydata)
+
+
+def images(which, hats, inverse, result):
+    extra = [] if result is None else [result]
+    return call(
+        image_kernel,
+        [SMEM, VMEM, VMEM] + [HBM] * len(extra),
+        [((CORE * PER_CORE, CYCLES, ANG), bf16)],
+        [
+            pltpu.VMEM((KD * HALF, LANES), f32),
+            pltpu.VMEM((KD * CYCLES, HALF), bf16),
+            pltpu.VMEM((KD * CYCLES, HALF), bf16),
+            pltpu.VMEM((KD, CYCLES, ANG), bf16),
+            pltpu.SemaphoreType.DMA((2,)),
+        ],
+        1000,
+        1000,
+        {3: 0} if extra else None,
+        [HBM],
+    )(which, hats, inverse, *extra)
+
+
+def body(particles, group_ids, ctf_table, references):
+    core, x_lo, z = (lax.axis_index(name) for name in ("core", "x_lo", ("z_hi", "z_lo")))
+    forward = jnp.asarray(forward_table())
+    place = jnp.stack([core, x_lo])
+
+    messages = share(group_ids, particles, ctf_table, forward)
+    own = lax.all_to_all(messages, ("x_lo", "x_hi", "y"), 0, 0, tiled=True)
+    start = (core * PER_CORE + x_lo * (KD - 1)).reshape(1)
+    rmat, power = classes(start, references, forward)
+    row = lax.broadcasted_iota(jnp.int32, (SLOT, LANES), 0)
+    edge = (z * CHUNK // HALF + 1) * HALF - z * CHUNK
+    before = (row < edge).astype(f32)
+    own, rmat, power, before = lax.optimization_barrier((own, rmat, power, before))
+    other = swap("core", own)
+
+    expo, stats, by_class, csq, ydata = scores(
+        place, own, other, rmat, power, jnp.asarray(search_table().reshape(2 * ROT, ANG))
+    )
+    all_stats = lax.all_to_all(stats, ("core", "x_lo", "x_hi", "y"), 0, 0, tiled=True)
+    post = posts(expo, jnp.asarray(post_table().reshape(2 * ANG, ROT)))
+    sums = sums_of(all_stats, stats, by_class, csq, post, ydata)
+
+    near = lax.all_to_all(sums, "z_lo", 0, 0, tiled=True)
+    near = call(fold_kernel, [VMEM], [((ZH, SLOT, LANES), bf16)], [], 10**6, 10**6, limit=20)(near)
+    got = jnp.sum(lax.all_to_all(near, "z_hi", 0, 0, tiled=True).astype(f32), axis=0)
     scales = got[CHUNK : CHUNK + 2]
     scales = scales[:, :CYCLES] + scales[:, CYCLES:] + PRIOR_WEIGHT
     scales = jnp.concatenate([scales, scales], axis=1)
-    row = lax.broadcasted_iota(jnp.int32, (SLOT, LANES), 0)
-    edge = (z * CHUNK // HALF + 1) * HALF - z * CHUNK
-    hat = (got / jnp.where(row < edge, scales[:1], scales[1:])).astype(bf16)
-
-    near = lax.all_gather(hat, "z")
+    hat = (got / jnp.where(before > 0.5, scales[:1], scales[1:])).astype(bf16)
+
+    inverse = jnp.asarray(inverse_table())
+    near = lax.all_gather(hat, ("z_hi", "z_lo"))
     far = swap("x_lo", near)
-    inverse = jnp.asarray(inverse_table())
-    result = None
-    for hats, which in (
-        (near, (core, x_lo)),
-        (swap("core", near), (1 - core, x_lo)),
-        (far, (core, 1 - x_lo)),
-        (swap("core", far), (1 - core, 1 - x_lo)),
-    ):
-        extra = [] if result is None else [result]
-        result = call(
-            image_kernel,
-            [SMEM, VMEM, VMEM] + [ANYWHERE] * len(extra),
-            [((CORE * PER_CORE, CYCLES, ANG), bf16)],
-            [
-                pltpu.VMEM((KD * HALF, LANES), f32),
-                pltpu.VMEM((KD * CYCLES, HALF), bf16),
-                pltpu.VMEM((KD * CYCLES, HALF), bf16),
-                pltpu.VMEM((KD, CYCLES, ANG), bf16),
-                pltpu.SemaphoreType.DMA((2,)),
-            ],
-            10**9,
-            2 * 10**6,
-            {3: 0} if extra else None,
-            [ANYWHERE],
-        )(jnp.stack(which), hats, inverse, *extra)
-    return result
+    near_other = swap("core", near)
+    result = images(jnp.stack([core, x_lo]), near, inverse, None)
+    far, result = lax.optimization_barrier((far, result))
+    far_other = swap("core", far)
+    result = images(jnp.stack([core, 1 - x_lo]), far, inverse, result)
+    result = images(jnp.stack([1 - core, x_lo]), near_other, inverse, result)
+    return images(jnp.stack([1 - core, 1 - x_lo]), far_other, inverse, result)
 
 
 def solution(mesh):
-    fine = Mesh(mesh.devices.reshape(X, Z, CORE, 2, 4), DOM + CLS)
+    fine = Mesh(mesh.devices.reshape(X, ZH, ZL, CORE, 2, 4), DOM + CLS)
     in_specs = (P(DOM + CLS, None, None), P(DOM + CLS), P(), P(CLS, None, None))
     return jax.shard_map(body, mesh=fine, in_specs=in_specs, out_specs=P(CLS, None, None), check_vma=False)

time: 168 us -> 158 us (0.940)
  blocking collectives: 52.3 us -> 66.3 us
  starting transfers between devices: 49.2 us -> 38.7 us
  waiting for transfers between devices: 26.4 us -> 16.3 us
  local copies, waits for them, and re-layouts: 8.91 us -> 0.72 us
  Pallas kernels: 30.2 us -> 33 us
    all_to_all x1 -> x2, blocking collectives: 24.3 us -> 44.1 us  [the longest x1 25.7 us: body(): lax.all_to_all(near, 'z_hi', 0, 0, tiled=True).astype(f32)]
    all_to_all x2, waiting for transfers between devices: 26.4 us -> 13.9 us  [the longest x1 9.66 us: body(): own = lax.all_to_all(messages, ('x_lo', 'x_hi', 'y'), 0, 0, tiled=True)]
    unnamed x24 -> x4, local copies, waits for them, and re-layouts: 8.08 us -> 0.01 us
    all_to_all x2, starting transfers between devices: 18.8 us -> 12.3 us  [the longest x1 7.64 us: body(): own = lax.all_to_all(messages, ('x_lo', 'x_hi', 'y'), 0, 0, tiled=True)]
    all_gather x1, blocking collectives: 28 us -> 22.2 us  [body(): near = lax.all_gather(hat, ('z_hi', 'z_lo'))]
    ppermute x4, starting transfers between devices: 30.4 us -> 26.4 us  [swap(): return lax.ppermute(value, axis, [(0, 1), (1, 0)])]
    pallas_call x9 -> x10, Pallas kernels: 30.2 us -> 33 us  [the longest x4 10.2 us: images(): call(image_kernel, [SMEM, VMEM, VMEM] + [HBM] * len(extra), [((CORE * PER...]
    ppermute x4, waiting for transfers between devices: 0.01 us -> 2.3 us  [swap(): return lax.ppermute(value, axis, [(0, 1), (1, 0)])]
  transfers between devices with their start and end apart: 6 -> 6, of which waited for: 2 -> 3; matrix products, arithmetic and copies ran while one was open for 0% -> 0% of each run, Pallas kernels for 8% -> 10%
where the time goes in v3:
time: 158 us; the launch traced here: 157 us
  blocking collectives  66.3 us (42%)
  starting transfers between devices  38.7 us (24%)
  Pallas kernels  33 us (21%)
  waiting for transfers between devices  16.3 us (10%)
  other arithmetic  1.77 us (1%)
    ppermute x4, starting transfers between devices, swap(): return lax.ppermute(value, axis, [(0, 1), (1, 0)])  26.4 us
    all_to_all x1, blocking collectives, body(): lax.all_to_all(near, 'z_hi', 0, 0, tiled=True).astype(f32)  25.7 us
    all_gather x1, blocking collectives, body(): near = lax.all_gather(hat, ('z_hi', 'z_lo'))  22.2 us
    all_to_all x1, blocking collectives, body(): near = lax.all_to_all(sums, 'z_lo', 0, 0, tiled=True)  18.4 us
    pallas_call x4, Pallas kernels, images(): call(image_kernel, [SMEM, VMEM, VMEM] + [HBM] * len(extra), [((CORE * PER...  10.2 us
    all_to_all x1, waiting for transfers between devices, body(): own = lax.all_to_all(messages, ('x_lo', 'x_hi', 'y'), 0, 0, tiled=True)  9.66 us
    all_to_all x1, starting transfers between devices, body(): own = lax.all_to_all(messages, ('x_lo', 'x_hi', 'y'), 0, 0, tiled=True)  7.64 us
    pallas_call x1, Pallas kernels, scores(): call(score_kernel, [SMEM] + [VMEM] * 5, [((ROT, KROWS * LANES), f32), ((C...  7.16 us
  transfers between devices with their start and end apart: 6, of which 3 were waited for; matrix products, arithmetic and copies ran while one was open for 0% of the time, Pallas kernels for 10%

profile of v3, /device:TPU:1, one launch (start us, length us, event | category | flops | bytes accessed | tf_op | source)
XLA Modules:
  0.0 157.0 jit_solution(17094461979085882002)
XLA Ops:
  0.0 2.6 %shard_map.82 = bf16[16,304,128]{2,1,0:T(8,128)(2,1)} custom-call(s32[2]{0:T(128)} %ids.1, bf16[2,64,288]{2,1,0:T(8,128)(2,1)} %x.1, f32[32,64]{1,0:T(8,128)} %ctf.1, bf16[2,288,288]{2,1,0:T(8,128)(2,1)} %constant.53.clone.table), custom_call_target="tpu_custom_call" | custom-call | flops 10000000 | bytes 1000000 | tf_op jit(solution)/shard_map/pallas_call | solution.py:363
  2.6 7.6 %all-to-all-start = ((bf16[16,304,128]{2,1,0:T(8,128)(2,1)}), bf16[16,304,128]{2,1,0:T(8,128)(2,1)}, u32[]{:S(2)}, u32[]{:S(2)}) async-start(bf16[16,304,128]{2,1,0:T(8,128)(2,1)} %shard_map.82), calls=%async_computation | async-start | bytes 2490368 | tf_op jit(solution)/shard_map/all_to_all | solution.py:476
  10.3 5.1 %shard_map.83 = (bf16[144,32,128]{2,1,0:T(8,128)(2,1)}, f32[16,128]{1,0:T(8,128)}) custom-call(s32[1]{0:T(128)} %bitcast.4.start, bf16[50,64,288]{2,1,0:T(8,128)(2,1)} %refs.1, bf16[2,288,288]{2,1,0:T(8,128)(2,1)} %constant.53.clone.table), custom_call_target="tpu_custom_call" | custom-call | flops 1000000000 | bytes 4000000 | tf_op jit(solution)/shard_map/pallas_call | solution.py:376
  15.4 9.7 %all-to-all-done.own = bf16[16,304,128]{2,1,0:T(8,128)(2,1)} async-done(((bf16[16,304,128]{2,1,0:T(8,128)(2,1)}), bf16[16,304,128]{2,1,0:T(8,128)(2,1)}, u32[]{:S(2)}, u32[]{:S(2)}) %all-to-all-start) | async-done | bytes 1245216 | tf_op jit(solution)/shard_map/all_to_all | solution.py:476
  25.1 0.7 iota.7
  25.8 7.2 %collective-permute-start = (bf16[16,304,128]{2,1,0:T(8,128)(2,1)}, bf16[16,304,128]{2,1,0:T(8,128)(2,1)}, u32[]{:S(2)}, u32[]{:S(2)}) collective-permute-start(bf16[16,304,128]{2,1,0:T(8,128)(2,1)} %all-to-all-done.own), channel_id=1, source_target_pairs={{0,8},{8,0},{1,9},{9,1},{2,10},{10,2},{3,11},{11,3},{4,12},{12,4},... | collective-permute-start | bytes 3735560 | tf_op jit(solution)/shard_map/ppermute | solution.py:359
  33.0 0.6 pad_add_fusion.3.place
  33.6 2.3 %collective-permute-done.other = bf16[16,304,128]{2,1,0:T(8,128)(2,1)} collective-permute-done((bf16[16,304,128]{2,1,0:T(8,128)(2,1)}, bf16[16,304,128]{2,1,0:T(8,128)(2,1)}, u32[]{:S(2)}, u32[]{:S(2)}) %collective-permute-start) | collective-permute-done | bytes 1245216 | tf_op jit(solution)/shard_map/ppermute | solution.py:359
  35.9 7.2 %shard_map.84 = (f32[72,1024]{1,0:T(8,128)}, f32[32,8,128]{2,1,0:T(8,128)}, f32[8,128]{1,0:T(8,128)}, f32[64,128]{1,0:T(8,128)}, bf16[144,64,128]{2,1,0:T(8,128)(2,1)}) custom-call(s32[2]{0:T(128)} %pad_add_fusion.3.place, bf16[16,304,128]{2,1,0:T(8,128)(2,1)} %all-to-all-done.own, bf16[16,304,128]{2,1,0:T(8,128)(2,1)} %collective-permute-done.other, ...), custom_call_target="tpu_custom_call" | custom-call | flops 1000000000 | bytes 8000000 | tf_op jit(solution)/shard_map/pallas_call | solution.py:392
  43.0 4.6 %all-to-all-start.1 = ((f32[32,8,128]{2,1,0:T(8,128)}), f32[32,8,128]{2,1,0:T(8,128)}, u32[]{:S(2)}, u32[]{:S(2)}) async-start(f32[32,8,128]{2,1,0:T(8,128)} %get-tuple-element.23.stats), calls=%async_computation.1 | async-start | bytes 262144 | tf_op jit(solution)/shard_map/all_to_all | solution.py:488
  47.7 3.3 %shard_map.85.far_post = f32[144,16,128]{2,1,0:T(8,128)} custom-call(f32[72,1024]{1,0:T(8,128)} %get-tuple-element.26.expo, bf16[576,72]{1,0:T(8,128)(2,1)} %constant.55.clone.table), custom_call_target="tpu_custom_call" | custom-call | flops 1000000000 | bytes 3000000 | tf_op jit(solution)/shard_map/pallas_call | solution.py:416
  51.0 4.3 %all-to-all-done.1.all_stats = f32[32,8,128]{2,1,0:T(8,128)} async-done(((f32[32,8,128]{2,1,0:T(8,128)}), f32[32,8,128]{2,1,0:T(8,128)}, u32[]{:S(2)}, u32[]{:S(2)}) %all-to-all-start.1) | async-done | bytes 131104 | tf_op jit(solution)/shard_map/all_to_all | solution.py:488
  55.3 4.6 %shard_map.86 = bf16[4,4,120,128]{3,2,1,0:T(8,128)(2,1)} custom-call(f32[32,8,128]{2,1,0:T(8,128)} %all-to-all-done.1.all_stats, f32[32,8,128]{2,1,0:T(8,128)} %get-tuple-element.23.stats, f32[8,128]{1,0:T(8,128)} %get-tuple-element.24.by_class, f32[64,128]{1,0:T(8,128)} %get-tuple-element.25.csq, f32[144,16,128]{2,1,0:T(8,128)} %shard_map.85.far_post, ...), custom_call_target="tpu_custom_call" | custom-call | flops 1000000000 | bytes 8000000 | tf_op jit(solution)/shard_map/pallas_call | solution.py:433
  59.9 18.4 %all_to_all.20.pieces = bf16[4,4,120,128]{3,2,1,0:T(8,128)(2,1)S(1)} all-to-all(bf16[4,4,120,128]{3,2,1,0:T(8,128)(2,1)} %shard_map.86), channel_id=1, replica_groups=mesh['x_lo'=2,'z_hi'=4,'z_lo'=4,'core'=2,'x_hi'=2,'y'=4] {'z_lo'}, dimensions={0} | all-to-all | bytes 983040 | tf_op jit(solution)/shard_map/all_to_all | solution.py:492
  78.4 25.7 %all_to_all.21 = bf16[4,120,128]{2,1,0:T(8,128)(2,1)S(1)} all-to-all(bf16[4,120,128]{2,1,0:T(8,128)(2,1)S(1)} %shard_map.87), channel_id=1, replica_groups=mesh['x_lo'=2,'z_hi'=4,'z_lo'=4,'core'=2,'x_hi'=2,'y'=4] {'z_hi'}, dimensions={0} | all-to-all | bytes 245760 | tf_op jit(solution)/shard_map/all_to_all | solution.py:494
  104.2 0.8 divide_convert_fusion
  105.1 22.2 %all-gather = bf16[1920,128]{1,0:T(8,128)(2,1)S(1)} all-gather(bf16[120,128]{1,0:T(8,128)(2,1)S(1)} %divide_convert_fusion), channel_id=2, replica_groups=mesh['x_lo'=2,'z_hi'=4,'z_lo'=4,'core'=2,'x_hi'=2,'y'=4] {'z_hi','z_lo'}, dimensions={0}, use_global_device_ids=true | all-gather | bytes 522240 | tf_op jit(solution)/shard_map/all_gather | solution.py:501
  127.3 2.2 %collective-permute-start.1 = (bf16[16,120,128]{2,1,0:T(8,128)(2,1)S(1)}, bf16[16,120,128]{2,1,0:T(8,128)(2,1)S(1)}, u32[]{:S(2)}, u32[]{:S(2)}) collective-permute-start(bf16[16,120,128]{2,1,0:T(8,128)(2,1)S(1)} %bitcast.10), channel_id=1, source_target_pairs={{0,256},{256,0},{1,257},{257,1},{2,258},{258,2},{3,259},{259,3},{4... | collective-permute-start | bytes 1474568 | tf_op jit(solution)/shard_map/ppermute | solution.py:359
  129.5 11.4 %collective-permute-start.3 = (bf16[16,120,128]{2,1,0:T(8,128)(2,1)S(1)}, bf16[16,120,128]{2,1,0:T(8,128)(2,1)S(1)}, u32[]{:S(2)}, u32[]{:S(2)}) collective-permute-start(bf16[16,120,128]{2,1,0:T(8,128)(2,1)S(1)} %bitcast.11), channel_id=1, source_target_pairs={{0,8},{8,0},{1,9},{9,1},{2,10},{10,2},{3,11},{11,3},{4,12},{12,4},... | collective-permute-start | bytes 1474568 | tf_op jit(solution)/shard_map/ppermute | solution.py:359
  140.9 2.6 %shard_map.88.rest_0_ = bf16[50,64,288]{2,1,0:T(8,128)(2,1)} custom-call(s32[2]{0:T(128)S(1)} %copy-done.1, bf16[16,120,128]{2,1,0:T(8,128)(2,1)S(1)} %bitcast.12, bf16[4,144,288]{2,1,0:T(8,128)(2,1)S(1)} %copy-done), custom_call_target="tpu_custom_call" | custom-call | flops 1000 | bytes 1000 | tf_op jit(solution)/shard_map/pallas_call | solution.py:452
  143.5 5.6 %collective-permute-start.2 = (bf16[16,120,128]{2,1,0:T(8,128)(2,1)S(1)}, bf16[16,120,128]{2,1,0:T(8,128)(2,1)S(1)}, u32[]{:S(2)}, u32[]{:S(2)}) collective-permute-start(bf16[16,120,128]{2,1,0:T(8,128)(2,1)S(1)} %collective-permute-done.1.hats), channel_id=1, source_target_pairs={{0,8},{8,0},{1,9},{9,1},{2,10},{10,2},{3,11},{11,3},{4,12},{12,4},... | collective-permute-start | bytes 1474568 | tf_op jit(solution)/shard_map/ppermute | solution.py:359
  149.2 2.6 %shard_map.89.rest_0_ = bf16[50,64,288]{2,1,0:T(8,128)(2,1)} custom-call(s32[2]{0:T(128)S(1)} %pad_add_fusion.place, bf16[16,120,128]{2,1,0:T(8,128)(2,1)S(1)} %collective-permute-done.1.hats, bf16[4,144,288]{2,1,0:T(8,128)(2,1)S(1)} %copy-done, bf16[50,64,288]{2,1,0:T(8,128)(2,1)} %shard_map.88.rest_0_), custom_call_target="tpu_custom_call", output_to_operand_aliasing={{}: (3, {})} | custom-call | flops 1000 | bytes 1000 | tf_op jit(solution)/shard_map/pallas_call | solution.py:452
  151.8 2.6 %shard_map.90.rest_0_ = bf16[50,64,288]{2,1,0:T(8,128)(2,1)} custom-call(s32[2]{0:T(128)S(1)} %get-tuple-element.34.place, bf16[16,120,128]{2,1,0:T(8,128)(2,1)S(1)} %collective-permute-done.3.hats, bf16[4,144,288]{2,1,0:T(8,128)(2,1)S(1)} %copy-done, bf16[50,64,288]{2,1,0:T(8,128)(2,1)} %shard_map.89.rest_0_), custom_call_target="tpu_custom_call", output_to_operand_aliasing={{}: (3, {})} | custom-call | flops 1000 | bytes 1000 | tf_op jit(solution)/shard_map/pallas_call | solution.py:452
  154.4 2.6 %shard_map.91 = bf16[50,64,288]{2,1,0:T(8,128)(2,1)} custom-call(s32[2]{0:T(128)S(1)} %get-tuple-element.33.place, bf16[16,120,128]{2,1,0:T(8,128)(2,1)S(1)} %collective-permute-done.2.hats, bf16[4,144,288]{2,1,0:T(8,128)(2,1)S(1)} %copy-done, bf16[50,64,288]{2,1,0:T(8,128)(2,1)} %shard_map.90.rest_0_), custom_call_target="tpu_custom_call", output_to_operand_aliasing={{}: (3, {})} | custom-call | flops 1000 | bytes 1000 | tf_op jit(solution)/shard_map/pallas_call | solution.py:452
  (15 shorter events, 0.4 us)
Async XLA Ops:
  2.6 22.4 %all-to-all-start = ((bf16[16,304,128]{2,1,0:T(8,128)(2,1)}), bf16[16,304,128]{2,1,0:T(8,128)(2,1)}, u32[]{:S(2)}, u32[]{:S(2)}) async-start(bf16[16,304,128]{2,1,0:T(8,128)(2,1)} %shard_map.82), calls=%async_computation | async-start | bytes 2490368 | tf_op jit(solution)/shard_map/all_to_all | solution.py:476
  25.8 10.1 %collective-permute-start = (bf16[16,304,128]{2,1,0:T(8,128)(2,1)}, bf16[16,304,128]{2,1,0:T(8,128)(2,1)}, u32[]{:S(2)}, u32[]{:S(2)}) collective-permute-start(bf16[16,304,128]{2,1,0:T(8,128)(2,1)} %all-to-all-done.own), channel_id=1, source_target_pairs={{0,8},{8,0},{1,9},{9,1},{2,10},{10,2},{3,11},{11,3},{4,12},{12,4},... | collective-permute-start | bytes 3735560 | tf_op jit(solution)/shard_map/ppermute | solution.py:359
  43.0 12.3 %all-to-all-start.1 = ((f32[32,8,128]{2,1,0:T(8,128)}), f32[32,8,128]{2,1,0:T(8,128)}, u32[]{:S(2)}, u32[]{:S(2)}) async-start(f32[32,8,128]{2,1,0:T(8,128)} %get-tuple-element.23.stats), calls=%async_computation.1 | async-start | bytes 262144 | tf_op jit(solution)/shard_map/all_to_all | solution.py:488
  59.9 81.0 %copy-start = (bf16[4,144,288]{2,1,0:T(8,128)(2,1)S(1)}, bf16[4,144,288]{2,1,0:T(8,128)(2,1)}, u32[]{:S(2)}) copy-start(bf16[4,144,288]{2,1,0:T(8,128)(2,1)} %constant.56.clone.table) | copy-start | bytes 995332
  59.9 81.0 %copy-start.1 = (s32[2]{0:T(128)S(1)}, s32[2]{0:T(128)}, u32[]{:S(2)}) copy-start(s32[2]{0:T(128)} %pad_add_fusion.3.place) | copy-start | bytes 28
  127.3 16.2 %collective-permute-start.1 = (bf16[16,120,128]{2,1,0:T(8,128)(2,1)S(1)}, bf16[16,120,128]{2,1,0:T(8,128)(2,1)S(1)}, u32[]{:S(2)}, u32[]{:S(2)}) collective-permute-start(bf16[16,120,128]{2,1,0:T(8,128)(2,1)S(1)} %bitcast.10), channel_id=1, source_target_pairs={{0,256},{256,0},{1,257},{257,1},{2,258},{258,2},{3,259},{259,3},{4... | collective-permute-start | bytes 1474568 | tf_op jit(solution)/shard_map/ppermute | solution.py:359
  129.5 22.3 %collective-permute-start.3 = (bf16[16,120,128]{2,1,0:T(8,128)(2,1)S(1)}, bf16[16,120,128]{2,1,0:T(8,128)(2,1)S(1)}, u32[]{:S(2)}, u32[]{:S(2)}) collective-permute-start(bf16[16,120,128]{2,1,0:T(8,128)(2,1)S(1)} %bitcast.11), channel_id=1, source_target_pairs={{0,8},{8,0},{1,9},{9,1},{2,10},{10,2},{3,11},{11,3},{4,12},{12,4},... | collective-permute-start | bytes 1474568 | tf_op jit(solution)/shard_map/ppermute | solution.py:359
  143.5 10.9 %collective-permute-start.2 = (bf16[16,120,128]{2,1,0:T(8,128)(2,1)S(1)}, bf16[16,120,128]{2,1,0:T(8,128)(2,1)S(1)}, u32[]{:S(2)}, u32[]{:S(2)}) collective-permute-start(bf16[16,120,128]{2,1,0:T(8,128)(2,1)S(1)} %collective-permute-done.1.hats), channel_id=1, source_target_pairs={{0,8},{8,0},{1,9},{9,1},{2,10},{10,2},{3,11},{11,3},{4,12},{12,4},... | collective-permute-start | bytes 1474568 | tf_op jit(solution)/shard_map/ppermute | solution.py:359

commit v4 on v3

--- a/solution.py
+++ b/solution.py
@@ -29,8 +29,9 @@
 SOURCES = X * SIDE
 COUNT = MINE * CORE * SOURCES
 MSG = MINE * HALF + 16
-CHUNK = KD * HALF // Z
-SLOT = 120
+CHUNK = KD * HALF // ZL
+SPAN = -(-CHUNK // HALF) + 1
+SLOT = 480
 
 DOM = ("x_lo", "z_hi", "z_lo", "core")
 CLS = ("x_hi", "y")
@@ -283,37 +284,49 @@
     weight = lax.dot_general(mass, csq[...], NN, precision=lax.Precision.HIGHEST, preferred_element_type=f32)
     high, low = halves(weight)
     scales = jnp.where(left(weight.shape), high.astype(f32), turn(low.astype(f32)))
-    for z in range(Z):
-        first = z * CHUNK // HALF
-        second = min(first + 1, KD - 1)
-        base = z * SLOT
-        slots[base + SLOT - 8 : base + SLOT] = jnp.zeros((8, LANES), f32)
-        slots[base : base + CHUNK] = rows[z * CHUNK : (z + 1) * CHUNK]
-        slots[base + CHUNK : base + CHUNK + 1] = scales[first : first + 1]
-        slots[base + CHUNK + 1 : base + CHUNK + 2] = scales[second : second + 1]
-        out[z % ZL, z // ZL] = slots[base : base + SLOT].astype(bf16)
+    for part in range(ZL):
+        first = part * CHUNK // HALF
+        base = part * SLOT
+        slots[base + CHUNK : base + SLOT] = jnp.zeros((SLOT - CHUNK, LANES), f32)
+        slots[base : base + CHUNK] = rows[part * CHUNK : (part + 1) * CHUNK]
+        slots[base + CHUNK : base + CHUNK + SPAN] = scales[first : first + SPAN]
+        out[part] = slots[base : base + SLOT].astype(bf16)
+
+
+LAST = CHUNK // 8 * 8
 
 
 def fold_kernel(pieces, out):
     total = pieces[0].astype(f32)
     for s in range(1, ZL):
         total = total + pieces[s].astype(f32)
-    last = SLOT - 8
-    row = lax.broadcasted_iota(jnp.int32, (8, LANES), 0)
-    for h in range(ZH):
-        rows = total[h, last:]
-        scales = rows + turn(rows)
-        high = scales.astype(bf16).astype(f32)
-        scales = jnp.where(left(scales.shape), high, scales - high)
-        rows = jnp.where(row < CHUNK - last, rows, scales)
-        out[h] = jnp.concatenate([total[h, :last], rows], axis=0).astype(bf16)
+    rows = total[LAST:]
+    scales = rows + turn(rows)
+    high = scales.astype(bf16).astype(f32)
+    scales = jnp.where(left(scales.shape), high, scales - high)
+    row = lax.broadcasted_iota(jnp.int32, rows.shape, 0)
+    rows = jnp.where(row < CHUNK - LAST, rows, scales)
+    out[...] = jnp.concatenate([total[:LAST], rows], axis=0).astype(bf16)
+
+
+def hat_kernel(part, pieces, out):
+    total = pieces[0].astype(f32)
+    for s in range(1, ZH):
+        total = total + pieces[s].astype(f32)
+    scales = total[CHUNK : CHUNK + SPAN]
+    scales = 1.0 / (scales + turn(scales) + PRIOR_WEIGHT)
+    row = lax.broadcasted_iota(jnp.int32, total.shape, 0) + part[0] * (CHUNK % HALF)
+    factor = jnp.broadcast_to(scales[SPAN - 1 :], total.shape)
+    for i in range(SPAN - 2, -1, -1):
+        factor = jnp.where(row < (i + 1) * HALF, scales[i : i + 1], factor)
+    out[...] = (total * factor).astype(bf16)
 
 
 def image_kernel(place, hats, table, *rest):
     out, flat, real, imag, stage, sem = rest[-6:]
     core, x_lo = place[0], place[1]
-    for z in range(Z):
-        flat[z * CHUNK : (z + 1) * CHUNK] = hats[z].astype(f32)[:CHUNK]
+    for part in range(ZL):
+        flat[part * CHUNK : (part + 1) * CHUNK] = hats[part].astype(f32)[:CHUNK]
     for k in range(KD):
         rows = flat[k * HALF : (k + 1) * HALF].T.astype(bf16)
         real[k * CYCLES : (k + 1) * CYCLES] = rows[:CYCLES]
@@ -433,10 +446,10 @@
     return call(
         sum_kernel,
         [VMEM] * 4 + [HBM] * 2,
-        [((ZL, ZH, SLOT, LANES), bf16)],
+        [((ZL, SLOT, LANES), bf16)],
         [
             pltpu.VMEM((KPAD * HALF, LANES), f32),
-            pltpu.VMEM((Z * SLOT, LANES), f32),
+            pltpu.VMEM((ZL * SLOT, LANES), f32),
             pltpu.VMEM((HALF, KPAD, LANES), f32),
             pltpu.VMEM((HALF, COUNT, LANES), bf16),
             pltpu.SemaphoreType.DMA((2, PARTS)),
@@ -468,7 +481,7 @@
 
 
 def body(particles, group_ids, ctf_table, references):
-    core, x_lo, z = (lax.axis_index(name) for name in ("core", "x_lo", ("z_hi", "z_lo")))
+    core, x_lo = lax.axis_index("core"), lax.axis_index("x_lo")
     forward = jnp.asarray(forward_table())
     place = jnp.stack([core, x_lo])
 
@@ -476,10 +489,8 @@
     own = lax.all_to_all(messages, ("x_lo", "x_hi", "y"), 0, 0, tiled=True)
     start = (core * PER_CORE + x_lo * (KD - 1)).reshape(1)
     rmat, power = classes(start, references, forward)
-    row = lax.broadcasted_iota(jnp.int32, (SLOT, LANES), 0)
-    edge = (z * CHUNK // HALF + 1) * HALF - z * CHUNK
-    before = (row < edge).astype(f32)
-    own, rmat, power, before = lax.optimization_barrier((own, rmat, power, before))
+    part = lax.axis_index("z_lo").reshape(1)
+    own, rmat, power, part = lax.optimization_barrier((own, rmat, power, part))
     other = swap("core", own)
 
     expo, stats, by_class, csq, ydata = scores(
@@ -490,15 +501,12 @@
     sums = sums_of(all_stats, stats, by_class, csq, post, ydata)
 
     near = lax.all_to_all(sums, "z_lo", 0, 0, tiled=True)
-    near = call(fold_kernel, [VMEM], [((ZH, SLOT, LANES), bf16)], [], 10**6, 10**6, limit=20)(near)
-    got = jnp.sum(lax.all_to_all(near, "z_hi", 0, 0, tiled=True).astype(f32), axis=0)
-    scales = got[CHUNK : CHUNK + 2]
-    scales = scales[:, :CYCLES] + scales[:, CYCLES:] + PRIOR_WEIGHT
-    scales = jnp.concatenate([scales, scales], axis=1)
-    hat = (got / jnp.where(before > 0.5, scales[:1], scales[1:])).astype(bf16)
+    near = call(fold_kernel, [VMEM], [((SLOT, LANES), bf16)], [], 10**6, 10**6, limit=20)(near)
+    near = lax.all_gather(near, "z_hi")
+    hat = call(hat_kernel, [SMEM, VMEM], [((SLOT, LANES), bf16)], [], 10**6, 10**6, limit=20)(part, near)
 
     inverse = jnp.asarray(inverse_table())
-    near = lax.all_gather(hat, ("z_hi", "z_lo"))
+    near = lax.all_gather(hat, "z_lo")
     far = swap("x_lo", near)
     near_other = swap("core", near)
     result = images(jnp.stack([core, x_lo]), near, inverse, None)

time: 158 us -> 147 us (0.930)
  blocking collectives: 66.3 us -> 58.5 us
    all_to_all x1 -> x0, blocking collectives: 25.7 us -> none  [body(): lax.all_to_all(near, 'z_hi', 0, 0, tiled=True).astype(f32)]
    all_gather x1 -> x2, blocking collectives: 22.2 us -> 40.1 us  [the longest x1 26.8 us: body(): near = lax.all_gather(near, 'z_hi')]
    pallas_call x2 -> x3, Pallas kernels: 4.67 us -> 4.8 us  [the longest x1 4.52 us: sums_of(): call(sum_kernel, [VMEM] * 4 + [HBM] * 2, [((ZL, SLOT, LANES), bf16)], [pl...]
  transfers between devices with their start and end apart: 6 -> 6, of which waited for: 3 -> 3; matrix products, arithmetic and copies ran while one was open for 0% -> 1% of each run, Pallas kernels for 10% -> 11%
where the time goes in v4:
time: 147 us
  blocking collectives  58.5 us (40%)
  starting transfers between devices  37.8 us (26%)
  Pallas kernels  33.2 us (23%)
  waiting for transfers between devices  16.2 us (11%)
    all_gather x1, blocking collectives, body(): near = lax.all_gather(near, 'z_hi')  26.8 us
    ppermute x4, starting transfers between devices, swap(): return lax.ppermute(value, axis, [(0, 1), (1, 0)])  25.5 us
    all_to_all x1, blocking collectives, body(): near = lax.all_to_all(sums, 'z_lo', 0, 0, tiled=True)  18.4 us
    all_gather x1, blocking collectives, body(): near = lax.all_gather(hat, 'z_lo')  13.4 us
    pallas_call x4, Pallas kernels, images(): call(image_kernel, [SMEM, VMEM, VMEM] + [HBM] * len(extra), [((CORE * PER...  10.2 us
    all_to_all x1, waiting for transfers between devices, body(): own = lax.all_to_all(messages, ('x_lo', 'x_hi', 'y'), 0, 0, tiled=True)  9.71 us
    all_to_all x1, starting transfers between devices, body(): own = lax.all_to_all(messages, ('x_lo', 'x_hi', 'y'), 0, 0, tiled=True)  7.64 us
    pallas_call x1, Pallas kernels, scores(): call(score_kernel, [SMEM] + [VMEM] * 5, [((ROT, KROWS * LANES), f32), ((C...  7.17 us
  transfers between devices with their start and end apart: 6, of which 3 were waited for; matrix products, arithmetic and copies ran while one was open for 1% of the time, Pallas kernels for 11%

profile of v4, /device:TPU:1, one launch (start us, length us, event | category | flops | bytes accessed | tf_op | source)
XLA Modules:
  0.0 146.8 jit_solution(13568901335104241692)
XLA Ops:
  0.0 2.6 %shard_map.82 = bf16[16,304,128]{2,1,0:T(8,128)(2,1)} custom-call(s32[2]{0:T(128)} %ids.1, bf16[2,64,288]{2,1,0:T(8,128)(2,1)} %x.1, f32[32,64]{1,0:T(8,128)} %ctf.1, bf16[2,288,288]{2,1,0:T(8,128)(2,1)} %constant.29.clone.table), custom_call_target="tpu_custom_call" | custom-call | flops 10000000 | bytes 1000000 | tf_op jit(solution)/shard_map/pallas_call | solution.py:376
  2.6 7.6 %all-to-all-start = ((bf16[16,304,128]{2,1,0:T(8,128)(2,1)}), bf16[16,304,128]{2,1,0:T(8,128)(2,1)}, u32[]{:S(2)}, u32[]{:S(2)}) async-start(bf16[16,304,128]{2,1,0:T(8,128)(2,1)} %shard_map.82), calls=%async_computation | async-start | bytes 2490368 | tf_op jit(solution)/shard_map/all_to_all | solution.py:489
  10.3 5.1 %shard_map.83 = (bf16[144,32,128]{2,1,0:T(8,128)(2,1)}, f32[16,128]{1,0:T(8,128)}) custom-call(s32[1]{0:T(128)} %bitcast.2.start, bf16[50,64,288]{2,1,0:T(8,128)(2,1)} %refs.1, bf16[2,288,288]{2,1,0:T(8,128)(2,1)} %constant.29.clone.table), custom_call_target="tpu_custom_call" | custom-call | flops 1000000000 | bytes 4000000 | tf_op jit(solution)/shard_map/pallas_call | solution.py:389
  15.3 9.7 %all-to-all-done.own = bf16[16,304,128]{2,1,0:T(8,128)(2,1)} async-done(((bf16[16,304,128]{2,1,0:T(8,128)(2,1)}), bf16[16,304,128]{2,1,0:T(8,128)(2,1)}, u32[]{:S(2)}, u32[]{:S(2)}) %all-to-all-start) | async-done | bytes 1245216 | tf_op jit(solution)/shard_map/all_to_all | solution.py:489
  25.1 7.2 %collective-permute-start = (bf16[16,304,128]{2,1,0:T(8,128)(2,1)}, bf16[16,304,128]{2,1,0:T(8,128)(2,1)}, u32[]{:S(2)}, u32[]{:S(2)}) collective-permute-start(bf16[16,304,128]{2,1,0:T(8,128)(2,1)} %all-to-all-done.own), channel_id=1, source_target_pairs={{0,8},{8,0},{1,9},{9,1},{2,10},{10,2},{3,11},{11,3},{4,12},{12,4},... | collective-permute-start | bytes 3735560 | tf_op jit(solution)/shard_map/ppermute | solution.py:372
  32.3 0.7 pad_add_fusion.3.place
  32.9 2.2 %collective-permute-done.other = bf16[16,304,128]{2,1,0:T(8,128)(2,1)} collective-permute-done((bf16[16,304,128]{2,1,0:T(8,128)(2,1)}, bf16[16,304,128]{2,1,0:T(8,128)(2,1)}, u32[]{:S(2)}, u32[]{:S(2)}) %collective-permute-start) | collective-permute-done | bytes 1245216 | tf_op jit(solution)/shard_map/ppermute | solution.py:372
  35.2 7.2 %shard_map.84 = (f32[72,1024]{1,0:T(8,128)}, f32[32,8,128]{2,1,0:T(8,128)}, f32[8,128]{1,0:T(8,128)}, f32[64,128]{1,0:T(8,128)}, bf16[144,64,128]{2,1,0:T(8,128)(2,1)}) custom-call(s32[2]{0:T(128)} %pad_add_fusion.3.place, bf16[16,304,128]{2,1,0:T(8,128)(2,1)} %all-to-all-done.own, bf16[16,304,128]{2,1,0:T(8,128)(2,1)} %collective-permute-done.other, ...), custom_call_target="tpu_custom_call" | custom-call | flops 1000000000 | bytes 8000000 | tf_op jit(solution)/shard_map/pallas_call | solution.py:405
  42.3 4.6 %all-to-all-start.1 = ((f32[32,8,128]{2,1,0:T(8,128)}), f32[32,8,128]{2,1,0:T(8,128)}, u32[]{:S(2)}, u32[]{:S(2)}) async-start(f32[32,8,128]{2,1,0:T(8,128)} %get-tuple-element.24.stats), calls=%async_computation.1 | async-start | bytes 262144 | tf_op jit(solution)/shard_map/all_to_all | solution.py:499
  47.0 3.3 %shard_map.85.far_post = f32[144,16,128]{2,1,0:T(8,128)} custom-call(f32[72,1024]{1,0:T(8,128)} %get-tuple-element.27.expo, bf16[576,72]{1,0:T(8,128)(2,1)} %constant.31.clone.table), custom_call_target="tpu_custom_call" | custom-call | flops 1000000000 | bytes 3000000 | tf_op jit(solution)/shard_map/pallas_call | solution.py:429
  50.3 4.3 %all-to-all-done.1.all_stats = f32[32,8,128]{2,1,0:T(8,128)} async-done(((f32[32,8,128]{2,1,0:T(8,128)}), f32[32,8,128]{2,1,0:T(8,128)}, u32[]{:S(2)}, u32[]{:S(2)}) %all-to-all-start.1) | async-done | bytes 131104 | tf_op jit(solution)/shard_map/all_to_all | solution.py:499
  54.6 4.5 %shard_map.86 = bf16[4,480,128]{2,1,0:T(8,128)(2,1)} custom-call(f32[32,8,128]{2,1,0:T(8,128)} %all-to-all-done.1.all_stats, f32[32,8,128]{2,1,0:T(8,128)} %get-tuple-element.24.stats, f32[8,128]{1,0:T(8,128)} %get-tuple-element.25.by_class, f32[64,128]{1,0:T(8,128)} %get-tuple-element.26.csq, f32[144,16,128]{2,1,0:T(8,128)} %shard_map.85.far_post, ...), custom_call_target="tpu_custom_call" | custom-call | flops 1000000000 | bytes 8000000 | tf_op jit(solution)/shard_map/pallas_call | solution.py:446
  59.1 18.4 %all_to_all.15.pieces = bf16[4,480,128]{2,1,0:T(8,128)(2,1)S(1)} all-to-all(bf16[4,480,128]{2,1,0:T(8,128)(2,1)} %shard_map.86), channel_id=1, replica_groups=mesh['x_lo'=2,'z_hi'=4,'z_lo'=4,'core'=2,'x_hi'=2,'y'=4] {'z_lo'}, dimensions={0} | all-to-all | bytes 983040 | tf_op jit(solution)/shard_map/all_to_all | solution.py:503
  77.5 0.1 shard_map.87
  77.6 26.8 %all-gather = bf16[1920,128]{1,0:T(8,128)(2,1)S(1)} all-gather(bf16[480,128]{1,0:T(8,128)(2,1)S(1)} %shard_map.87), channel_id=2, replica_groups=mesh['x_lo'=2,'z_hi'=4,'z_lo'=4,'core'=2,'x_hi'=2,'y'=4] {'z_hi'}, dimensions={0}, use_global_device_ids=true | all-gather | bytes 614400 | tf_op jit(solution)/shard_map/all_gather | solution.py:505
  104.4 0.2 shard_map.88
  104.6 13.4 %all-gather.1 = bf16[1920,128]{1,0:T(8,128)(2,1)S(1)} all-gather(bf16[480,128]{1,0:T(8,128)(2,1)S(1)} %shard_map.88), channel_id=3, replica_groups=mesh['x_lo'=2,'z_hi'=4,'z_lo'=4,'core'=2,'x_hi'=2,'y'=4] {'z_lo'}, dimensions={0}, use_global_device_ids=true | all-gather | bytes 614400 | tf_op jit(solution)/shard_map/all_gather | solution.py:509
  118.0 2.2 %collective-permute-start.1 = (bf16[4,480,128]{2,1,0:T(8,128)(2,1)S(1)}, bf16[4,480,128]{2,1,0:T(8,128)(2,1)S(1)}, u32[]{:S(2)}, u32[]{:S(2)}) collective-permute-start(bf16[4,480,128]{2,1,0:T(8,128)(2,1)S(1)} %bitcast.8), channel_id=1, source_target_pairs={{0,256},{256,0},{1,257},{257,1},{2,258},{258,2},{3,259},{259,3},{4... | collective-permute-start | bytes 1474568 | tf_op jit(solution)/shard_map/ppermute | solution.py:372
  120.2 10.5 %collective-permute-start.3 = (bf16[4,480,128]{2,1,0:T(8,128)(2,1)S(1)}, bf16[4,480,128]{2,1,0:T(8,128)(2,1)S(1)}, u32[]{:S(2)}, u32[]{:S(2)}) collective-permute-start(bf16[4,480,128]{2,1,0:T(8,128)(2,1)S(1)} %bitcast.9), channel_id=1, source_target_pairs={{0,8},{8,0},{1,9},{9,1},{2,10},{10,2},{3,11},{11,3},{4,12},{12,4},... | collective-permute-start | bytes 1474568 | tf_op jit(solution)/shard_map/ppermute | solution.py:372
  130.7 2.5 %shard_map.89.rest_0_ = bf16[50,64,288]{2,1,0:T(8,128)(2,1)} custom-call(s32[2]{0:T(128)S(1)} %copy-done.1, bf16[4,480,128]{2,1,0:T(8,128)(2,1)S(1)} %bitcast.10, bf16[4,144,288]{2,1,0:T(8,128)(2,1)S(1)} %copy-done), custom_call_target="tpu_custom_call" | custom-call | flops 1000 | bytes 1000 | tf_op jit(solution)/shard_map/pallas_call | solution.py:465
  133.3 5.6 %collective-permute-start.2 = (bf16[4,480,128]{2,1,0:T(8,128)(2,1)S(1)}, bf16[4,480,128]{2,1,0:T(8,128)(2,1)S(1)}, u32[]{:S(2)}, u32[]{:S(2)}) collective-permute-start(bf16[4,480,128]{2,1,0:T(8,128)(2,1)S(1)} %collective-permute-done.1.hats), channel_id=1, source_target_pairs={{0,8},{8,0},{1,9},{9,1},{2,10},{10,2},{3,11},{11,3},{4,12},{12,4},... | collective-permute-start | bytes 1474568 | tf_op jit(solution)/shard_map/ppermute | solution.py:372
  139.1 2.6 %shard_map.90.rest_0_ = bf16[50,64,288]{2,1,0:T(8,128)(2,1)} custom-call(s32[2]{0:T(128)S(1)} %pad_add_fusion.place, bf16[4,480,128]{2,1,0:T(8,128)(2,1)S(1)} %collective-permute-done.1.hats, bf16[4,144,288]{2,1,0:T(8,128)(2,1)S(1)} %copy-done, bf16[50,64,288]{2,1,0:T(8,128)(2,1)} %shard_map.89.rest_0_), custom_call_target="tpu_custom_call", output_to_operand_aliasing={{}: (3, {})} | custom-call | flops 1000 | bytes 1000 | tf_op jit(solution)/shard_map/pallas_call | solution.py:465
  141.6 2.6 %shard_map.91.rest_0_ = bf16[50,64,288]{2,1,0:T(8,128)(2,1)} custom-call(s32[2]{0:T(128)S(1)} %get-tuple-element.32.place, bf16[4,480,128]{2,1,0:T(8,128)(2,1)S(1)} %collective-permute-done.3.hats, bf16[4,144,288]{2,1,0:T(8,128)(2,1)S(1)} %copy-done, bf16[50,64,288]{2,1,0:T(8,128)(2,1)} %shard_map.90.rest_0_), custom_call_target="tpu_custom_call", output_to_operand_aliasing={{}: (3, {})} | custom-call | flops 1000 | bytes 1000 | tf_op jit(solution)/shard_map/pallas_call | solution.py:465
  144.2 2.6 %shard_map.92 = bf16[50,64,288]{2,1,0:T(8,128)(2,1)} custom-call(s32[2]{0:T(128)S(1)} %get-tuple-element.31.place, bf16[4,480,128]{2,1,0:T(8,128)(2,1)S(1)} %collective-permute-done.2.hats, bf16[4,144,288]{2,1,0:T(8,128)(2,1)S(1)} %copy-done, bf16[50,64,288]{2,1,0:T(8,128)(2,1)} %shard_map.91.rest_0_), custom_call_target="tpu_custom_call", output_to_operand_aliasing={{}: (3, {})} | custom-call | flops 1000 | bytes 1000 | tf_op jit(solution)/shard_map/pallas_call | solution.py:465
  (9 shorter events, 0.2 us)
Async XLA Ops:
  2.6 22.5 %all-to-all-start = ((bf16[16,304,128]{2,1,0:T(8,128)(2,1)}), bf16[16,304,128]{2,1,0:T(8,128)(2,1)}, u32[]{:S(2)}, u32[]{:S(2)}) async-start(bf16[16,304,128]{2,1,0:T(8,128)(2,1)} %shard_map.82), calls=%async_computation | async-start | bytes 2490368 | tf_op jit(solution)/shard_map/all_to_all | solution.py:489
  25.1 10.1 %collective-permute-start = (bf16[16,304,128]{2,1,0:T(8,128)(2,1)}, bf16[16,304,128]{2,1,0:T(8,128)(2,1)}, u32[]{:S(2)}, u32[]{:S(2)}) collective-permute-start(bf16[16,304,128]{2,1,0:T(8,128)(2,1)} %all-to-all-done.own), channel_id=1, source_target_pairs={{0,8},{8,0},{1,9},{9,1},{2,10},{10,2},{3,11},{11,3},{4,12},{12,4},... | collective-permute-start | bytes 3735560 | tf_op jit(solution)/shard_map/ppermute | solution.py:372
  42.3 12.3 %all-to-all-start.1 = ((f32[32,8,128]{2,1,0:T(8,128)}), f32[32,8,128]{2,1,0:T(8,128)}, u32[]{:S(2)}, u32[]{:S(2)}) async-start(f32[32,8,128]{2,1,0:T(8,128)} %get-tuple-element.24.stats), calls=%async_computation.1 | async-start | bytes 262144 | tf_op jit(solution)/shard_map/all_to_all | solution.py:499
  59.1 71.6 %copy-start = (bf16[4,144,288]{2,1,0:T(8,128)(2,1)S(1)}, bf16[4,144,288]{2,1,0:T(8,128)(2,1)}, u32[]{:S(2)}) copy-start(bf16[4,144,288]{2,1,0:T(8,128)(2,1)} %constant.32.clone.table) | copy-start | bytes 995332
  59.1 71.6 %copy-start.1 = (s32[2]{0:T(128)S(1)}, s32[2]{0:T(128)}, u32[]{:S(2)}) copy-start(s32[2]{0:T(128)} %pad_add_fusion.3.place) | copy-start | bytes 28
  118.0 15.3 %collective-permute-start.1 = (bf16[4,480,128]{2,1,0:T(8,128)(2,1)S(1)}, bf16[4,480,128]{2,1,0:T(8,128)(2,1)S(1)}, u32[]{:S(2)}, u32[]{:S(2)}) collective-permute-start(bf16[4,480,128]{2,1,0:T(8,128)(2,1)S(1)} %bitcast.8), channel_id=1, source_target_pairs={{0,256},{256,0},{1,257},{257,1},{2,258},{258,2},{3,259},{259,3},{4... | collective-permute-start | bytes 1474568 | tf_op jit(solution)/shard_map/ppermute | solution.py:372
  120.2 21.4 %collective-permute-start.3 = (bf16[4,480,128]{2,1,0:T(8,128)(2,1)S(1)}, bf16[4,480,128]{2,1,0:T(8,128)(2,1)S(1)}, u32[]{:S(2)}, u32[]{:S(2)}) collective-permute-start(bf16[4,480,128]{2,1,0:T(8,128)(2,1)S(1)} %bitcast.9), channel_id=1, source_target_pairs={{0,8},{8,0},{1,9},{9,1},{2,10},{10,2},{3,11},{11,3},{4,12},{12,4},... | collective-permute-start | bytes 1474568 | tf_op jit(solution)/shard_map/ppermute | solution.py:372
  133.3 10.9 %collective-permute-start.2 = (bf16[4,480,128]{2,1,0:T(8,128)(2,1)S(1)}, bf16[4,480,128]{2,1,0:T(8,128)(2,1)S(1)}, u32[]{:S(2)}, u32[]{:S(2)}) collective-permute-start(bf16[4,480,128]{2,1,0:T(8,128)(2,1)S(1)} %collective-permute-done.1.hats), channel_id=1, source_target_pairs={{0,8},{8,0},{1,9},{9,1},{2,10},{10,2},{3,11},{11,3},{4,12},{12,4},... | collective-permute-start | bytes 1474568 | tf_op jit(solution)/shard_map/ppermute | solution.py:372

commit v5 on v4

--- a/solution.py
+++ b/solution.py
@@ -26,6 +26,7 @@
 KPAD = 16
 KROWS = KPAD // 2
 PARTS = 2
+GROUPS = ((0, 5), (5, 9), (9, 13))
 SOURCES = X * SIDE
 COUNT = MINE * CORE * SOURCES
 MSG = MINE * HALF + 16
@@ -252,7 +253,13 @@
     keep.wait()
 
 
-def sum_kernel(all_stats, stats, by_class, csq, far_post, far_ydata, out, rows, slots, post, ydata, sem):
+def sum_kernel(*refs):
+    far_small, (far_post, far_ydata, out, rows, slots, post, ydata) = refs[:4], refs[4:11]
+    small, (sem, small_sem) = refs[11:15], refs[15:]
+    all_stats, stats, by_class, csq = small
+    first_copies = [pltpu.make_async_copy(a, b, small_sem.at[i]) for i, (a, b) in enumerate(zip(far_small, small))]
+    for copy in first_copies:
+        copy.start()
     copies = []
     for part in range(PARTS):
         lines = pl.ds(part * HALF // PARTS, HALF // PARTS)
@@ -260,6 +267,8 @@
         copies.append(pltpu.make_async_copy(far_ydata.at[lines], ydata.at[lines], sem.at[1, part]))
     for copy in copies:
         copy.start()
+    for copy in first_copies:
+        copy.wait()
     tops, totals = all_stats[:, 0, :], all_stats[:, 1, :]
     top = jnp.max(tops, axis=0, keepdims=True)
     total = jnp.sum(totals * jnp.exp(tops - top), axis=0, keepdims=True)
@@ -322,29 +331,38 @@
     out[...] = (total * factor).astype(bf16)
 
 
-def image_kernel(place, hats, table, *rest):
-    out, flat, real, imag, stage, sem = rest[-6:]
-    core, x_lo = place[0], place[1]
-    for part in range(ZL):
-        flat[part * CHUNK : (part + 1) * CHUNK] = hats[part].astype(f32)[:CHUNK]
-    for k in range(KD):
-        rows = flat[k * HALF : (k + 1) * HALF].T.astype(bf16)
-        real[k * CYCLES : (k + 1) * CYCLES] = rows[:CYCLES]
-        imag[k * CYCLES : (k + 1) * CYCLES] = rows[CYCLES:]
-    image = dot(real[...], table[0]) + dot(imag[...], table[2])
-    image = image + (dot(real[...], table[1]) + dot(imag[...], table[3]))
-    stage[...] = image.astype(bf16).reshape(KD, CYCLES, ANG)
-    base = core * PER_CORE + x_lo * (KD - 1)
-    copy = pltpu.make_async_copy(stage.at[pl.ds(x_lo, KD - 1)], out.at[pl.ds(base + x_lo, KD - 1)], sem.at[0])
-    copy.start()
-
-    @pl.when(x_lo == 0)
-    def _():
-        last = pltpu.make_async_copy(stage.at[pl.ds(KD - 1, 1)], out.at[pl.ds(base + KD - 1, 1)], sem.at[1])
-        last.start()
-        last.wait()
-
-    copy.wait()
+def image_kernel(place, table, hats, *refs):
+    out, flat, real, imag, stage, sem = refs[-6:]
+    x_lo = place[0]
+    copies = []
+    for core in range(CORE):
+        i = core
+        base = core * PER_CORE + x_lo * (KD - 1)
+        for part in range(ZL):
+            flat[i, part * CHUNK : (part + 1) * CHUNK] = hats[i, part].astype(f32)[:CHUNK]
+        for step, (first, last) in enumerate(GROUPS):
+            for k in range(first, last):
+                rows = flat[i, k * HALF : (k + 1) * HALF].T.astype(bf16)
+                real[i, k * CYCLES : (k + 1) * CYCLES] = rows[:CYCLES]
+                imag[i, k * CYCLES : (k + 1) * CYCLES] = rows[CYCLES:]
+            lines = slice(first * CYCLES, last * CYCLES)
+            image = dot(real[i, lines], table[0]) + dot(imag[i, lines], table[2])
+            image = image + (dot(real[i, lines], table[1]) + dot(imag[i, lines], table[3]))
+            stage[i, first:last] = image.astype(bf16).reshape(last - first, CYCLES, ANG)
+            begin = max(first, 1)
+            here, there = pl.ds(begin, last - begin), pl.ds(base + begin, last - begin)
+            copy = pltpu.make_async_copy(stage.at[i, here], out.at[there], sem.at[i, step])
+            copy.start()
+            copies.append(copy)
+
+        @pl.when(x_lo == 0)
+        def _():
+            shared = pltpu.make_async_copy(stage.at[i, pl.ds(0, 1)], out.at[pl.ds(base, 1)], sem.at[i, len(GROUPS)])
+            shared.start()
+            shared.wait()
+
+    for copy in copies:
+        copy.wait()
 
 
 VMEM = pl.BlockSpec(memory_space=pltpu.VMEM)
@@ -445,14 +463,19 @@
 def sums_of(all_stats, stats, by_class, csq, post, ydata):
     return call(
         sum_kernel,
-        [VMEM] * 4 + [HBM] * 2,
+        [HBM] * 6,
         [((ZL, SLOT, LANES), bf16)],
         [
             pltpu.VMEM((KPAD * HALF, LANES), f32),
             pltpu.VMEM((ZL * SLOT, LANES), f32),
             pltpu.VMEM((HALF, KPAD, LANES), f32),
             pltpu.VMEM((HALF, COUNT, LANES), bf16),
+            pltpu.VMEM((CORE * SOURCES, 8, LANES), f32),
+            pltpu.VMEM((CORE * SOURCES, 8, LANES), f32),
+            pltpu.VMEM((KROWS, LANES), f32),
+            pltpu.VMEM((COUNT, LANES), f32),
             pltpu.SemaphoreType.DMA((2, PARTS)),
+            pltpu.SemaphoreType.DMA((4,)),
         ],
         10**9,
         8 * 10**6,
@@ -460,24 +483,24 @@
     )(all_stats, stats, by_class, csq, post, ydata)
 
 
-def images(which, hats, inverse, result):
+def images(place, hats, inverse, result):
     extra = [] if result is None else [result]
     return call(
         image_kernel,
         [SMEM, VMEM, VMEM] + [HBM] * len(extra),
         [((CORE * PER_CORE, CYCLES, ANG), bf16)],
         [
-            pltpu.VMEM((KD * HALF, LANES), f32),
-            pltpu.VMEM((KD * CYCLES, HALF), bf16),
-            pltpu.VMEM((KD * CYCLES, HALF), bf16),
-            pltpu.VMEM((KD, CYCLES, ANG), bf16),
-            pltpu.SemaphoreType.DMA((2,)),
+            pltpu.VMEM((CORE, KD * HALF, LANES), f32),
+            pltpu.VMEM((CORE, KD * CYCLES, HALF), bf16),
+            pltpu.VMEM((CORE, KD * CYCLES, HALF), bf16),
+            pltpu.VMEM((CORE, KD, CYCLES, ANG), bf16),
+            pltpu.SemaphoreType.DMA((CORE, len(GROUPS) + 1)),
         ],
         1000,
         1000,
         {3: 0} if extra else None,
         [HBM],
-    )(which, hats, inverse, *extra)
+    )(place.reshape(1), inverse, hats, *extra)
 
 
 def body(particles, group_ids, ctf_table, references):
@@ -508,13 +531,9 @@
     inverse = jnp.asarray(inverse_table())
     near = lax.all_gather(hat, "z_lo")
     far = swap("x_lo", near)
-    near_other = swap("core", near)
-    result = images(jnp.stack([core, x_lo]), near, inverse, None)
+    result = images(x_lo, lax.all_gather(near, "core"), inverse, None)
     far, result = lax.optimization_barrier((far, result))
-    far_other = swap("core", far)
-    result = images(jnp.stack([core, 1 - x_lo]), far, inverse, result)
-    result = images(jnp.stack([1 - core, x_lo]), near_other, inverse, result)
-    return images(jnp.stack([1 - core, 1 - x_lo]), far_other, inverse, result)
+    return images(1 - x_lo, lax.all_gather(far, "core"), inverse, result)
 
 
 def solution(mesh):

time: 147 us -> 142 us (0.966)
  starting transfers between devices: 37.8 us -> 21.6 us
  blocking collectives: 58.5 us -> 73.8 us
  Pallas kernels: 33.2 us -> 29 us
    ppermute x4 -> x2, starting transfers between devices: 25.5 us -> 9.33 us  [swap(): return lax.ppermute(value, axis, [(0, 1), (1, 0)])]
    all_gather x0 -> x2, blocking collectives: none -> 15.3 us  [the longest x1 10.7 us: body(): result = images(x_lo, lax.all_gather(near, 'core'), inverse, None)]
    pallas_call x4 -> x2, Pallas kernels: 10.2 us -> 6.87 us  [images(): call(image_kernel, [SMEM, VMEM, VMEM] + [HBM] * len(extra), [((CORE * PER...]
  transfers between devices with their start and end apart: 6 -> 4, of which waited for: 3 -> 3; matrix products, arithmetic and copies ran while one was open for 1% -> 0% of each run, Pallas kernels for 11% -> 9%
where the time goes in v5:
time: 142 us; the launch traced here: 141 us
  blocking collectives  73.8 us (52%)
  Pallas kernels  29 us (20%)
  starting transfers between devices  21.6 us (15%)
  waiting for transfers between devices  16.3 us (11%)
    all_gather x1, blocking collectives, body(): near = lax.all_gather(near, 'z_hi')  26.4 us
    all_to_all x1, blocking collectives, body(): near = lax.all_to_all(sums, 'z_lo', 0, 0, tiled=True)  18.3 us
    all_gather x1, blocking collectives, body(): near = lax.all_gather(hat, 'z_lo')  13.8 us
    all_gather x1, blocking collectives, body(): result = images(x_lo, lax.all_gather(near, 'core'), inverse, None)  10.7 us
    all_to_all x1, waiting for transfers between devices, body(): own = lax.all_to_all(messages, ('x_lo', 'x_hi', 'y'), 0, 0, tiled=True)  9.72 us
    ppermute x2, starting transfers between devices, swap(): return lax.ppermute(value, axis, [(0, 1), (1, 0)])  9.33 us
    all_to_all x1, starting transfers between devices, body(): own = lax.all_to_all(messages, ('x_lo', 'x_hi', 'y'), 0, 0, tiled=True)  7.64 us
    pallas_call x1, Pallas kernels, scores(): call(score_kernel, [SMEM] + [VMEM] * 5, [((ROT, KROWS * LANES), f32), ((C...  7.14 us
  transfers between devices with their start and end apart: 4, of which 3 were waited for; matrix products, arithmetic and copies ran while one was open for 0% of the time, Pallas kernels for 9%

profile of v5, /device:TPU:1, one launch (start us, length us, event | category | flops | bytes accessed | tf_op | source)
XLA Modules:
  0.0 141.4 jit_solution(4565632618223001468)
XLA Ops:
  0.0 2.6 %shard_map.82 = bf16[16,304,128]{2,1,0:T(8,128)(2,1)} custom-call(s32[2]{0:T(128)} %ids.1, bf16[2,64,288]{2,1,0:T(8,128)(2,1)} %x.1, f32[32,64]{1,0:T(8,128)} %ctf.1, bf16[2,288,288]{2,1,0:T(8,128)(2,1)} %constant.29.clone.table), custom_call_target="tpu_custom_call" | custom-call | flops 10000000 | bytes 1000000 | tf_op jit(solution)/shard_map/pallas_call | solution.py:394
  2.6 7.6 %all-to-all-start = ((bf16[16,304,128]{2,1,0:T(8,128)(2,1)}), bf16[16,304,128]{2,1,0:T(8,128)(2,1)}, u32[]{:S(2)}, u32[]{:S(2)}) async-start(bf16[16,304,128]{2,1,0:T(8,128)(2,1)} %shard_map.82), calls=%async_computation | async-start | bytes 2490368 | tf_op jit(solution)/shard_map/all_to_all | solution.py:512
  10.3 5.1 %shard_map.83 = (bf16[144,32,128]{2,1,0:T(8,128)(2,1)}, f32[16,128]{1,0:T(8,128)}) custom-call(s32[1]{0:T(128)} %bitcast.1.start, bf16[50,64,288]{2,1,0:T(8,128)(2,1)} %refs.1, bf16[2,288,288]{2,1,0:T(8,128)(2,1)} %constant.29.clone.table), custom_call_target="tpu_custom_call" | custom-call | flops 1000000000 | bytes 4000000 | tf_op jit(solution)/shard_map/pallas_call | solution.py:407
  15.3 9.7 %all-to-all-done.own = bf16[16,304,128]{2,1,0:T(8,128)(2,1)} async-done(((bf16[16,304,128]{2,1,0:T(8,128)(2,1)}), bf16[16,304,128]{2,1,0:T(8,128)(2,1)}, u32[]{:S(2)}, u32[]{:S(2)}) %all-to-all-start) | async-done | bytes 1245216 | tf_op jit(solution)/shard_map/all_to_all | solution.py:512
  25.1 7.2 %collective-permute-start = (bf16[16,304,128]{2,1,0:T(8,128)(2,1)}, bf16[16,304,128]{2,1,0:T(8,128)(2,1)}, u32[]{:S(2)}, u32[]{:S(2)}) collective-permute-start(bf16[16,304,128]{2,1,0:T(8,128)(2,1)} %all-to-all-done.own), channel_id=1, source_target_pairs={{0,8},{8,0},{1,9},{9,1},{2,10},{10,2},{3,11},{11,3},{4,12},{12,4},... | collective-permute-start | bytes 3735560 | tf_op jit(solution)/shard_map/ppermute | solution.py:390
  32.3 0.6 pad_add_fusion.place
  32.9 2.3 %collective-permute-done.other = bf16[16,304,128]{2,1,0:T(8,128)(2,1)} collective-permute-done((bf16[16,304,128]{2,1,0:T(8,128)(2,1)}, bf16[16,304,128]{2,1,0:T(8,128)(2,1)}, u32[]{:S(2)}, u32[]{:S(2)}) %collective-permute-start) | collective-permute-done | bytes 1245216 | tf_op jit(solution)/shard_map/ppermute | solution.py:390
  35.2 7.1 %shard_map.84 = (f32[72,1024]{1,0:T(8,128)}, f32[32,8,128]{2,1,0:T(8,128)}, f32[8,128]{1,0:T(8,128)}, f32[64,128]{1,0:T(8,128)}, bf16[144,64,128]{2,1,0:T(8,128)(2,1)}) custom-call(s32[2]{0:T(128)} %pad_add_fusion.place, bf16[16,304,128]{2,1,0:T(8,128)(2,1)} %all-to-all-done.own, bf16[16,304,128]{2,1,0:T(8,128)(2,1)} %collective-permute-done.other, ...), custom_call_target="tpu_custom_call" | custom-call | flops 1000000000 | bytes 8000000 | tf_op jit(solution)/shard_map/pallas_call | solution.py:423
  42.3 4.6 %all-to-all-start.1 = ((f32[32,8,128]{2,1,0:T(8,128)}), f32[32,8,128]{2,1,0:T(8,128)}, u32[]{:S(2)}, u32[]{:S(2)}) async-start(f32[32,8,128]{2,1,0:T(8,128)} %get-tuple-element.24.refs_1_), calls=%async_computation.1 | async-start | bytes 262144 | tf_op jit(solution)/shard_map/all_to_all | solution.py:522
  47.0 3.3 %shard_map.85.refs_4_ = f32[144,16,128]{2,1,0:T(8,128)} custom-call(f32[72,1024]{1,0:T(8,128)} %get-tuple-element.27.expo, bf16[576,72]{1,0:T(8,128)(2,1)} %constant.31.clone.table), custom_call_target="tpu_custom_call" | custom-call | flops 1000000000 | bytes 3000000 | tf_op jit(solution)/shard_map/pallas_call | solution.py:447
  50.3 4.3 %all-to-all-done.1.refs_0_ = f32[32,8,128]{2,1,0:T(8,128)} async-done(((f32[32,8,128]{2,1,0:T(8,128)}), f32[32,8,128]{2,1,0:T(8,128)}, u32[]{:S(2)}, u32[]{:S(2)}) %all-to-all-start.1) | async-done | bytes 131104 | tf_op jit(solution)/shard_map/all_to_all | solution.py:522
  54.6 3.8 %shard_map.86 = bf16[4,480,128]{2,1,0:T(8,128)(2,1)} custom-call(f32[32,8,128]{2,1,0:T(8,128)} %all-to-all-done.1.refs_0_, f32[32,8,128]{2,1,0:T(8,128)} %get-tuple-element.24.refs_1_, f32[8,128]{1,0:T(8,128)} %get-tuple-element.25.refs_2_, f32[64,128]{1,0:T(8,128)} %get-tuple-element.26.refs_3_, f32[144,16,128]{2,1,0:T(8,128)} %shard_map.85.refs_4_, ...), custom_call_target="tpu_custom_call" | custom-call | flops 1000000000 | bytes 8000000 | tf_op jit(solution)/shard_map/pallas_call | solution.py:464
  58.3 18.3 %all_to_all.15.pieces = bf16[4,480,128]{2,1,0:T(8,128)(2,1)S(1)} all-to-all(bf16[4,480,128]{2,1,0:T(8,128)(2,1)} %shard_map.86), channel_id=1, replica_groups=mesh['x_lo'=2,'z_hi'=4,'z_lo'=4,'core'=2,'x_hi'=2,'y'=4] {'z_lo'}, dimensions={0} | all-to-all | bytes 983040 | tf_op jit(solution)/shard_map/all_to_all | solution.py:526
  76.6 0.1 shard_map.87
  76.7 26.4 %all-gather = bf16[1920,128]{1,0:T(8,128)(2,1)S(1)} all-gather(bf16[480,128]{1,0:T(8,128)(2,1)S(1)} %shard_map.87), channel_id=2, replica_groups=mesh['x_lo'=2,'z_hi'=4,'z_lo'=4,'core'=2,'x_hi'=2,'y'=4] {'z_hi'}, dimensions={0}, use_global_device_ids=true | all-gather | bytes 614400 | tf_op jit(solution)/shard_map/all_gather | solution.py:528
  103.1 0.2 shard_map.88
  103.3 13.8 %all-gather.1 = bf16[1920,128]{1,0:T(8,128)(2,1)S(1)} all-gather(bf16[480,128]{1,0:T(8,128)(2,1)S(1)} %shard_map.88), channel_id=3, replica_groups=mesh['x_lo'=2,'z_hi'=4,'z_lo'=4,'core'=2,'x_hi'=2,'y'=4] {'z_lo'}, dimensions={0}, use_global_device_ids=true | all-gather | bytes 614400 | tf_op jit(solution)/shard_map/all_gather | solution.py:532
  117.1 2.1 %collective-permute-start.1 = (bf16[4,480,128]{2,1,0:T(8,128)(2,1)S(1)}, bf16[4,480,128]{2,1,0:T(8,128)(2,1)S(1)}, u32[]{:S(2)}, u32[]{:S(2)}) collective-permute-start(bf16[4,480,128]{2,1,0:T(8,128)(2,1)S(1)} %bitcast.12), channel_id=1, source_target_pairs={{0,256},{256,0},{1,257},{257,1},{2,258},{258,2},{3,259},{259,3},{4... | collective-permute-start | bytes 1474568 | tf_op jit(solution)/shard_map/ppermute | solution.py:390
  119.2 10.7 %all-gather.2 = bf16[8,480,128]{2,1,0:T(8,128)(2,1)S(1)} all-gather(bf16[4,480,128]{2,1,0:T(8,128)(2,1)S(1)} %bitcast.13), channel_id=4, replica_groups=mesh['x_lo'=2,'z_hi'=4,'z_lo'=4,'core'=2,'x_hi'=2,'y'=4] {'core'}, dimensions={0}, use_global_device_ids=true | all-gather | bytes 1474560 | tf_op jit(solution)/shard_map/all_gather | solution.py:534
  130.0 0.0 copy-done
  130.0 3.8 %shard_map.89.refs_0_ = bf16[50,64,288]{2,1,0:T(8,128)(2,1)} custom-call(s32[1]{0:T(128)} %bitcast.4.place, bf16[4,144,288]{2,1,0:T(8,128)(2,1)S(1)} %copy-done, bf16[2,4,480,128]{3,2,1,0:T(8,128)(2,1)S(1)} %bitcast.10), custom_call_target="tpu_custom_call" | custom-call | flops 1000 | bytes 1000 | tf_op jit(solution)/shard_map/pallas_call | solution.py:488
  133.8 0.0 collective-permute-done.1
  133.8 4.6 %all-gather.3 = bf16[8,480,128]{2,1,0:T(8,128)(2,1)S(1)} all-gather(bf16[4,480,128]{2,1,0:T(8,128)(2,1)S(1)} %collective-permute-done.1), channel_id=5, replica_groups=mesh['x_lo'=2,'z_hi'=4,'z_lo'=4,'core'=2,'x_hi'=2,'y'=4] {'core'}, dimensions={0}, use_global_device_ids=true | all-gather | bytes 1474560 | tf_op jit(solution)/shard_map/all_gather | solution.py:536
  138.4 3.1 %shard_map.90 = bf16[50,64,288]{2,1,0:T(8,128)(2,1)} custom-call(s32[1]{0:T(128)} %bitcast.place, bf16[4,144,288]{2,1,0:T(8,128)(2,1)S(1)} %copy-done, bf16[2,4,480,128]{3,2,1,0:T(8,128)(2,1)S(1)} %bitcast.9, bf16[50,64,288]{2,1,0:T(8,128)(2,1)} %shard_map.89.refs_0_), custom_call_target="tpu_custom_call", output_to_operand_aliasing={{}: (3, {})} | custom-call | flops 1000 | bytes 1000 | tf_op jit(solution)/shard_map/pallas_call | solution.py:488
  (1 shorter events, 0.0 us)
Async XLA Ops:
  2.6 22.5 %all-to-all-start = ((bf16[16,304,128]{2,1,0:T(8,128)(2,1)}), bf16[16,304,128]{2,1,0:T(8,128)(2,1)}, u32[]{:S(2)}, u32[]{:S(2)}) async-start(bf16[16,304,128]{2,1,0:T(8,128)(2,1)} %shard_map.82), calls=%async_computation | async-start | bytes 2490368 | tf_op jit(solution)/shard_map/all_to_all | solution.py:512
  25.1 10.1 %collective-permute-start = (bf16[16,304,128]{2,1,0:T(8,128)(2,1)}, bf16[16,304,128]{2,1,0:T(8,128)(2,1)}, u32[]{:S(2)}, u32[]{:S(2)}) collective-permute-start(bf16[16,304,128]{2,1,0:T(8,128)(2,1)} %all-to-all-done.own), channel_id=1, source_target_pairs={{0,8},{8,0},{1,9},{9,1},{2,10},{10,2},{3,11},{11,3},{4,12},{12,4},... | collective-permute-start | bytes 3735560 | tf_op jit(solution)/shard_map/ppermute | solution.py:390
  42.3 12.3 %all-to-all-start.1 = ((f32[32,8,128]{2,1,0:T(8,128)}), f32[32,8,128]{2,1,0:T(8,128)}, u32[]{:S(2)}, u32[]{:S(2)}) async-start(f32[32,8,128]{2,1,0:T(8,128)} %get-tuple-element.24.refs_1_), calls=%async_computation.1 | async-start | bytes 262144 | tf_op jit(solution)/shard_map/all_to_all | solution.py:522
  103.1 26.9 %copy-start = (bf16[4,144,288]{2,1,0:T(8,128)(2,1)S(1)}, bf16[4,144,288]{2,1,0:T(8,128)(2,1)}, u32[]{:S(2)}) copy-start(bf16[4,144,288]{2,1,0:T(8,128)(2,1)} %constant.32.clone.table) | copy-start | bytes 995332
  117.1 16.7 %collective-permute-start.1 = (bf16[4,480,128]{2,1,0:T(8,128)(2,1)S(1)}, bf16[4,480,128]{2,1,0:T(8,128)(2,1)S(1)}, u32[]{:S(2)}, u32[]{:S(2)}) collective-permute-start(bf16[4,480,128]{2,1,0:T(8,128)(2,1)S(1)} %bitcast.12), channel_id=1, source_target_pairs={{0,256},{256,0},{1,257},{257,1},{2,258},{258,2},{3,259},{259,3},{4... | collective-permute-start | bytes 1474568 | tf_op jit(solution)/shard_map/ppermute | solution.py:390

commit v6 on v5

--- a/solution.py
+++ b/solution.py
@@ -48,18 +48,19 @@
     return 2.0 * math.pi * index / ANG
 
 
-def split(table):
-    table = table.astype(np.float32)
-    high = table.astype(ml_dtypes.bfloat16)
-    low = (table - high.astype(np.float32)).astype(ml_dtypes.bfloat16)
-    return np.stack([high, low])
+def split(table, count):
+    rest, pieces = table.astype(np.float32), []
+    for _ in range(count):
+        pieces.append(rest.astype(ml_dtypes.bfloat16))
+        rest = rest - pieces[-1].astype(np.float32)
+    return np.stack(pieces)
 
 
 def forward_table():
     angle = angles(HALF + 1, ANG, 1)
     real = np.cos(angle[:HALF])
     imag = np.concatenate([np.cos(angle[HALF:]), np.sin(angle[1:HALF])])
-    return split(np.concatenate([real, imag]))
+    return split(np.concatenate([real, imag]), 3)
 
 
 def weights_of_rows():
@@ -69,12 +70,12 @@
 def search_table():
     angle = angles(HALF, ROT, ANG // ROT)
     scale = weights_of_rows()
-    return split(np.concatenate([np.cos(angle) * scale, -np.sin(angle) * scale]).T)
+    return split(np.concatenate([np.cos(angle) * scale, -np.sin(angle) * scale]).T, 3)
 
 
 def post_table():
     angle = angles(HALF, ROT, ANG // ROT)
-    return split(np.concatenate([np.cos(angle), np.sin(angle)]))
+    return split(np.concatenate([np.cos(angle), np.sin(angle)]), 3)
 
 
 def inverse_table():
@@ -82,7 +83,7 @@
     scale = weights_of_rows()
     real = np.cos(angle[:HALF]) * scale
     imag = np.concatenate([np.cos(angle[HALF:]), np.sin(angle[1:HALF])]) * scale
-    return np.concatenate([split(real), split(imag)])
+    return np.concatenate([split(real, 2), split(imag, 2)])
 
 
 def dot(a, b, dims=NN):
@@ -94,11 +95,24 @@
     return high, (values - high.astype(f32)).astype(bf16)
 
 
+def thirds(values):
+    high = values.astype(bf16)
+    rest = values - high.astype(f32)
+    mid = rest.astype(bf16)
+    return high, mid, (rest - mid.astype(f32)).astype(bf16)
+
+
 def dot3(table, values):
-    high, low = halves(values)
-    rows = table.shape[0] // 2
-    both = dot(table[...], high)
-    return both[:rows] + (both[rows:] + dot(table[:rows], low))
+    high, mid, low = thirds(values)
+    rows = table.shape[0] // 3
+    first = dot(table[...], high)
+    second = dot(table[: 2 * rows], mid)
+    small = (first[2 * rows :] + second[rows:]) + dot(table[:rows], low)
+    return first[:rows] + (first[rows : 2 * rows] + second[:rows] + small)
+
+
+def transform(table, images):
+    return dot(table[0], images, NT) + (dot(table[1], images, NT) + dot(table[2], images, NT))
 
 
 def turn(values):
@@ -118,16 +132,13 @@
 def share_kernel(ids, x, ctf, table, outs, out, sem):
     images = x[...].reshape(MINE * CYCLES, ANG)
     factor = jnp.concatenate([ctf[pl.ds(ids[0], 1), :], ctf[pl.ds(ids[1], 1), :]], axis=1)
-    spec = (dot(table[0], images, NT) + dot(table[1], images, NT)) * factor
+    spec = transform(table, images) * factor
     first, second = fold(spec)
     out[0:HALF] = first.astype(bf16)
     out[HALF : 2 * HALF] = second.astype(bf16)
-    high, rest = halves(factor)
-    rest = factor - high.astype(f32)
-    mid = rest.astype(bf16)
-    low = rest - mid.astype(f32)
+    high, mid, low = thirds(factor)
     row = lax.broadcasted_iota(jnp.int32, (16, LANES), 0)
-    tags = jnp.where(row == 0, high.astype(f32), jnp.where(row == 1, mid.astype(f32), jnp.where(row == 2, low, 0.0)))
+    tags = jnp.where(row == 0, high.astype(f32), jnp.where(row == 1, mid.astype(f32), jnp.where(row == 2, low.astype(f32), 0.0)))
     out[2 * HALF : MSG] = tags.astype(bf16)
     copies = [pltpu.make_async_copy(out, outs.at[s], sem.at[s]) for s in range(SOURCES)]
     for copy in copies:
@@ -144,7 +155,7 @@
     copy.wait()
     for step in range(KPAD // 4):
         block = images[4 * step : 4 * step + 4].reshape(4 * CYCLES, ANG)
-        spec = dot(table[0], block, NT) + dot(table[1], block, NT)
+        spec = transform(table, block)
         wide = block.astype(f32)
         high, low = halves(wide * wide)
         energy = dot(ones, high, NT) + dot(ones, low, NT)
@@ -161,9 +172,7 @@
 
     def step(j, carry):
         plain = rows[pl.ds(j, KPAD, stride=HALF), :]
-        other = turn(plain)
-        other = jnp.where(left(other.shape), other, -other)
-        out[j] = jnp.concatenate([plain, other], axis=0).astype(bf16)
+        out[j] = plain.astype(bf16)
         return carry
 
     lax.fori_loop(0, HALF, step, 0, unroll=36)
@@ -179,7 +188,7 @@
         wide[pl.ds(theirs, MSG), :] = other[s].astype(f32)
         return carry
 
-    lax.fori_loop(0, SOURCES, widen, 0)
+    lax.fori_loop(0, SOURCES, widen, 0, unroll=2)
     many = CORE * SOURCES
     factor = wide[pl.ds(2 * HALF, many, stride=MSG), :] + wide[pl.ds(2 * HALF + 1, many, stride=MSG), :]
     factor = factor + wide[pl.ds(2 * HALF + 2, many, stride=MSG), :]
@@ -201,7 +210,10 @@
         rows = jnp.concatenate([wide[pl.ds(j, many, stride=MSG), :], wide[pl.ds(HALF + j, many, stride=MSG), :]], axis=0)
         rows = rows.astype(bf16)
         ydata[j] = rows
-        both = dot(rmat[j], rows, NT)
+        plain = rmat[j].astype(f32)
+        cross = turn(plain)
+        cross = jnp.where(left(cross.shape), cross, -cross)
+        both = dot(jnp.concatenate([plain, cross], axis=0).astype(bf16), rows, NT)
         straight = jnp.concatenate([both[:KROWS], both[KROWS : 2 * KROWS]], axis=1)
         crossed = jnp.concatenate([both[2 * KROWS : 3 * KROWS], both[3 * KROWS :]], axis=1)
         pairs[pl.ds(j, KROWS, stride=ANG), :] = straight
@@ -213,8 +225,13 @@
     keep.start()
     top = jnp.full((1, LANES), -3.0e38, f32)
     lane_side = left((ROT, LANES))
+    crosses = []
+    for kk in range(0, KROWS, 2):
+        two = [pairs[k * ANG : (k + 1) * ANG] for k in (kk, kk + 1)]
+        wide_cross = dot3(table, jnp.concatenate(two, axis=1))
+        crosses += [wide_cross[:, :LANES], wide_cross[:, LANES:]]
     for kk in range(KROWS):
-        cross = dot3(table, pairs[kk * ANG : (kk + 1) * ANG])
+        cross = crosses[kk]
         score = SCORE_SCALE * (cross - 0.5 * energy[kk : kk + 1])
         if kk + KROWS >= KD:
             score = jnp.where(lane_side, score, -3.0e38)
@@ -238,8 +255,10 @@
 
 
 def post_kernel(expo, table, far, rows, out, sem):
-    for kk in range(KROWS):
-        rows[kk * ANG : (kk + 1) * ANG] = dot3(table, expo[:, kk * LANES : (kk + 1) * LANES])
+    for kk in range(0, KROWS, 2):
+        both = dot3(table, expo[:, kk * LANES : (kk + 2) * LANES])
+        rows[kk * ANG : (kk + 1) * ANG] = both[:, :LANES]
+        rows[(kk + 1) * ANG : (kk + 2) * ANG] = both[:, LANES:]
 
     def step(j, carry):
         real = rows[pl.ds(j, KROWS, stride=ANG), :]
@@ -407,10 +426,10 @@
     return call(
         class_kernel,
         [SMEM, HBM, VMEM],
-        [((HALF, 2 * KPAD, LANES), bf16), ((KPAD, LANES), f32)],
+        [((HALF, KPAD, LANES), bf16), ((KPAD, LANES), f32)],
         [
             pltpu.VMEM((KPAD, CYCLES, ANG), bf16),
-            pltpu.VMEM((KPAD * HALF, LANES), f32),
+            pltpu.VMEM(((KPAD + 1) * HALF, LANES), f32),
             pltpu.SemaphoreType.DMA,
         ],
         10**9,
@@ -431,8 +450,8 @@
             ((HALF, COUNT, LANES), bf16),
         ],
         [
-            pltpu.VMEM((CORE * SOURCES * MSG, LANES), f32),
-            pltpu.VMEM((KROWS * ANG, LANES), f32),
+            pltpu.VMEM(((CORE * SOURCES + 1) * MSG, LANES), f32),
+            pltpu.VMEM(((KROWS + 1) * ANG, LANES), f32),
             pltpu.VMEM((HALF, COUNT, LANES), bf16),
             pltpu.SemaphoreType.DMA,
         ],
@@ -449,7 +468,7 @@
         [VMEM, VMEM],
         [((HALF, KPAD, LANES), f32)],
         [
-            pltpu.VMEM((KROWS * ANG, LANES), f32),
+            pltpu.VMEM(((KROWS + 1) * ANG, LANES), f32),
             pltpu.VMEM((HALF, KPAD, LANES), f32),
             pltpu.SemaphoreType.DMA,
         ],
@@ -466,7 +485,7 @@
         [HBM] * 6,
         [((ZL, SLOT, LANES), bf16)],
         [
-            pltpu.VMEM((KPAD * HALF, LANES), f32),
+            pltpu.VMEM(((KPAD + 1) * HALF, LANES), f32),
             pltpu.VMEM((ZL * SLOT, LANES), f32),
             pltpu.VMEM((HALF, KPAD, LANES), f32),
             pltpu.VMEM((HALF, COUNT, LANES), bf16),
@@ -517,10 +536,10 @@
     other = swap("core", own)
 
     expo, stats, by_class, csq, ydata = scores(
-        place, own, other, rmat, power, jnp.asarray(search_table().reshape(2 * ROT, ANG))
+        place, own, other, rmat, power, jnp.asarray(search_table().reshape(3 * ROT, ANG))
     )
     all_stats = lax.all_to_all(stats, ("core", "x_lo", "x_hi", "y"), 0, 0, tiled=True)
-    post = posts(expo, jnp.asarray(post_table().reshape(2 * ANG, ROT)))
+    post = posts(expo, jnp.asarray(post_table().reshape(3 * ANG, ROT)))
     sums = sums_of(all_stats, stats, by_class, csq, post, ydata)
 
     near = lax.all_to_all(sums, "z_lo", 0, 0, tiled=True)

time: 142 us -> 142 us (level)
  no operation moved by 1% of the time
where the time goes in v6:
time: 142 us
  blocking collectives  73.9 us (52%)
  Pallas kernels  29.4 us (21%)
  starting transfers between devices  21.6 us (15%)
  waiting for transfers between devices  15.8 us (11%)
    all_gather x1, blocking collectives, body(): near = lax.all_gather(near, 'z_hi')  26.5 us
    all_to_all x1, blocking collectives, body(): near = lax.all_to_all(sums, 'z_lo', 0, 0, tiled=True)  18.4 us
    all_gather x1, blocking collectives, body(): near = lax.all_gather(hat, 'z_lo')  13.8 us
    all_gather x1, blocking collectives, body(): result = images(x_lo, lax.all_gather(near, 'core'), inverse, None)  10.7 us
    all_to_all x1, waiting for transfers between devices, body(): own = lax.all_to_all(messages, ('x_lo', 'x_hi', 'y'), 0, 0, tiled=True)  9.81 us
    ppermute x2, starting transfers between devices, swap(): return lax.ppermute(value, axis, [(0, 1), (1, 0)])  9.33 us
    all_to_all x1, starting transfers between devices, body(): own = lax.all_to_all(messages, ('x_lo', 'x_hi', 'y'), 0, 0, tiled=True)  7.64 us
    pallas_call x1, Pallas kernels, scores(): call(score_kernel, [SMEM] + [VMEM] * 5, [((ROT, KROWS * LANES), f32), ((C...  6.93 us
  transfers between devices with their start and end apart: 4, of which 3 were waited for; matrix products, arithmetic and copies ran while one was open for 0% of the time, Pallas kernels for 9%

profile of v6, /device:TPU:1, one launch (start us, length us, event | category | flops | bytes accessed | tf_op | source)
XLA Modules:
  0.0 141.5 jit_solution(2959280605774177786)
XLA Ops:
  0.0 2.7 %shard_map.82 = bf16[16,304,128]{2,1,0:T(8,128)(2,1)} custom-call(s32[2]{0:T(128)} %ids.1, bf16[2,64,288]{2,1,0:T(8,128)(2,1)} %x.1, f32[32,64]{1,0:T(8,128)} %ctf.1, bf16[3,288,288]{2,1,0:T(8,128)(2,1)} %constant.29.clone.table), custom_call_target="tpu_custom_call" | custom-call | flops 10000000 | bytes 1000000 | tf_op jit(solution)/shard_map/pallas_call | solution.py:413
  2.8 7.6 %all-to-all-start = ((bf16[16,304,128]{2,1,0:T(8,128)(2,1)}), bf16[16,304,128]{2,1,0:T(8,128)(2,1)}, u32[]{:S(2)}, u32[]{:S(2)}) async-start(bf16[16,304,128]{2,1,0:T(8,128)(2,1)} %shard_map.82), calls=%async_computation | async-start | bytes 2490368 | tf_op jit(solution)/shard_map/all_to_all | solution.py:531
  10.4 5.0 %shard_map.83 = (bf16[144,16,128]{2,1,0:T(8,128)(2,1)}, f32[16,128]{1,0:T(8,128)}) custom-call(s32[1]{0:T(128)} %bitcast.1.start, bf16[50,64,288]{2,1,0:T(8,128)(2,1)} %refs.1, bf16[3,288,288]{2,1,0:T(8,128)(2,1)} %constant.29.clone.table), custom_call_target="tpu_custom_call" | custom-call | flops 1000000000 | bytes 4000000 | tf_op jit(solution)/shard_map/pallas_call | solution.py:426
  15.4 9.8 %all-to-all-done.own = bf16[16,304,128]{2,1,0:T(8,128)(2,1)} async-done(((bf16[16,304,128]{2,1,0:T(8,128)(2,1)}), bf16[16,304,128]{2,1,0:T(8,128)(2,1)}, u32[]{:S(2)}, u32[]{:S(2)}) %all-to-all-start) | async-done | bytes 1245216 | tf_op jit(solution)/shard_map/all_to_all | solution.py:531
  25.2 7.2 %collective-permute-start = (bf16[16,304,128]{2,1,0:T(8,128)(2,1)}, bf16[16,304,128]{2,1,0:T(8,128)(2,1)}, u32[]{:S(2)}, u32[]{:S(2)}) collective-permute-start(bf16[16,304,128]{2,1,0:T(8,128)(2,1)} %all-to-all-done.own), channel_id=1, source_target_pairs={{0,8},{8,0},{1,9},{9,1},{2,10},{10,2},{3,11},{11,3},{4,12},{12,4},... | collective-permute-start | bytes 3735560 | tf_op jit(solution)/shard_map/ppermute | solution.py:409
  32.4 0.7 pad_add_fusion.place
  33.1 2.2 %collective-permute-done.other = bf16[16,304,128]{2,1,0:T(8,128)(2,1)} collective-permute-done((bf16[16,304,128]{2,1,0:T(8,128)(2,1)}, bf16[16,304,128]{2,1,0:T(8,128)(2,1)}, u32[]{:S(2)}, u32[]{:S(2)}) %collective-permute-start) | collective-permute-done | bytes 1245216 | tf_op jit(solution)/shard_map/ppermute | solution.py:409
  35.3 6.9 %shard_map.84 = (f32[72,1024]{1,0:T(8,128)}, f32[32,8,128]{2,1,0:T(8,128)}, f32[8,128]{1,0:T(8,128)}, f32[64,128]{1,0:T(8,128)}, bf16[144,64,128]{2,1,0:T(8,128)(2,1)}) custom-call(s32[2]{0:T(128)} %pad_add_fusion.place, bf16[16,304,128]{2,1,0:T(8,128)(2,1)} %all-to-all-done.own, bf16[16,304,128]{2,1,0:T(8,128)(2,1)} %collective-permute-done.other, ...), custom_call_target="tpu_custom_call" | custom-call | flops 1000000000 | bytes 8000000 | tf_op jit(solution)/shard_map/pallas_call | solution.py:442
  42.2 4.6 %all-to-all-start.1 = ((f32[32,8,128]{2,1,0:T(8,128)}), f32[32,8,128]{2,1,0:T(8,128)}, u32[]{:S(2)}, u32[]{:S(2)}) async-start(f32[32,8,128]{2,1,0:T(8,128)} %get-tuple-element.24.refs_1_), calls=%async_computation.1 | async-start | bytes 262144 | tf_op jit(solution)/shard_map/all_to_all | solution.py:541
  46.9 3.8 %shard_map.85.refs_4_ = f32[144,16,128]{2,1,0:T(8,128)} custom-call(f32[72,1024]{1,0:T(8,128)} %get-tuple-element.27.expo, bf16[864,72]{1,0:T(8,128)(2,1)} %constant.31.clone.table), custom_call_target="tpu_custom_call" | custom-call | flops 1000000000 | bytes 3000000 | tf_op jit(solution)/shard_map/pallas_call | solution.py:466
  50.7 3.8 %all-to-all-done.1.refs_0_ = f32[32,8,128]{2,1,0:T(8,128)} async-done(((f32[32,8,128]{2,1,0:T(8,128)}), f32[32,8,128]{2,1,0:T(8,128)}, u32[]{:S(2)}, u32[]{:S(2)}) %all-to-all-start.1) | async-done | bytes 131104 | tf_op jit(solution)/shard_map/all_to_all | solution.py:541
  54.5 3.8 %shard_map.86 = bf16[4,480,128]{2,1,0:T(8,128)(2,1)} custom-call(f32[32,8,128]{2,1,0:T(8,128)} %all-to-all-done.1.refs_0_, f32[32,8,128]{2,1,0:T(8,128)} %get-tuple-element.24.refs_1_, f32[8,128]{1,0:T(8,128)} %get-tuple-element.25.refs_2_, f32[64,128]{1,0:T(8,128)} %get-tuple-element.26.refs_3_, f32[144,16,128]{2,1,0:T(8,128)} %shard_map.85.refs_4_, ...), custom_call_target="tpu_custom_call" | custom-call | flops 1000000000 | bytes 8000000 | tf_op jit(solution)/shard_map/pallas_call | solution.py:483
  58.3 0.0 copy-start
  58.3 18.4 %all_to_all.15.pieces = bf16[4,480,128]{2,1,0:T(8,128)(2,1)S(1)} all-to-all(bf16[4,480,128]{2,1,0:T(8,128)(2,1)} %shard_map.86), channel_id=1, replica_groups=mesh['x_lo'=2,'z_hi'=4,'z_lo'=4,'core'=2,'x_hi'=2,'y'=4] {'z_lo'}, dimensions={0} | all-to-all | bytes 983040 | tf_op jit(solution)/shard_map/all_to_all | solution.py:545
  76.7 0.1 shard_map.87
  76.8 26.5 %all-gather = bf16[1920,128]{1,0:T(8,128)(2,1)S(1)} all-gather(bf16[480,128]{1,0:T(8,128)(2,1)S(1)} %shard_map.87), channel_id=2, replica_groups=mesh['x_lo'=2,'z_hi'=4,'z_lo'=4,'core'=2,'x_hi'=2,'y'=4] {'z_hi'}, dimensions={0}, use_global_device_ids=true | all-gather | bytes 614400 | tf_op jit(solution)/shard_map/all_gather | solution.py:547
  103.2 0.2 shard_map.88
  103.4 13.8 %all-gather.1 = bf16[1920,128]{1,0:T(8,128)(2,1)S(1)} all-gather(bf16[480,128]{1,0:T(8,128)(2,1)S(1)} %shard_map.88), channel_id=3, replica_groups=mesh['x_lo'=2,'z_hi'=4,'z_lo'=4,'core'=2,'x_hi'=2,'y'=4] {'z_lo'}, dimensions={0}, use_global_device_ids=true | all-gather | bytes 614400 | tf_op jit(solution)/shard_map/all_gather | solution.py:551
  117.2 2.1 %collective-permute-start.1 = (bf16[4,480,128]{2,1,0:T(8,128)(2,1)S(1)}, bf16[4,480,128]{2,1,0:T(8,128)(2,1)S(1)}, u32[]{:S(2)}, u32[]{:S(2)}) collective-permute-start(bf16[4,480,128]{2,1,0:T(8,128)(2,1)S(1)} %bitcast.12), channel_id=1, source_target_pairs={{0,256},{256,0},{1,257},{257,1},{2,258},{258,2},{3,259},{259,3},{4... | collective-permute-start | bytes 1474568 | tf_op jit(solution)/shard_map/ppermute | solution.py:409
  119.3 10.7 %all-gather.2 = bf16[8,480,128]{2,1,0:T(8,128)(2,1)S(1)} all-gather(bf16[4,480,128]{2,1,0:T(8,128)(2,1)S(1)} %bitcast.13), channel_id=4, replica_groups=mesh['x_lo'=2,'z_hi'=4,'z_lo'=4,'core'=2,'x_hi'=2,'y'=4] {'core'}, dimensions={0}, use_global_device_ids=true | all-gather | bytes 1474560 | tf_op jit(solution)/shard_map/all_gather | solution.py:553
  130.1 3.8 %shard_map.89.refs_0_ = bf16[50,64,288]{2,1,0:T(8,128)(2,1)} custom-call(s32[1]{0:T(128)} %bitcast.4.place, bf16[4,144,288]{2,1,0:T(8,128)(2,1)S(1)} %copy-done, bf16[2,4,480,128]{3,2,1,0:T(8,128)(2,1)S(1)} %bitcast.10), custom_call_target="tpu_custom_call" | custom-call | flops 1000 | bytes 1000 | tf_op jit(solution)/shard_map/pallas_call | solution.py:507
  133.9 0.0 collective-permute-done.1
  133.9 4.6 %all-gather.3 = bf16[8,480,128]{2,1,0:T(8,128)(2,1)S(1)} all-gather(bf16[4,480,128]{2,1,0:T(8,128)(2,1)S(1)} %collective-permute-done.1), channel_id=5, replica_groups=mesh['x_lo'=2,'z_hi'=4,'z_lo'=4,'core'=2,'x_hi'=2,'y'=4] {'core'}, dimensions={0}, use_global_device_ids=true | all-gather | bytes 1474560 | tf_op jit(solution)/shard_map/all_gather | solution.py:555
  138.4 3.1 %shard_map.90 = bf16[50,64,288]{2,1,0:T(8,128)(2,1)} custom-call(s32[1]{0:T(128)} %bitcast.place, bf16[4,144,288]{2,1,0:T(8,128)(2,1)S(1)} %copy-done, bf16[2,4,480,128]{3,2,1,0:T(8,128)(2,1)S(1)} %bitcast.9, bf16[50,64,288]{2,1,0:T(8,128)(2,1)} %shard_map.89.refs_0_), custom_call_target="tpu_custom_call", output_to_operand_aliasing={{}: (3, {})} | custom-call | flops 1000 | bytes 1000 | tf_op jit(solution)/shard_map/pallas_call | solution.py:507
  (1 shorter events, 0.0 us)
Async XLA Ops:
  2.8 22.4 %all-to-all-start = ((bf16[16,304,128]{2,1,0:T(8,128)(2,1)}), bf16[16,304,128]{2,1,0:T(8,128)(2,1)}, u32[]{:S(2)}, u32[]{:S(2)}) async-start(bf16[16,304,128]{2,1,0:T(8,128)(2,1)} %shard_map.82), calls=%async_computation | async-start | bytes 2490368 | tf_op jit(solution)/shard_map/all_to_all | solution.py:531
  25.2 10.1 %collective-permute-start = (bf16[16,304,128]{2,1,0:T(8,128)(2,1)}, bf16[16,304,128]{2,1,0:T(8,128)(2,1)}, u32[]{:S(2)}, u32[]{:S(2)}) collective-permute-start(bf16[16,304,128]{2,1,0:T(8,128)(2,1)} %all-to-all-done.own), channel_id=1, source_target_pairs={{0,8},{8,0},{1,9},{9,1},{2,10},{10,2},{3,11},{11,3},{4,12},{12,4},... | collective-permute-start | bytes 3735560 | tf_op jit(solution)/shard_map/ppermute | solution.py:409
  42.2 12.3 %all-to-all-start.1 = ((f32[32,8,128]{2,1,0:T(8,128)}), f32[32,8,128]{2,1,0:T(8,128)}, u32[]{:S(2)}, u32[]{:S(2)}) async-start(f32[32,8,128]{2,1,0:T(8,128)} %get-tuple-element.24.refs_1_), calls=%async_computation.1 | async-start | bytes 262144 | tf_op jit(solution)/shard_map/all_to_all | solution.py:541
  58.3 71.8 %copy-start = (bf16[4,144,288]{2,1,0:T(8,128)(2,1)S(1)}, bf16[4,144,288]{2,1,0:T(8,128)(2,1)}, u32[]{:S(2)}) copy-start(bf16[4,144,288]{2,1,0:T(8,128)(2,1)} %constant.32.clone.table) | copy-start | bytes 995332
  117.2 16.7 %collective-permute-start.1 = (bf16[4,480,128]{2,1,0:T(8,128)(2,1)S(1)}, bf16[4,480,128]{2,1,0:T(8,128)(2,1)S(1)}, u32[]{:S(2)}, u32[]{:S(2)}) collective-permute-start(bf16[4,480,128]{2,1,0:T(8,128)(2,1)S(1)} %bitcast.12), channel_id=1, source_target_pairs={{0,256},{256,0},{1,257},{257,1},{2,258},{258,2},{3,259},{259,3},{4... | collective-permute-start | bytes 1474568 | tf_op jit(solution)/shard_map/ppermute | solution.py:409

commit v7 on v6

--- a/solution.py
+++ b/solution.py
@@ -353,7 +353,7 @@
 def image_kernel(place, table, hats, *refs):
     out, flat, real, imag, stage, sem = refs[-6:]
     x_lo = place[0]
-    copies = []
+    copies, shares = [], []
     for core in range(CORE):
         i = core
         base = core * PER_CORE + x_lo * (KD - 1)
@@ -374,14 +374,14 @@
             copy.start()
             copies.append(copy)
 
-        @pl.when(x_lo == 0)
-        def _():
-            shared = pltpu.make_async_copy(stage.at[i, pl.ds(0, 1)], out.at[pl.ds(base, 1)], sem.at[i, len(GROUPS)])
-            shared.start()
-            shared.wait()
+        shared = pltpu.make_async_copy(stage.at[i, pl.ds(0, 1)], out.at[pl.ds(base, 1)], sem.at[i, len(GROUPS)])
+        pl.when(x_lo == 0)(shared.start)
+        shares.append(shared)
 
     for copy in copies:
         copy.wait()
+    for shared in shares:
+        pl.when(x_lo == 0)(shared.wait)
 
 
 VMEM = pl.BlockSpec(memory_space=pltpu.VMEM)

time: 142 us -> 142 us (level)
  transfers between devices with their start and end apart: 4 -> 4, of which waited for: 3 -> 3; matrix products, arithmetic and copies ran while one was open for 0% -> 0% of each run, Pallas kernels for 9% -> 8%
where the time goes in v7:
time: 142 us; the launch traced here: 141 us
  blocking collectives  74.9 us (53%)
  Pallas kernels  28.2 us (20%)
  starting transfers between devices  21.6 us (15%)
  waiting for transfers between devices  15.8 us (11%)
    all_gather x1, blocking collectives, body(): near = lax.all_gather(near, 'z_hi')  26.5 us
    all_to_all x1, blocking collectives, body(): near = lax.all_to_all(sums, 'z_lo', 0, 0, tiled=True)  18.4 us
    all_gather x1, blocking collectives, body(): near = lax.all_gather(hat, 'z_lo')  13.8 us
    all_gather x1, blocking collectives, body(): result = images(x_lo, lax.all_gather(near, 'core'), inverse, None)  10.7 us
    all_to_all x1, waiting for transfers between devices, body(): own = lax.all_to_all(messages, ('x_lo', 'x_hi', 'y'), 0, 0, tiled=True)  9.81 us
    ppermute x2, starting transfers between devices, swap(): return lax.ppermute(value, axis, [(0, 1), (1, 0)])  9.33 us
    all_to_all x1, starting transfers between devices, body(): own = lax.all_to_all(messages, ('x_lo', 'x_hi', 'y'), 0, 0, tiled=True)  7.64 us
    pallas_call x1, Pallas kernels, scores(): call(score_kernel, [SMEM] + [VMEM] * 5, [((ROT, KROWS * LANES), f32), ((C...  6.93 us
  transfers between devices with their start and end apart: 4, of which 3 were waited for; matrix products, arithmetic and copies ran while one was open for 0% of the time, Pallas kernels for 8%

profile of v7, /device:TPU:1, one launch (start us, length us, event | category | flops | bytes accessed | tf_op | source)
XLA Modules:
  0.0 141.3 jit_solution(2523061173654957147)
XLA Ops:
  0.0 2.7 %shard_map.82 = bf16[16,304,128]{2,1,0:T(8,128)(2,1)} custom-call(s32[2]{0:T(128)} %ids.1, bf16[2,64,288]{2,1,0:T(8,128)(2,1)} %x.1, f32[32,64]{1,0:T(8,128)} %ctf.1, bf16[3,288,288]{2,1,0:T(8,128)(2,1)} %constant.29.clone.table), custom_call_target="tpu_custom_call" | custom-call | flops 10000000 | bytes 1000000 | tf_op jit(solution)/shard_map/pallas_call | solution.py:413
  2.8 7.6 %all-to-all-start = ((bf16[16,304,128]{2,1,0:T(8,128)(2,1)}), bf16[16,304,128]{2,1,0:T(8,128)(2,1)}, u32[]{:S(2)}, u32[]{:S(2)}) async-start(bf16[16,304,128]{2,1,0:T(8,128)(2,1)} %shard_map.82), calls=%async_computation | async-start | bytes 2490368 | tf_op jit(solution)/shard_map/all_to_all | solution.py:531
  10.4 5.0 %shard_map.83 = (bf16[144,16,128]{2,1,0:T(8,128)(2,1)}, f32[16,128]{1,0:T(8,128)}) custom-call(s32[1]{0:T(128)} %bitcast.1.start, bf16[50,64,288]{2,1,0:T(8,128)(2,1)} %refs.1, bf16[3,288,288]{2,1,0:T(8,128)(2,1)} %constant.29.clone.table), custom_call_target="tpu_custom_call" | custom-call | flops 1000000000 | bytes 4000000 | tf_op jit(solution)/shard_map/pallas_call | solution.py:426
  15.4 9.8 %all-to-all-done.own = bf16[16,304,128]{2,1,0:T(8,128)(2,1)} async-done(((bf16[16,304,128]{2,1,0:T(8,128)(2,1)}), bf16[16,304,128]{2,1,0:T(8,128)(2,1)}, u32[]{:S(2)}, u32[]{:S(2)}) %all-to-all-start) | async-done | bytes 1245216 | tf_op jit(solution)/shard_map/all_to_all | solution.py:531
  25.2 7.2 %collective-permute-start = (bf16[16,304,128]{2,1,0:T(8,128)(2,1)}, bf16[16,304,128]{2,1,0:T(8,128)(2,1)}, u32[]{:S(2)}, u32[]{:S(2)}) collective-permute-start(bf16[16,304,128]{2,1,0:T(8,128)(2,1)} %all-to-all-done.own), channel_id=1, source_target_pairs={{0,8},{8,0},{1,9},{9,1},{2,10},{10,2},{3,11},{11,3},{4,12},{12,4},... | collective-permute-start | bytes 3735560 | tf_op jit(solution)/shard_map/ppermute | solution.py:409
  32.4 0.7 pad_add_fusion.place
  33.1 2.2 %collective-permute-done.other = bf16[16,304,128]{2,1,0:T(8,128)(2,1)} collective-permute-done((bf16[16,304,128]{2,1,0:T(8,128)(2,1)}, bf16[16,304,128]{2,1,0:T(8,128)(2,1)}, u32[]{:S(2)}, u32[]{:S(2)}) %collective-permute-start) | collective-permute-done | bytes 1245216 | tf_op jit(solution)/shard_map/ppermute | solution.py:409
  35.3 6.9 %shard_map.84 = (f32[72,1024]{1,0:T(8,128)}, f32[32,8,128]{2,1,0:T(8,128)}, f32[8,128]{1,0:T(8,128)}, f32[64,128]{1,0:T(8,128)}, bf16[144,64,128]{2,1,0:T(8,128)(2,1)}) custom-call(s32[2]{0:T(128)} %pad_add_fusion.place, bf16[16,304,128]{2,1,0:T(8,128)(2,1)} %all-to-all-done.own, bf16[16,304,128]{2,1,0:T(8,128)(2,1)} %collective-permute-done.other, ...), custom_call_target="tpu_custom_call" | custom-call | flops 1000000000 | bytes 8000000 | tf_op jit(solution)/shard_map/pallas_call | solution.py:442
  42.2 4.6 %all-to-all-start.1 = ((f32[32,8,128]{2,1,0:T(8,128)}), f32[32,8,128]{2,1,0:T(8,128)}, u32[]{:S(2)}, u32[]{:S(2)}) async-start(f32[32,8,128]{2,1,0:T(8,128)} %get-tuple-element.24.refs_1_), calls=%async_computation.1 | async-start | bytes 262144 | tf_op jit(solution)/shard_map/all_to_all | solution.py:541
  46.9 3.8 %shard_map.85.refs_4_ = f32[144,16,128]{2,1,0:T(8,128)} custom-call(f32[72,1024]{1,0:T(8,128)} %get-tuple-element.27.expo, bf16[864,72]{1,0:T(8,128)(2,1)} %constant.31.clone.table), custom_call_target="tpu_custom_call" | custom-call | flops 1000000000 | bytes 3000000 | tf_op jit(solution)/shard_map/pallas_call | solution.py:466
  50.7 3.8 %all-to-all-done.1.refs_0_ = f32[32,8,128]{2,1,0:T(8,128)} async-done(((f32[32,8,128]{2,1,0:T(8,128)}), f32[32,8,128]{2,1,0:T(8,128)}, u32[]{:S(2)}, u32[]{:S(2)}) %all-to-all-start.1) | async-done | bytes 131104 | tf_op jit(solution)/shard_map/all_to_all | solution.py:541
  54.5 3.8 %shard_map.86 = bf16[4,480,128]{2,1,0:T(8,128)(2,1)} custom-call(f32[32,8,128]{2,1,0:T(8,128)} %all-to-all-done.1.refs_0_, f32[32,8,128]{2,1,0:T(8,128)} %get-tuple-element.24.refs_1_, f32[8,128]{1,0:T(8,128)} %get-tuple-element.25.refs_2_, f32[64,128]{1,0:T(8,128)} %get-tuple-element.26.refs_3_, f32[144,16,128]{2,1,0:T(8,128)} %shard_map.85.refs_4_, ...), custom_call_target="tpu_custom_call" | custom-call | flops 1000000000 | bytes 8000000 | tf_op jit(solution)/shard_map/pallas_call | solution.py:483
  58.3 0.0 copy-start
  58.3 18.4 %all_to_all.15.pieces = bf16[4,480,128]{2,1,0:T(8,128)(2,1)S(1)} all-to-all(bf16[4,480,128]{2,1,0:T(8,128)(2,1)} %shard_map.86), channel_id=1, replica_groups=mesh['x_lo'=2,'z_hi'=4,'z_lo'=4,'core'=2,'x_hi'=2,'y'=4] {'z_lo'}, dimensions={0} | all-to-all | bytes 983040 | tf_op jit(solution)/shard_map/all_to_all | solution.py:545
  76.7 0.1 shard_map.87
  76.8 26.5 %all-gather = bf16[1920,128]{1,0:T(8,128)(2,1)S(1)} all-gather(bf16[480,128]{1,0:T(8,128)(2,1)S(1)} %shard_map.87), channel_id=2, replica_groups=mesh['x_lo'=2,'z_hi'=4,'z_lo'=4,'core'=2,'x_hi'=2,'y'=4] {'z_hi'}, dimensions={0}, use_global_device_ids=true | all-gather | bytes 614400 | tf_op jit(solution)/shard_map/all_gather | solution.py:547
  103.2 0.2 shard_map.88
  103.4 13.8 %all-gather.1 = bf16[1920,128]{1,0:T(8,128)(2,1)S(1)} all-gather(bf16[480,128]{1,0:T(8,128)(2,1)S(1)} %shard_map.88), channel_id=3, replica_groups=mesh['x_lo'=2,'z_hi'=4,'z_lo'=4,'core'=2,'x_hi'=2,'y'=4] {'z_lo'}, dimensions={0}, use_global_device_ids=true | all-gather | bytes 614400 | tf_op jit(solution)/shard_map/all_gather | solution.py:551
  117.2 2.1 %collective-permute-start.1 = (bf16[4,480,128]{2,1,0:T(8,128)(2,1)S(1)}, bf16[4,480,128]{2,1,0:T(8,128)(2,1)S(1)}, u32[]{:S(2)}, u32[]{:S(2)}) collective-permute-start(bf16[4,480,128]{2,1,0:T(8,128)(2,1)S(1)} %bitcast.12), channel_id=1, source_target_pairs={{0,256},{256,0},{1,257},{257,1},{2,258},{258,2},{3,259},{259,3},{4... | collective-permute-start | bytes 1474568 | tf_op jit(solution)/shard_map/ppermute | solution.py:409
  119.3 10.7 %all-gather.2 = bf16[8,480,128]{2,1,0:T(8,128)(2,1)S(1)} all-gather(bf16[4,480,128]{2,1,0:T(8,128)(2,1)S(1)} %bitcast.13), channel_id=4, replica_groups=mesh['x_lo'=2,'z_hi'=4,'z_lo'=4,'core'=2,'x_hi'=2,'y'=4] {'core'}, dimensions={0}, use_global_device_ids=true | all-gather | bytes 1474560 | tf_op jit(solution)/shard_map/all_gather | solution.py:553
  130.1 2.8 %shard_map.89.refs_0_ = bf16[50,64,288]{2,1,0:T(8,128)(2,1)} custom-call(s32[1]{0:T(128)} %bitcast.4.place, bf16[4,144,288]{2,1,0:T(8,128)(2,1)S(1)} %copy-done, bf16[2,4,480,128]{3,2,1,0:T(8,128)(2,1)S(1)} %bitcast.10), custom_call_target="tpu_custom_call" | custom-call | flops 1000 | bytes 1000 | tf_op jit(solution)/shard_map/pallas_call | solution.py:507
  132.9 0.0 collective-permute-done.1
  132.9 5.5 %all-gather.3 = bf16[8,480,128]{2,1,0:T(8,128)(2,1)S(1)} all-gather(bf16[4,480,128]{2,1,0:T(8,128)(2,1)S(1)} %collective-permute-done.1), channel_id=5, replica_groups=mesh['x_lo'=2,'z_hi'=4,'z_lo'=4,'core'=2,'x_hi'=2,'y'=4] {'core'}, dimensions={0}, use_global_device_ids=true | all-gather | bytes 1474560 | tf_op jit(solution)/shard_map/all_gather | solution.py:555
  138.4 2.8 %shard_map.90 = bf16[50,64,288]{2,1,0:T(8,128)(2,1)} custom-call(s32[1]{0:T(128)} %bitcast.place, bf16[4,144,288]{2,1,0:T(8,128)(2,1)S(1)} %copy-done, bf16[2,4,480,128]{3,2,1,0:T(8,128)(2,1)S(1)} %bitcast.9, bf16[50,64,288]{2,1,0:T(8,128)(2,1)} %shard_map.89.refs_0_), custom_call_target="tpu_custom_call", output_to_operand_aliasing={{}: (3, {})} | custom-call | flops 1000 | bytes 1000 | tf_op jit(solution)/shard_map/pallas_call | solution.py:507
  (1 shorter events, 0.0 us)
Async XLA Ops:
  2.8 22.4 %all-to-all-start = ((bf16[16,304,128]{2,1,0:T(8,128)(2,1)}), bf16[16,304,128]{2,1,0:T(8,128)(2,1)}, u32[]{:S(2)}, u32[]{:S(2)}) async-start(bf16[16,304,128]{2,1,0:T(8,128)(2,1)} %shard_map.82), calls=%async_computation | async-start | bytes 2490368 | tf_op jit(solution)/shard_map/all_to_all | solution.py:531
  25.2 10.1 %collective-permute-start = (bf16[16,304,128]{2,1,0:T(8,128)(2,1)}, bf16[16,304,128]{2,1,0:T(8,128)(2,1)}, u32[]{:S(2)}, u32[]{:S(2)}) collective-permute-start(bf16[16,304,128]{2,1,0:T(8,128)(2,1)} %all-to-all-done.own), channel_id=1, source_target_pairs={{0,8},{8,0},{1,9},{9,1},{2,10},{10,2},{3,11},{11,3},{4,12},{12,4},... | collective-permute-start | bytes 3735560 | tf_op jit(solution)/shard_map/ppermute | solution.py:409
  42.2 12.3 %all-to-all-start.1 = ((f32[32,8,128]{2,1,0:T(8,128)}), f32[32,8,128]{2,1,0:T(8,128)}, u32[]{:S(2)}, u32[]{:S(2)}) async-start(f32[32,8,128]{2,1,0:T(8,128)} %get-tuple-element.24.refs_1_), calls=%async_computation.1 | async-start | bytes 262144 | tf_op jit(solution)/shard_map/all_to_all | solution.py:541
  58.3 71.8 %copy-start = (bf16[4,144,288]{2,1,0:T(8,128)(2,1)S(1)}, bf16[4,144,288]{2,1,0:T(8,128)(2,1)}, u32[]{:S(2)}) copy-start(bf16[4,144,288]{2,1,0:T(8,128)(2,1)} %constant.32.clone.table) | copy-start | bytes 995332
  117.2 15.7 %collective-permute-start.1 = (bf16[4,480,128]{2,1,0:T(8,128)(2,1)S(1)}, bf16[4,480,128]{2,1,0:T(8,128)(2,1)S(1)}, u32[]{:S(2)}, u32[]{:S(2)}) collective-permute-start(bf16[4,480,128]{2,1,0:T(8,128)(2,1)S(1)} %bitcast.12), channel_id=1, source_target_pairs={{0,256},{256,0},{1,257},{257,1},{2,258},{258,2},{3,259},{259,3},{4... | collective-permute-start | bytes 1474568 | tf_op jit(solution)/shard_map/ppermute | solution.py:409

commit v8 on v7

--- a/solution.py
+++ b/solution.py
@@ -26,6 +26,10 @@
 KPAD = 16
 KROWS = KPAD // 2
 PARTS = 2
+EXPO = 8 * 72
+KEPT = EXPO + 8 + 64
+ROOMY = 36000
+LONG = 1100
 GROUPS = ((0, 5), (5, 9), (9, 13))
 SOURCES = X * SIDE
 COUNT = MINE * CORE * SOURCES
@@ -178,7 +182,7 @@
     lax.fori_loop(0, HALF, step, 0, unroll=36)
 
 
-def score_kernel(place, own, other, rmat, power, table, expo, stats, by_class, csq, far, wide, pairs, ydata, sem):
+def score_kernel(place, own, other, rmat, power, table, stats, far_kept, far, wide, pairs, ydata, kept, sem):
     core, x_lo = place[0], place[1]
 
     def widen(s, carry):
@@ -195,7 +199,7 @@
     square = factor * factor
     side = left(square.shape)
     square = jnp.concatenate([jnp.where(side, square, 0.0), jnp.where(side, turn(square), 0.0)], axis=0)
-    csq[...] = square
+    kept[EXPO + KROWS : KEPT] = square
     energy = lax.dot_general(
         power[...],
         jnp.concatenate([square, square], axis=0),
@@ -221,7 +225,7 @@
         return carry
 
     lax.fori_loop(0, HALF, step, 0, unroll=48)
-    keep = pltpu.make_async_copy(ydata, far, sem)
+    keep = pltpu.make_async_copy(ydata, far.at[pl.ds(0, HALF)], sem.at[0])
     keep.start()
     top = jnp.full((1, LANES), -3.0e38, f32)
     lane_side = left((ROT, LANES))
@@ -237,26 +241,32 @@
             score = jnp.where(lane_side, score, -3.0e38)
         if kk == 0:
             score = jnp.where(jnp.logical_and(lane_side, x_lo == 1), -3.0e38, score)
-        expo[:, kk * LANES : (kk + 1) * LANES] = score
+        kept[kk * ROT : (kk + 1) * ROT] = score
         top = jnp.maximum(top, jnp.max(score, axis=0, keepdims=True))
     top = jnp.maximum(top, turn(top))
     total = jnp.zeros((1, LANES), f32)
     for kk in range(KROWS):
-        value = jnp.exp(expo[:, kk * LANES : (kk + 1) * LANES] - top)
-        expo[:, kk * LANES : (kk + 1) * LANES] = value
+        value = jnp.exp(kept[kk * ROT : (kk + 1) * ROT] - top)
+        kept[kk * ROT : (kk + 1) * ROT] = value
         part = jnp.sum(value, axis=0, keepdims=True)
-        by_class[kk : kk + 1] = part
+        kept[EXPO + kk : EXPO + kk + 1] = part
         total = total + part
     total = total + turn(total)
+    store = pltpu.make_async_copy(kept, far_kept.at[pl.ds(0, KEPT)], sem.at[1])
+    store.start()
     pair = jnp.where(lax.broadcasted_iota(jnp.int32, (8, LANES), 0) == 0, top, total)
     for s in range(CORE * SOURCES):
         stats[s] = pair
     keep.wait()
-
-
-def post_kernel(expo, table, far, rows, out, sem):
+    store.wait()
+
+
+def post_kernel(far_kept, table, far, rows, out, expo, sem):
+    fetch = pltpu.make_async_copy(far_kept.at[pl.ds(0, EXPO)], expo, sem)
+    fetch.start()
+    fetch.wait()
     for kk in range(0, KROWS, 2):
-        both = dot3(table, expo[:, kk * LANES : (kk + 2) * LANES])
+        both = dot3(table, jnp.concatenate([expo[k * ROT : (k + 1) * ROT] for k in (kk, kk + 1)], axis=1))
         rows[kk * ANG : (kk + 1) * ANG] = both[:, :LANES]
         rows[(kk + 1) * ANG : (kk + 2) * ANG] = both[:, LANES:]
 
@@ -273,8 +283,10 @@
 
 
 def sum_kernel(*refs):
-    far_small, (far_post, far_ydata, out, rows, slots, post, ydata) = refs[:4], refs[4:11]
-    small, (sem, small_sem) = refs[11:15], refs[15:]
+    kept = refs[2]
+    far_small = refs[:2] + (kept.at[pl.ds(EXPO, KROWS)], kept.at[pl.ds(EXPO + KROWS, COUNT)])
+    far_post, far_ydata, out, rows, slots, post, ydata = refs[3:10]
+    small, (sem, small_sem) = refs[10:14], refs[14:]
     all_stats, stats, by_class, csq = small
     first_copies = [pltpu.make_async_copy(a, b, small_sem.at[i]) for i, (a, b) in enumerate(zip(far_small, small))]
     for copy in first_copies:
@@ -434,7 +446,7 @@
         ],
         10**9,
         4 * 10**6,
-        limit=64,
+        limit=24,
     )(start, references, forward)
 
 
@@ -443,33 +455,33 @@
         score_kernel,
         [SMEM] + [VMEM] * 5,
         [
-            ((ROT, KROWS * LANES), f32),
             ((CORE * SOURCES, 8, LANES), f32),
-            ((KROWS, LANES), f32),
-            ((COUNT, LANES), f32),
-            ((HALF, COUNT, LANES), bf16),
+            ((ROOMY, LANES), f32),
+            ((LONG, COUNT, LANES), bf16),
         ],
         [
             pltpu.VMEM(((CORE * SOURCES + 1) * MSG, LANES), f32),
             pltpu.VMEM(((KROWS + 1) * ANG, LANES), f32),
             pltpu.VMEM((HALF, COUNT, LANES), bf16),
-            pltpu.SemaphoreType.DMA,
+            pltpu.VMEM((KEPT, LANES), f32),
+            pltpu.SemaphoreType.DMA((2,)),
         ],
         10**9,
         8 * 10**6,
-        limit=64,
-        out_specs=[VMEM] * 4 + [HBM],
+        limit=48,
+        out_specs=[VMEM, HBM, HBM],
     )(place, own, other, rmat, power, table)
 
 
 def posts(expo, table):
     return call(
         post_kernel,
-        [VMEM, VMEM],
+        [HBM, VMEM],
         [((HALF, KPAD, LANES), f32)],
         [
             pltpu.VMEM(((KROWS + 1) * ANG, LANES), f32),
             pltpu.VMEM((HALF, KPAD, LANES), f32),
+            pltpu.VMEM((EXPO, LANES), f32),
             pltpu.SemaphoreType.DMA,
         ],
         10**9,
@@ -479,10 +491,10 @@
     )(expo, table)
 
 
-def sums_of(all_stats, stats, by_class, csq, post, ydata):
+def sums_of(all_stats, stats, kept, post, ydata):
     return call(
         sum_kernel,
-        [HBM] * 6,
+        [HBM] * 5,
         [((ZL, SLOT, LANES), bf16)],
         [
             pltpu.VMEM(((KPAD + 1) * HALF, LANES), f32),
@@ -499,7 +511,7 @@
         10**9,
         8 * 10**6,
         limit=64,
-    )(all_stats, stats, by_class, csq, post, ydata)
+    )(all_stats, stats, kept, post, ydata)
 
 
 def images(place, hats, inverse, result):
@@ -532,15 +544,15 @@
     start = (core * PER_CORE + x_lo * (KD - 1)).reshape(1)
     rmat, power = classes(start, references, forward)
     part = lax.axis_index("z_lo").reshape(1)
-    own, rmat, power, part = lax.optimization_barrier((own, rmat, power, part))
+    own, part = lax.optimization_barrier((own, part))
     other = swap("core", own)
 
-    expo, stats, by_class, csq, ydata = scores(
+    stats, kept, ydata = scores(
         place, own, other, rmat, power, jnp.asarray(search_table().reshape(3 * ROT, ANG))
     )
     all_stats = lax.all_to_all(stats, ("core", "x_lo", "x_hi", "y"), 0, 0, tiled=True)
-    post = posts(expo, jnp.asarray(post_table().reshape(3 * ANG, ROT)))
-    sums = sums_of(all_stats, stats, by_class, csq, post, ydata)
+    post = posts(kept, jnp.asarray(post_table().reshape(3 * ANG, ROT)))
+    sums = sums_of(all_stats, stats, kept, post, ydata)
 
     near = lax.all_to_all(sums, "z_lo", 0, 0, tiled=True)
     near = call(fold_kernel, [VMEM], [((SLOT, LANES), bf16)], [], 10**6, 10**6, limit=20)(near)

time: 142 us -> 141 us (level)
  Pallas kernels: 28.2 us -> 25.1 us
  waiting for transfers between devices: 15.8 us -> 17.6 us
  local copies, waits for them, and re-layouts: 0.01 us -> 1.71 us
    all_to_all x1, waiting for transfers between devices: 9.81 us -> 14.8 us  [body(): own = lax.all_to_all(messages, ('x_lo', 'x_hi', 'y'), 0, 0, tiled=True)]
    pallas_call x1, Pallas kernels: 4.97 us -> 2.18 us  [classes(): call(class_kernel, [SMEM, HBM, VMEM], [((HALF, KPAD, LANES), bf16), ((KPA...]
    ppermute x2, waiting for transfers between devices: 2.22 us -> 0.01 us  [swap(): return lax.ppermute(value, axis, [(0, 1), (1, 0)])]
    unnamed x2 -> x8, local copies, waits for them, and re-layouts: 0.01 us -> 1.71 us
  transfers between devices with their start and end apart: 4 -> 4, of which waited for: 3 -> 2; matrix products, arithmetic and copies ran while one was open for 0% -> 0% of each run, Pallas kernels for 8% -> 7%
where the time goes in v8:
time: 141 us
  blocking collectives  74.8 us (53%)
  Pallas kernels  25.1 us (18%)
  starting transfers between devices  21.4 us (15%)
  waiting for transfers between devices  17.6 us (12%)
  local copies, waits for them, and re-layouts  1.71 us (1%)
    all_gather x1, blocking collectives, body(): near = lax.all_gather(near, 'z_hi')  26.8 us
    all_to_all x1, blocking collectives, body(): near = lax.all_to_all(sums, 'z_lo', 0, 0, tiled=True)  18.6 us
    all_to_all x1, waiting for transfers between devices, body(): own = lax.all_to_all(messages, ('x_lo', 'x_hi', 'y'), 0, 0, tiled=True)  14.8 us
    all_gather x1, blocking collectives, body(): near = lax.all_gather(hat, 'z_lo')  13.4 us
    all_gather x1, blocking collectives, body(): result = images(x_lo, lax.all_gather(near, 'core'), inverse, None)  10.7 us
    ppermute x2, starting transfers between devices, swap(): return lax.ppermute(value, axis, [(0, 1), (1, 0)])  9.26 us
    all_to_all x1, starting transfers between devices, body(): own = lax.all_to_all(messages, ('x_lo', 'x_hi', 'y'), 0, 0, tiled=True)  7.73 us
    pallas_call x1, Pallas kernels, scores(): call(score_kernel, [SMEM] + [VMEM] * 5, [((CORE * SOURCES, 8, LANES), f32...  5.79 us
  transfers between devices with their start and end apart: 4, of which 2 were waited for; matrix products, arithmetic and copies ran while one was open for 0% of the time, Pallas kernels for 7%

profile of v8, /device:TPU:1, one launch (start us, length us, event | category | flops | bytes accessed | tf_op | source)
XLA Modules:
  0.0 140.8 jit_solution(2645494602384079749)
XLA Ops:
  0.0 2.7 %shard_map.82 = bf16[16,304,128]{2,1,0:T(8,128)(2,1)} custom-call(s32[2]{0:T(128)} %ids.1, bf16[2,64,288]{2,1,0:T(8,128)(2,1)} %x.1, f32[32,64]{1,0:T(8,128)} %ctf.1, bf16[3,288,288]{2,1,0:T(8,128)(2,1)} %constant.29.clone.table), custom_call_target="tpu_custom_call" | custom-call | flops 10000000 | bytes 1000000 | tf_op jit(solution)/shard_map/pallas_call | solution.py:425
  2.8 0.0 copy-start.1
  2.8 0.0 copy-start.3
  2.8 7.7 %all-to-all-start = ((bf16[16,304,128]{2,1,0:T(8,128)(2,1)}), bf16[16,304,128]{2,1,0:T(8,128)(2,1)S(1)}, u32[]{:S(2)}, u32[]{:S(2)}) async-start(bf16[16,304,128]{2,1,0:T(8,128)(2,1)} %shard_map.82), calls=%async_computation | async-start | bytes 2490368 | tf_op jit(solution)/shard_map/all_to_all | solution.py:543
  10.5 14.8 %all-to-all-done.own = bf16[16,304,128]{2,1,0:T(8,128)(2,1)S(1)} async-done(((bf16[16,304,128]{2,1,0:T(8,128)(2,1)}), bf16[16,304,128]{2,1,0:T(8,128)(2,1)S(1)}, u32[]{:S(2)}, u32[]{:S(2)}) %all-to-all-start) | async-done | bytes 1245216 | tf_op jit(solution)/shard_map/all_to_all | solution.py:543
  25.3 7.0 %collective-permute-start = (bf16[16,304,128]{2,1,0:T(8,128)(2,1)S(1)}, bf16[16,304,128]{2,1,0:T(8,128)(2,1)S(1)}, u32[]{:S(2)}, u32[]{:S(2)}) collective-permute-start(bf16[16,304,128]{2,1,0:T(8,128)(2,1)S(1)} %all-to-all-done.own), channel_id=1, source_target_pairs={{0,8},{8,0},{1,9},{9,1},{2,10},{10,2},{3,11},{11,3},{4,12},{12,4},... | collective-permute-start | bytes 3735560 | tf_op jit(solution)/shard_map/ppermute | solution.py:421
  32.4 1.7 %copy-done.2 = bf16[50,64,288]{2,1,0:T(8,128)(2,1)S(1)} copy-done((bf16[50,64,288]{2,1,0:T(8,128)(2,1)S(1)}, bf16[50,64,288]{2,1,0:T(8,128)(2,1)}, u32[]{:S(2)}) %copy-start.2) | copy-done | bytes 1843224
  34.1 2.2 %shard_map.83 = (bf16[144,16,128]{2,1,0:T(8,128)(2,1)S(1)}, f32[16,128]{1,0:T(8,128)S(1)}) custom-call(s32[1]{0:T(128)} %bitcast.4.start, bf16[50,64,288]{2,1,0:T(8,128)(2,1)S(1)} %copy-done.2, bf16[3,288,288]{2,1,0:T(8,128)(2,1)S(1)} %copy-done.1), custom_call_target="tpu_custom_call" | custom-call | flops 1000000000 | bytes 4000000 | tf_op jit(solution)/shard_map/pallas_call | solution.py:438
  36.3 0.1 pad_add_fusion.place
  36.3 5.8 %shard_map.84 = (f32[32,8,128]{2,1,0:T(8,128)}, f32[36000,128]{1,0:T(8,128)}, bf16[1100,64,128]{2,1,0:T(8,128)(2,1)}) custom-call(s32[2]{0:T(128)S(1)} %pad_add_fusion.place, bf16[16,304,128]{2,1,0:T(8,128)(2,1)S(1)} %all-to-all-done.own, bf16[16,304,128]{2,1,0:T(8,128)(2,1)S(1)} %collective-permute-done.other, ...), custom_call_target="tpu_custom_call" | custom-call | flops 1000000000 | bytes 8000000 | tf_op jit(solution)/shard_map/pallas_call | solution.py:454
  42.1 4.4 %all-to-all-start.1 = ((f32[32,8,128]{2,1,0:T(8,128)}), f32[32,8,128]{2,1,0:T(8,128)}, u32[]{:S(2)}, u32[]{:S(2)}) async-start(f32[32,8,128]{2,1,0:T(8,128)} %get-tuple-element.18.refs_1_), calls=%async_computation.1 | async-start | bytes 262144 | tf_op jit(solution)/shard_map/all_to_all | solution.py:553
  46.5 4.7 %shard_map.85.refs_3_ = f32[144,16,128]{2,1,0:T(8,128)} custom-call(f32[36000,128]{1,0:T(8,128)} %get-tuple-element.19.far_kept.refs_2_, bf16[864,72]{1,0:T(8,128)(2,1)} %constant.31.clone.table), custom_call_target="tpu_custom_call" | custom-call | flops 1000000000 | bytes 3000000 | tf_op jit(solution)/shard_map/pallas_call | solution.py:477
  51.2 2.9 %all-to-all-done.1.refs_0_ = f32[32,8,128]{2,1,0:T(8,128)} async-done(((f32[32,8,128]{2,1,0:T(8,128)}), f32[32,8,128]{2,1,0:T(8,128)}, u32[]{:S(2)}, u32[]{:S(2)}) %all-to-all-start.1) | async-done | bytes 131104 | tf_op jit(solution)/shard_map/all_to_all | solution.py:553
  54.1 3.7 %shard_map.86 = bf16[4,480,128]{2,1,0:T(8,128)(2,1)} custom-call(f32[32,8,128]{2,1,0:T(8,128)} %all-to-all-done.1.refs_0_, f32[32,8,128]{2,1,0:T(8,128)} %get-tuple-element.18.refs_1_, f32[36000,128]{1,0:T(8,128)} %get-tuple-element.19.far_kept.refs_2_, f32[144,16,128]{2,1,0:T(8,128)} %shard_map.85.refs_3_, bf16[1100,64,128]{2,1,0:T(8,128)(2,1)} %get-tuple-element.20.refs_4_), custom_call_target="tpu_custom_call" | custom-call | flops 1000000000 | bytes 8000000 | tf_op jit(solution)/shard_map/pallas_call | solution.py:495
  57.8 18.6 %all_to_all.15.pieces = bf16[4,480,128]{2,1,0:T(8,128)(2,1)S(1)} all-to-all(bf16[4,480,128]{2,1,0:T(8,128)(2,1)} %shard_map.86), channel_id=1, replica_groups=mesh['x_lo'=2,'z_hi'=4,'z_lo'=4,'core'=2,'x_hi'=2,'y'=4] {'z_lo'}, dimensions={0} | all-to-all | bytes 983040 | tf_op jit(solution)/shard_map/all_to_all | solution.py:557
  76.4 0.1 shard_map.87
  76.5 26.8 %all-gather = bf16[1920,128]{1,0:T(8,128)(2,1)S(1)} all-gather(bf16[480,128]{1,0:T(8,128)(2,1)S(1)} %shard_map.87), channel_id=2, replica_groups=mesh['x_lo'=2,'z_hi'=4,'z_lo'=4,'core'=2,'x_hi'=2,'y'=4] {'z_hi'}, dimensions={0}, use_global_device_ids=true | all-gather | bytes 614400 | tf_op jit(solution)/shard_map/all_gather | solution.py:559
  103.3 0.2 shard_map.88
  103.4 13.4 %all-gather.1 = bf16[1920,128]{1,0:T(8,128)(2,1)S(1)} all-gather(bf16[480,128]{1,0:T(8,128)(2,1)S(1)} %shard_map.88), channel_id=3, replica_groups=mesh['x_lo'=2,'z_hi'=4,'z_lo'=4,'core'=2,'x_hi'=2,'y'=4] {'z_lo'}, dimensions={0}, use_global_device_ids=true | all-gather | bytes 614400 | tf_op jit(solution)/shard_map/all_gather | solution.py:563
  116.8 2.2 %collective-permute-start.1 = (bf16[4,480,128]{2,1,0:T(8,128)(2,1)S(1)}, bf16[4,480,128]{2,1,0:T(8,128)(2,1)S(1)}, u32[]{:S(2)}, u32[]{:S(2)}) collective-permute-start(bf16[4,480,128]{2,1,0:T(8,128)(2,1)S(1)} %bitcast.12), channel_id=1, source_target_pairs={{0,256},{256,0},{1,257},{257,1},{2,258},{258,2},{3,259},{259,3},{4... | collective-permute-start | bytes 1474568 | tf_op jit(solution)/shard_map/ppermute | solution.py:421
  119.1 10.7 %all-gather.2 = bf16[8,480,128]{2,1,0:T(8,128)(2,1)S(1)} all-gather(bf16[4,480,128]{2,1,0:T(8,128)(2,1)S(1)} %bitcast.13), channel_id=4, replica_groups=mesh['x_lo'=2,'z_hi'=4,'z_lo'=4,'core'=2,'x_hi'=2,'y'=4] {'core'}, dimensions={0}, use_global_device_ids=true | all-gather | bytes 1474560 | tf_op jit(solution)/shard_map/all_gather | solution.py:565
  129.8 2.8 %shard_map.89.refs_0_ = bf16[50,64,288]{2,1,0:T(8,128)(2,1)} custom-call(s32[1]{0:T(128)} %bitcast.3.place, bf16[4,144,288]{2,1,0:T(8,128)(2,1)S(1)} %copy-done, bf16[2,4,480,128]{3,2,1,0:T(8,128)(2,1)S(1)} %bitcast.10), custom_call_target="tpu_custom_call" | custom-call | flops 1000 | bytes 1000 | tf_op jit(solution)/shard_map/pallas_call | solution.py:519
  132.7 5.3 %all-gather.3 = bf16[8,480,128]{2,1,0:T(8,128)(2,1)S(1)} all-gather(bf16[4,480,128]{2,1,0:T(8,128)(2,1)S(1)} %collective-permute-done.1), channel_id=5, replica_groups=mesh['x_lo'=2,'z_hi'=4,'z_lo'=4,'core'=2,'x_hi'=2,'y'=4] {'core'}, dimensions={0}, use_global_device_ids=true | all-gather | bytes 1474560 | tf_op jit(solution)/shard_map/all_gather | solution.py:567
  138.0 2.8 %shard_map.90 = bf16[50,64,288]{2,1,0:T(8,128)(2,1)} custom-call(s32[1]{0:T(128)} %bitcast.place, bf16[4,144,288]{2,1,0:T(8,128)(2,1)S(1)} %copy-done, bf16[2,4,480,128]{3,2,1,0:T(8,128)(2,1)S(1)} %bitcast.9, bf16[50,64,288]{2,1,0:T(8,128)(2,1)} %shard_map.89.refs_0_), custom_call_target="tpu_custom_call", output_to_operand_aliasing={{}: (3, {})} | custom-call | flops 1000 | bytes 1000 | tf_op jit(solution)/shard_map/pallas_call | solution.py:519
  (7 shorter events, 0.0 us)
Async XLA Ops:
  2.8 29.6 %copy-start.1 = (bf16[3,288,288]{2,1,0:T(8,128)(2,1)S(1)}, bf16[3,288,288]{2,1,0:T(8,128)(2,1)}, u32[]{:S(2)}) copy-start(bf16[3,288,288]{2,1,0:T(8,128)(2,1)} %constant.29.clone.table) | copy-start | bytes 1492996
  2.8 33.6 %copy-start.3 = (bf16[216,288]{1,0:T(8,128)(2,1)S(1)}, bf16[216,288]{1,0:T(8,128)(2,1)}, u32[]{:S(2)}) copy-start(bf16[216,288]{1,0:T(8,128)(2,1)} %constant.30.clone.table) | copy-start | bytes 373252
  2.8 22.5 %all-to-all-start = ((bf16[16,304,128]{2,1,0:T(8,128)(2,1)}), bf16[16,304,128]{2,1,0:T(8,128)(2,1)S(1)}, u32[]{:S(2)}, u32[]{:S(2)}) async-start(bf16[16,304,128]{2,1,0:T(8,128)(2,1)} %shard_map.82), calls=%async_computation | async-start | bytes 2490368 | tf_op jit(solution)/shard_map/all_to_all | solution.py:543
  25.3 11.0 %collective-permute-start = (bf16[16,304,128]{2,1,0:T(8,128)(2,1)S(1)}, bf16[16,304,128]{2,1,0:T(8,128)(2,1)S(1)}, u32[]{:S(2)}, u32[]{:S(2)}) collective-permute-start(bf16[16,304,128]{2,1,0:T(8,128)(2,1)S(1)} %all-to-all-done.own), channel_id=1, source_target_pairs={{0,8},{8,0},{1,9},{9,1},{2,10},{10,2},{3,11},{11,3},{4,12},{12,4},... | collective-permute-start | bytes 3735560 | tf_op jit(solution)/shard_map/ppermute | solution.py:421
  32.4 1.7 %copy-start.2 = (bf16[50,64,288]{2,1,0:T(8,128)(2,1)S(1)}, bf16[50,64,288]{2,1,0:T(8,128)(2,1)}, u32[]{:S(2)}) copy-start(bf16[50,64,288]{2,1,0:T(8,128)(2,1)} %refs.1) | copy-start | bytes 5529604
  42.1 11.9 %all-to-all-start.1 = ((f32[32,8,128]{2,1,0:T(8,128)}), f32[32,8,128]{2,1,0:T(8,128)}, u32[]{:S(2)}, u32[]{:S(2)}) async-start(f32[32,8,128]{2,1,0:T(8,128)} %get-tuple-element.18.refs_1_), calls=%async_computation.1 | async-start | bytes 262144 | tf_op jit(solution)/shard_map/all_to_all | solution.py:553
  57.8 72.0 %copy-start = (bf16[4,144,288]{2,1,0:T(8,128)(2,1)S(1)}, bf16[4,144,288]{2,1,0:T(8,128)(2,1)}, u32[]{:S(2)}) copy-start(bf16[4,144,288]{2,1,0:T(8,128)(2,1)} %constant.32.clone.table) | copy-start | bytes 995332
  116.8 15.8 %collective-permute-start.1 = (bf16[4,480,128]{2,1,0:T(8,128)(2,1)S(1)}, bf16[4,480,128]{2,1,0:T(8,128)(2,1)S(1)}, u32[]{:S(2)}, u32[]{:S(2)}) collective-permute-start(bf16[4,480,128]{2,1,0:T(8,128)(2,1)S(1)} %bitcast.12), channel_id=1, source_target_pairs={{0,256},{256,0},{1,257},{257,1},{2,258},{258,2},{3,259},{259,3},{4... | collective-permute-start | bytes 1474568 | tf_op jit(solution)/shard_map/ppermute | solution.py:421

commit v9 on v8

--- a/solution.py
+++ b/solution.py
@@ -151,8 +151,8 @@
         copy.wait()
 
 
-def class_kernel(start, refs, table, out, power, images, rows, sem):
-    copy = pltpu.make_async_copy(refs.at[pl.ds(start[0], KD)], images.at[pl.ds(0, KD)], sem)
+def class_kernel(refs, table, out, power, images, rows, sem):
+    copy = pltpu.make_async_copy(refs, images.at[pl.ds(0, KD)], sem)
     copy.start()
     images[KD:] = jnp.zeros((KPAD - KD, CYCLES, ANG), bf16)
     ones = jnp.ones((8, ANG), bf16)
@@ -434,10 +434,10 @@
     )(group_ids, particles, ctf_table, forward)
 
 
-def classes(start, references, forward):
+def classes(references, forward):
     return call(
         class_kernel,
-        [SMEM, HBM, VMEM],
+        [HBM, VMEM],
         [((HALF, KPAD, LANES), bf16), ((KPAD, LANES), f32)],
         [
             pltpu.VMEM((KPAD, CYCLES, ANG), bf16),
@@ -447,7 +447,7 @@
         10**9,
         4 * 10**6,
         limit=24,
-    )(start, references, forward)
+    )(references, forward)
 
 
 def scores(place, own, other, rmat, power, table):
@@ -541,10 +541,10 @@
 
     messages = share(group_ids, particles, ctf_table, forward)
     own = lax.all_to_all(messages, ("x_lo", "x_hi", "y"), 0, 0, tiled=True)
-    start = (core * PER_CORE + x_lo * (KD - 1)).reshape(1)
-    rmat, power = classes(start, references, forward)
+    mine = lax.dynamic_slice_in_dim(references, core * PER_CORE + x_lo * (KD - 1), KD, 0)
     part = lax.axis_index("z_lo").reshape(1)
-    own, part = lax.optimization_barrier((own, part))
+    own, part, mine = lax.optimization_barrier((own, part, mine))
+    rmat, power = classes(mine, forward)
     other = swap("core", own)
 
     stats, kept, ydata = scores(

time: 141 us -> 140 us (level)
    unnamed x8 -> x6, local copies, waits for them, and re-layouts: 1.71 us -> 0.02 us
  transfers between devices with their start and end apart: 4 -> 4, of which waited for: 2 -> 3; matrix products, arithmetic and copies ran while one was open for 0% -> 1% of each run, Pallas kernels for 7% -> 7%
where the time goes in v9:
time: 140 us
  blocking collectives  74.6 us (53%)
  Pallas kernels  25.1 us (18%)
  starting transfers between devices  21.7 us (16%)
  waiting for transfers between devices  16.8 us (12%)
    all_gather x1, blocking collectives, body(): near = lax.all_gather(near, 'z_hi')  26.8 us
    all_to_all x1, blocking collectives, body(): near = lax.all_to_all(sums, 'z_lo', 0, 0, tiled=True)  18.5 us
    all_to_all x1, waiting for transfers between devices, body(): own = lax.all_to_all(messages, ('x_lo', 'x_hi', 'y'), 0, 0, tiled=True)  13.6 us
    all_gather x1, blocking collectives, body(): near = lax.all_gather(hat, 'z_lo')  13.4 us
    all_gather x1, blocking collectives, body(): result = images(x_lo, lax.all_gather(near, 'core'), inverse, None)  10.8 us
    ppermute x2, starting transfers between devices, swap(): return lax.ppermute(value, axis, [(0, 1), (1, 0)])  9.34 us
    all_to_all x1, starting transfers between devices, body(): own = lax.all_to_all(messages, ('x_lo', 'x_hi', 'y'), 0, 0, tiled=True)  7.73 us
    pallas_call x1, Pallas kernels, scores(): call(score_kernel, [SMEM] + [VMEM] * 5, [((CORE * SOURCES, 8, LANES), f32...  5.88 us
  transfers between devices with their start and end apart: 4, of which 3 were waited for; matrix products, arithmetic and copies ran while one was open for 1% of the time, Pallas kernels for 7%

profile of v9, /device:TPU:1, one launch (start us, length us, event | category | flops | bytes accessed | tf_op | source)
XLA Modules:
  0.0 139.7 jit_solution(4797236889057887383)
XLA Ops:
  0.0 2.7 %shard_map.82 = bf16[16,304,128]{2,1,0:T(8,128)(2,1)} custom-call(s32[2]{0:T(128)} %ids.1, bf16[2,64,288]{2,1,0:T(8,128)(2,1)} %x.1, f32[32,64]{1,0:T(8,128)} %ctf.1, bf16[3,288,288]{2,1,0:T(8,128)(2,1)} %constant.33.clone.table), custom_call_target="tpu_custom_call" | custom-call | flops 10000000 | bytes 1000000 | tf_op jit(solution)/shard_map/pallas_call | solution.py:425
  2.8 0.0 copy-start.1
  2.8 7.7 %all-to-all-start = ((bf16[16,304,128]{2,1,0:T(8,128)(2,1)}), bf16[16,304,128]{2,1,0:T(8,128)(2,1)S(1)}, u32[]{:S(2)}, u32[]{:S(2)}) async-start(bf16[16,304,128]{2,1,0:T(8,128)(2,1)} %shard_map.82), calls=%async_computation | async-start | bytes 2490368 | tf_op jit(solution)/shard_map/all_to_all | solution.py:543
  10.5 1.2 constant_dynamic-slice_fusion.refs
  11.7 13.6 %all-to-all-done.own = bf16[16,304,128]{2,1,0:T(8,128)(2,1)S(1)} async-done(((bf16[16,304,128]{2,1,0:T(8,128)(2,1)}), bf16[16,304,128]{2,1,0:T(8,128)(2,1)S(1)}, u32[]{:S(2)}, u32[]{:S(2)}) %all-to-all-start) | async-done | bytes 1245216 | tf_op jit(solution)/shard_map/all_to_all | solution.py:543
  25.3 7.0 %collective-permute-start = (bf16[16,304,128]{2,1,0:T(8,128)(2,1)S(1)}, bf16[16,304,128]{2,1,0:T(8,128)(2,1)S(1)}, u32[]{:S(2)}, u32[]{:S(2)}) collective-permute-start(bf16[16,304,128]{2,1,0:T(8,128)(2,1)S(1)} %all-to-all-done.own), channel_id=1, source_target_pairs={{0,8},{8,0},{1,9},{9,1},{2,10},{10,2},{3,11},{11,3},{4,12},{12,4},... | collective-permute-start | bytes 3735560 | tf_op jit(solution)/shard_map/ppermute | solution.py:421
  32.4 0.1 pad_add_fusion.place
  32.4 2.2 %shard_map.83 = (bf16[144,16,128]{2,1,0:T(8,128)(2,1)S(1)}, f32[16,128]{1,0:T(8,128)S(1)}) custom-call(bf16[13,64,288]{2,1,0:T(8,128)(2,1)S(1)} %constant_dynamic-slice_fusion.refs, bf16[3,288,288]{2,1,0:T(8,128)(2,1)S(1)} %copy-done.1), custom_call_target="tpu_custom_call" | custom-call | flops 1000000000 | bytes 4000000 | tf_op jit(solution)/shard_map/pallas_call | solution.py:438
  34.6 0.3 collective-permute-done.other
  34.9 5.9 %shard_map.84 = (f32[32,8,128]{2,1,0:T(8,128)}, f32[36000,128]{1,0:T(8,128)}, bf16[1100,64,128]{2,1,0:T(8,128)(2,1)}) custom-call(s32[2]{0:T(128)S(1)} %pad_add_fusion.place, bf16[16,304,128]{2,1,0:T(8,128)(2,1)S(1)} %all-to-all-done.own, bf16[16,304,128]{2,1,0:T(8,128)(2,1)S(1)} %collective-permute-done.other, ...), custom_call_target="tpu_custom_call" | custom-call | flops 1000000000 | bytes 8000000 | tf_op jit(solution)/shard_map/pallas_call | solution.py:454
  40.8 4.6 %all-to-all-start.1 = ((f32[32,8,128]{2,1,0:T(8,128)}), f32[32,8,128]{2,1,0:T(8,128)}, u32[]{:S(2)}, u32[]{:S(2)}) async-start(f32[32,8,128]{2,1,0:T(8,128)} %get-tuple-element.20.refs_1_), calls=%async_computation.1 | async-start | bytes 262144 | tf_op jit(solution)/shard_map/all_to_all | solution.py:553
  45.4 4.7 %shard_map.85.refs_3_ = f32[144,16,128]{2,1,0:T(8,128)} custom-call(f32[36000,128]{1,0:T(8,128)} %get-tuple-element.21.far_kept.refs_2_, bf16[864,72]{1,0:T(8,128)(2,1)} %constant.35.clone.table), custom_call_target="tpu_custom_call" | custom-call | flops 1000000000 | bytes 3000000 | tf_op jit(solution)/shard_map/pallas_call | solution.py:477
  50.1 2.9 %all-to-all-done.1.refs_0_ = f32[32,8,128]{2,1,0:T(8,128)} async-done(((f32[32,8,128]{2,1,0:T(8,128)}), f32[32,8,128]{2,1,0:T(8,128)}, u32[]{:S(2)}, u32[]{:S(2)}) %all-to-all-start.1) | async-done | bytes 131104 | tf_op jit(solution)/shard_map/all_to_all | solution.py:553
  53.1 3.7 %shard_map.86 = bf16[4,480,128]{2,1,0:T(8,128)(2,1)} custom-call(f32[32,8,128]{2,1,0:T(8,128)} %all-to-all-done.1.refs_0_, f32[32,8,128]{2,1,0:T(8,128)} %get-tuple-element.20.refs_1_, f32[36000,128]{1,0:T(8,128)} %get-tuple-element.21.far_kept.refs_2_, f32[144,16,128]{2,1,0:T(8,128)} %shard_map.85.refs_3_, bf16[1100,64,128]{2,1,0:T(8,128)(2,1)} %get-tuple-element.22.refs_4_), custom_call_target="tpu_custom_call" | custom-call | flops 1000000000 | bytes 8000000 | tf_op jit(solution)/shard_map/pallas_call | solution.py:495
  56.8 18.5 %all_to_all.15.pieces = bf16[4,480,128]{2,1,0:T(8,128)(2,1)S(1)} all-to-all(bf16[4,480,128]{2,1,0:T(8,128)(2,1)} %shard_map.86), channel_id=1, replica_groups=mesh['x_lo'=2,'z_hi'=4,'z_lo'=4,'core'=2,'x_hi'=2,'y'=4] {'z_lo'}, dimensions={0} | all-to-all | bytes 983040 | tf_op jit(solution)/shard_map/all_to_all | solution.py:557
  75.3 0.1 shard_map.87
  75.4 26.8 %all-gather = bf16[1920,128]{1,0:T(8,128)(2,1)S(1)} all-gather(bf16[480,128]{1,0:T(8,128)(2,1)S(1)} %shard_map.87), channel_id=2, replica_groups=mesh['x_lo'=2,'z_hi'=4,'z_lo'=4,'core'=2,'x_hi'=2,'y'=4] {'z_hi'}, dimensions={0}, use_global_device_ids=true | all-gather | bytes 614400 | tf_op jit(solution)/shard_map/all_gather | solution.py:559
  102.1 0.2 shard_map.88
  102.3 13.4 %all-gather.1 = bf16[1920,128]{1,0:T(8,128)(2,1)S(1)} all-gather(bf16[480,128]{1,0:T(8,128)(2,1)S(1)} %shard_map.88), channel_id=3, replica_groups=mesh['x_lo'=2,'z_hi'=4,'z_lo'=4,'core'=2,'x_hi'=2,'y'=4] {'z_lo'}, dimensions={0}, use_global_device_ids=true | all-gather | bytes 614400 | tf_op jit(solution)/shard_map/all_gather | solution.py:563
  115.7 2.3 %collective-permute-start.1 = (bf16[4,480,128]{2,1,0:T(8,128)(2,1)S(1)}, bf16[4,480,128]{2,1,0:T(8,128)(2,1)S(1)}, u32[]{:S(2)}, u32[]{:S(2)}) collective-permute-start(bf16[4,480,128]{2,1,0:T(8,128)(2,1)S(1)} %bitcast.11), channel_id=1, source_target_pairs={{0,256},{256,0},{1,257},{257,1},{2,258},{258,2},{3,259},{259,3},{4... | collective-permute-start | bytes 1474568 | tf_op jit(solution)/shard_map/ppermute | solution.py:421
  118.0 10.8 %all-gather.2 = bf16[8,480,128]{2,1,0:T(8,128)(2,1)S(1)} all-gather(bf16[4,480,128]{2,1,0:T(8,128)(2,1)S(1)} %bitcast.12), channel_id=4, replica_groups=mesh['x_lo'=2,'z_hi'=4,'z_lo'=4,'core'=2,'x_hi'=2,'y'=4] {'core'}, dimensions={0}, use_global_device_ids=true | all-gather | bytes 1474560 | tf_op jit(solution)/shard_map/all_gather | solution.py:565
  128.9 2.8 %shard_map.89.refs_0_ = bf16[50,64,288]{2,1,0:T(8,128)(2,1)} custom-call(s32[1]{0:T(128)} %bitcast.3.place, bf16[4,144,288]{2,1,0:T(8,128)(2,1)S(1)} %copy-done, bf16[2,4,480,128]{3,2,1,0:T(8,128)(2,1)S(1)} %bitcast.9), custom_call_target="tpu_custom_call" | custom-call | flops 1000 | bytes 1000 | tf_op jit(solution)/shard_map/pallas_call | solution.py:519
  131.7 5.1 %all-gather.3 = bf16[8,480,128]{2,1,0:T(8,128)(2,1)S(1)} all-gather(bf16[4,480,128]{2,1,0:T(8,128)(2,1)S(1)} %collective-permute-done.1), channel_id=5, replica_groups=mesh['x_lo'=2,'z_hi'=4,'z_lo'=4,'core'=2,'x_hi'=2,'y'=4] {'core'}, dimensions={0}, use_global_device_ids=true | all-gather | bytes 1474560 | tf_op jit(solution)/shard_map/all_gather | solution.py:567
  136.9 2.8 %shard_map.90 = bf16[50,64,288]{2,1,0:T(8,128)(2,1)} custom-call(s32[1]{0:T(128)} %bitcast.place, bf16[4,144,288]{2,1,0:T(8,128)(2,1)S(1)} %copy-done, bf16[2,4,480,128]{3,2,1,0:T(8,128)(2,1)S(1)} %bitcast.8, bf16[50,64,288]{2,1,0:T(8,128)(2,1)} %shard_map.89.refs_0_), custom_call_target="tpu_custom_call", output_to_operand_aliasing={{}: (3, {})} | custom-call | flops 1000 | bytes 1000 | tf_op jit(solution)/shard_map/pallas_call | solution.py:519
  (6 shorter events, 0.0 us)
Async XLA Ops:
  2.8 29.7 %copy-start.1 = (bf16[3,288,288]{2,1,0:T(8,128)(2,1)S(1)}, bf16[3,288,288]{2,1,0:T(8,128)(2,1)}, u32[]{:S(2)}) copy-start(bf16[3,288,288]{2,1,0:T(8,128)(2,1)} %constant.33.clone.table) | copy-start | bytes 1492996
  2.8 22.5 %all-to-all-start = ((bf16[16,304,128]{2,1,0:T(8,128)(2,1)}), bf16[16,304,128]{2,1,0:T(8,128)(2,1)S(1)}, u32[]{:S(2)}, u32[]{:S(2)}) async-start(bf16[16,304,128]{2,1,0:T(8,128)(2,1)} %shard_map.82), calls=%async_computation | async-start | bytes 2490368 | tf_op jit(solution)/shard_map/all_to_all | solution.py:543
  10.5 24.4 %copy-start.2 = (bf16[216,288]{1,0:T(8,128)(2,1)S(1)}, bf16[216,288]{1,0:T(8,128)(2,1)}, u32[]{:S(2)}) copy-start(bf16[216,288]{1,0:T(8,128)(2,1)} %constant.34.clone.table) | copy-start | bytes 373252
  25.3 9.6 %collective-permute-start = (bf16[16,304,128]{2,1,0:T(8,128)(2,1)S(1)}, bf16[16,304,128]{2,1,0:T(8,128)(2,1)S(1)}, u32[]{:S(2)}, u32[]{:S(2)}) collective-permute-start(bf16[16,304,128]{2,1,0:T(8,128)(2,1)S(1)} %all-to-all-done.own), channel_id=1, source_target_pairs={{0,8},{8,0},{1,9},{9,1},{2,10},{10,2},{3,11},{11,3},{4,12},{12,4},... | collective-permute-start | bytes 3735560 | tf_op jit(solution)/shard_map/ppermute | solution.py:421
  40.8 12.3 %all-to-all-start.1 = ((f32[32,8,128]{2,1,0:T(8,128)}), f32[32,8,128]{2,1,0:T(8,128)}, u32[]{:S(2)}, u32[]{:S(2)}) async-start(f32[32,8,128]{2,1,0:T(8,128)} %get-tuple-element.20.refs_1_), calls=%async_computation.1 | async-start | bytes 262144 | tf_op jit(solution)/shard_map/all_to_all | solution.py:553
  56.8 72.1 %copy-start = (bf16[4,144,288]{2,1,0:T(8,128)(2,1)S(1)}, bf16[4,144,288]{2,1,0:T(8,128)(2,1)}, u32[]{:S(2)}) copy-start(bf16[4,144,288]{2,1,0:T(8,128)(2,1)} %constant.36.clone.table) | copy-start | bytes 995332
  115.7 16.0 %collective-permute-start.1 = (bf16[4,480,128]{2,1,0:T(8,128)(2,1)S(1)}, bf16[4,480,128]{2,1,0:T(8,128)(2,1)S(1)}, u32[]{:S(2)}, u32[]{:S(2)}) collective-permute-start(bf16[4,480,128]{2,1,0:T(8,128)(2,1)S(1)} %bitcast.11), channel_id=1, source_target_pairs={{0,256},{256,0},{1,257},{257,1},{2,258},{258,2},{3,259},{259,3},{4... | collective-permute-start | bytes 1474568 | tf_op jit(solution)/shard_map/ppermute | solution.py:421

commit v10 on v9

--- a/solution.py
+++ b/solution.py
@@ -510,7 +510,7 @@
         ],
         10**9,
         8 * 10**6,
-        limit=64,
+        limit=48,
     )(all_stats, stats, kept, post, ydata)
 
 

time: 140 us -> 140 us (level)
    all_gather x1, blocking collectives: 10.8 us -> 7.09 us  [body(): result = images(x_lo, lax.all_gather(near, 'core'), inverse, None)]
    all_gather x1, blocking collectives: 26.8 us -> 30.1 us  [body(): near = lax.all_gather(near, 'z_hi')]
where the time goes in v10:
time: 140 us
  blocking collectives  74.5 us (53%)
  Pallas kernels  24.2 us (17%)
  starting transfers between devices  21.6 us (15%)
  waiting for transfers between devices  16.8 us (12%)
  local copies, waits for them, and re-layouts  2.48 us (2%)
    all_gather x1, blocking collectives, body(): near = lax.all_gather(near, 'z_hi')  30.1 us
    all_to_all x1, blocking collectives, body(): near = lax.all_to_all(sums, 'z_lo', 0, 0, tiled=True)  18.3 us
    all_gather x1, blocking collectives, body(): near = lax.all_gather(hat, 'z_lo')  13.6 us
    all_to_all x1, waiting for transfers between devices, body(): own = lax.all_to_all(messages, ('x_lo', 'x_hi', 'y'), 0, 0, tiled=True)  13.6 us
    ppermute x2, starting transfers between devices, swap(): return lax.ppermute(value, axis, [(0, 1), (1, 0)])  9.26 us
    all_to_all x1, starting transfers between devices, body(): own = lax.all_to_all(messages, ('x_lo', 'x_hi', 'y'), 0, 0, tiled=True)  7.73 us
    all_gather x1, blocking collectives, body(): result = images(x_lo, lax.all_gather(near, 'core'), inverse, None)  7.09 us
    pallas_call x1, Pallas kernels, scores(): call(score_kernel, [SMEM] + [VMEM] * 5, [((CORE * SOURCES, 8, LANES), f32...  5.87 us
  transfers between devices with their start and end apart: 4, of which 3 were waited for; matrix products, arithmetic and copies ran while one was open for 1% of the time, Pallas kernels for 7%

profile of v10, /device:TPU:1, one launch (start us, length us, event | category | flops | bytes accessed | tf_op | source)
XLA Modules:
  0.0 139.8 jit_solution(13821241637517901704)
XLA Ops:
  0.0 2.7 %shard_map.82 = bf16[16,304,128]{2,1,0:T(8,128)(2,1)} custom-call(s32[2]{0:T(128)} %ids.1, bf16[2,64,288]{2,1,0:T(8,128)(2,1)} %x.1, f32[32,64]{1,0:T(8,128)} %ctf.1, bf16[3,288,288]{2,1,0:T(8,128)(2,1)} %constant.33.clone.table), custom_call_target="tpu_custom_call" | custom-call | flops 10000000 | bytes 1000000 | tf_op jit(solution)/shard_map/pallas_call | solution.py:425
  2.8 7.7 %all-to-all-start = ((bf16[16,304,128]{2,1,0:T(8,128)(2,1)}), bf16[16,304,128]{2,1,0:T(8,128)(2,1)S(1)}, u32[]{:S(2)}, u32[]{:S(2)}) async-start(bf16[16,304,128]{2,1,0:T(8,128)(2,1)} %shard_map.82), calls=%async_computation | async-start | bytes 2490368 | tf_op jit(solution)/shard_map/all_to_all | solution.py:543
  10.5 1.2 constant_dynamic-slice_fusion.refs
  11.7 13.6 %all-to-all-done.own = bf16[16,304,128]{2,1,0:T(8,128)(2,1)S(1)} async-done(((bf16[16,304,128]{2,1,0:T(8,128)(2,1)}), bf16[16,304,128]{2,1,0:T(8,128)(2,1)S(1)}, u32[]{:S(2)}, u32[]{:S(2)}) %all-to-all-start) | async-done | bytes 1245216 | tf_op jit(solution)/shard_map/all_to_all | solution.py:543
  25.3 7.0 %collective-permute-start = (bf16[16,304,128]{2,1,0:T(8,128)(2,1)S(1)}, bf16[16,304,128]{2,1,0:T(8,128)(2,1)S(1)}, u32[]{:S(2)}, u32[]{:S(2)}) collective-permute-start(bf16[16,304,128]{2,1,0:T(8,128)(2,1)S(1)} %all-to-all-done.own), channel_id=1, source_target_pairs={{0,8},{8,0},{1,9},{9,1},{2,10},{10,2},{3,11},{11,3},{4,12},{12,4},... | collective-permute-start | bytes 3735560 | tf_op jit(solution)/shard_map/ppermute | solution.py:421
  32.4 0.1 pad_add_fusion.place
  32.4 2.2 %shard_map.83 = (bf16[144,16,128]{2,1,0:T(8,128)(2,1)S(1)}, f32[16,128]{1,0:T(8,128)S(1)}) custom-call(bf16[13,64,288]{2,1,0:T(8,128)(2,1)S(1)} %constant_dynamic-slice_fusion.refs, bf16[3,288,288]{2,1,0:T(8,128)(2,1)S(1)} %copy-done.2), custom_call_target="tpu_custom_call" | custom-call | flops 1000000000 | bytes 4000000 | tf_op jit(solution)/shard_map/pallas_call | solution.py:438
  34.6 0.3 collective-permute-done.other
  34.9 5.9 %shard_map.84 = (f32[32,8,128]{2,1,0:T(8,128)}, f32[36000,128]{1,0:T(8,128)}, bf16[1100,64,128]{2,1,0:T(8,128)(2,1)}) custom-call(s32[2]{0:T(128)S(1)} %pad_add_fusion.place, bf16[16,304,128]{2,1,0:T(8,128)(2,1)S(1)} %all-to-all-done.own, bf16[16,304,128]{2,1,0:T(8,128)(2,1)S(1)} %collective-permute-done.other, ...), custom_call_target="tpu_custom_call" | custom-call | flops 1000000000 | bytes 8000000 | tf_op jit(solution)/shard_map/pallas_call | solution.py:454
  40.8 4.6 %all-to-all-start.1 = ((f32[32,8,128]{2,1,0:T(8,128)}), f32[32,8,128]{2,1,0:T(8,128)}, u32[]{:S(2)}, u32[]{:S(2)}) async-start(f32[32,8,128]{2,1,0:T(8,128)} %get-tuple-element.20.refs_1_), calls=%async_computation.1 | async-start | bytes 262144 | tf_op jit(solution)/shard_map/all_to_all | solution.py:553
  45.4 4.7 %shard_map.85.refs_3_ = f32[144,16,128]{2,1,0:T(8,128)} custom-call(f32[36000,128]{1,0:T(8,128)} %get-tuple-element.21.far_kept.refs_2_, bf16[864,72]{1,0:T(8,128)(2,1)} %constant.35.clone.table), custom_call_target="tpu_custom_call" | custom-call | flops 1000000000 | bytes 3000000 | tf_op jit(solution)/shard_map/pallas_call | solution.py:477
  50.1 2.9 %all-to-all-done.1.refs_0_ = f32[32,8,128]{2,1,0:T(8,128)} async-done(((f32[32,8,128]{2,1,0:T(8,128)}), f32[32,8,128]{2,1,0:T(8,128)}, u32[]{:S(2)}, u32[]{:S(2)}) %all-to-all-start.1) | async-done | bytes 131104 | tf_op jit(solution)/shard_map/all_to_all | solution.py:553
  53.1 1.3 copy-done
  54.3 2.8 %shard_map.86 = bf16[4,480,128]{2,1,0:T(8,128)(2,1)S(1)} custom-call(f32[32,8,128]{2,1,0:T(8,128)} %all-to-all-done.1.refs_0_, f32[32,8,128]{2,1,0:T(8,128)} %get-tuple-element.20.refs_1_, f32[36000,128]{1,0:T(8,128)} %get-tuple-element.21.far_kept.refs_2_, f32[144,16,128]{2,1,0:T(8,128)S(1)} %copy-done, bf16[1100,64,128]{2,1,0:T(8,128)(2,1)} %get-tuple-element.22.refs_4_), custom_call_target="tpu_custom_call" | custom-call | flops 1000000000 | bytes 8000000 | tf_op jit(solution)/shard_map/pallas_call | solution.py:495
  57.1 18.3 %all_to_all.15.pieces = bf16[4,480,128]{2,1,0:T(8,128)(2,1)S(1)} all-to-all(bf16[4,480,128]{2,1,0:T(8,128)(2,1)S(1)} %shard_map.86), channel_id=1, replica_groups=mesh['x_lo'=2,'z_hi'=4,'z_lo'=4,'core'=2,'x_hi'=2,'y'=4] {'z_lo'}, dimensions={0} | all-to-all | bytes 983040 | tf_op jit(solution)/shard_map/all_to_all | solution.py:557
  75.4 0.1 shard_map.87
  75.5 30.1 %all-gather = bf16[1920,128]{1,0:T(8,128)(2,1)S(1)} all-gather(bf16[480,128]{1,0:T(8,128)(2,1)S(1)} %shard_map.87), channel_id=2, replica_groups=mesh['x_lo'=2,'z_hi'=4,'z_lo'=4,'core'=2,'x_hi'=2,'y'=4] {'z_hi'}, dimensions={0}, use_global_device_ids=true | all-gather | bytes 614400 | tf_op jit(solution)/shard_map/all_gather | solution.py:559
  105.6 0.2 shard_map.88
  105.8 13.6 %all-gather.1 = bf16[1920,128]{1,0:T(8,128)(2,1)S(1)} all-gather(bf16[480,128]{1,0:T(8,128)(2,1)S(1)} %shard_map.88), channel_id=3, replica_groups=mesh['x_lo'=2,'z_hi'=4,'z_lo'=4,'core'=2,'x_hi'=2,'y'=4] {'z_lo'}, dimensions={0}, use_global_device_ids=true | all-gather | bytes 614400 | tf_op jit(solution)/shard_map/all_gather | solution.py:563
  119.4 2.2 %collective-permute-start.1 = (bf16[4,480,128]{2,1,0:T(8,128)(2,1)S(1)}, bf16[4,480,128]{2,1,0:T(8,128)(2,1)S(1)}, u32[]{:S(2)}, u32[]{:S(2)}) collective-permute-start(bf16[4,480,128]{2,1,0:T(8,128)(2,1)S(1)} %bitcast.11), channel_id=1, source_target_pairs={{0,256},{256,0},{1,257},{257,1},{2,258},{258,2},{3,259},{259,3},{4... | collective-permute-start | bytes 1474568 | tf_op jit(solution)/shard_map/ppermute | solution.py:421
  121.6 7.1 %all-gather.2 = bf16[8,480,128]{2,1,0:T(8,128)(2,1)S(1)} all-gather(bf16[4,480,128]{2,1,0:T(8,128)(2,1)S(1)} %bitcast.12), channel_id=4, replica_groups=mesh['x_lo'=2,'z_hi'=4,'z_lo'=4,'core'=2,'x_hi'=2,'y'=4] {'core'}, dimensions={0}, use_global_device_ids=true | all-gather | bytes 1474560 | tf_op jit(solution)/shard_map/all_gather | solution.py:565
  128.7 2.8 %shard_map.89.refs_0_ = bf16[50,64,288]{2,1,0:T(8,128)(2,1)} custom-call(s32[1]{0:T(128)} %bitcast.3.place, bf16[4,144,288]{2,1,0:T(8,128)(2,1)S(1)} %copy-done.1, bf16[2,4,480,128]{3,2,1,0:T(8,128)(2,1)S(1)} %bitcast.9), custom_call_target="tpu_custom_call" | custom-call | flops 1000 | bytes 1000 | tf_op jit(solution)/shard_map/pallas_call | solution.py:519
  131.5 5.5 %all-gather.3 = bf16[8,480,128]{2,1,0:T(8,128)(2,1)S(1)} all-gather(bf16[4,480,128]{2,1,0:T(8,128)(2,1)S(1)} %collective-permute-done.1), channel_id=5, replica_groups=mesh['x_lo'=2,'z_hi'=4,'z_lo'=4,'core'=2,'x_hi'=2,'y'=4] {'core'}, dimensions={0}, use_global_device_ids=true | all-gather | bytes 1474560 | tf_op jit(solution)/shard_map/all_gather | solution.py:567
  137.0 2.8 %shard_map.90 = bf16[50,64,288]{2,1,0:T(8,128)(2,1)} custom-call(s32[1]{0:T(128)} %bitcast.place, bf16[4,144,288]{2,1,0:T(8,128)(2,1)S(1)} %copy-done.1, bf16[2,4,480,128]{3,2,1,0:T(8,128)(2,1)S(1)} %bitcast.8, bf16[50,64,288]{2,1,0:T(8,128)(2,1)} %shard_map.89.refs_0_), custom_call_target="tpu_custom_call", output_to_operand_aliasing={{}: (3, {})} | custom-call | flops 1000 | bytes 1000 | tf_op jit(solution)/shard_map/pallas_call | solution.py:519
  (8 shorter events, 0.0 us)
Async XLA Ops:
  2.8 29.7 %copy-start.2 = (bf16[3,288,288]{2,1,0:T(8,128)(2,1)S(1)}, bf16[3,288,288]{2,1,0:T(8,128)(2,1)}, u32[]{:S(2)}) copy-start(bf16[3,288,288]{2,1,0:T(8,128)(2,1)} %constant.33.clone.table) | copy-start | bytes 1492996
  2.8 22.5 %all-to-all-start = ((bf16[16,304,128]{2,1,0:T(8,128)(2,1)}), bf16[16,304,128]{2,1,0:T(8,128)(2,1)S(1)}, u32[]{:S(2)}, u32[]{:S(2)}) async-start(bf16[16,304,128]{2,1,0:T(8,128)(2,1)} %shard_map.82), calls=%async_computation | async-start | bytes 2490368 | tf_op jit(solution)/shard_map/all_to_all | solution.py:543
  10.5 24.4 %copy-start.3 = (bf16[216,288]{1,0:T(8,128)(2,1)S(1)}, bf16[216,288]{1,0:T(8,128)(2,1)}, u32[]{:S(2)}) copy-start(bf16[216,288]{1,0:T(8,128)(2,1)} %constant.34.clone.table) | copy-start | bytes 373252
  25.3 9.6 %collective-permute-start = (bf16[16,304,128]{2,1,0:T(8,128)(2,1)S(1)}, bf16[16,304,128]{2,1,0:T(8,128)(2,1)S(1)}, u32[]{:S(2)}, u32[]{:S(2)}) collective-permute-start(bf16[16,304,128]{2,1,0:T(8,128)(2,1)S(1)} %all-to-all-done.own), channel_id=1, source_target_pairs={{0,8},{8,0},{1,9},{9,1},{2,10},{10,2},{3,11},{11,3},{4,12},{12,4},... | collective-permute-start | bytes 3735560 | tf_op jit(solution)/shard_map/ppermute | solution.py:421
  40.8 12.3 %all-to-all-start.1 = ((f32[32,8,128]{2,1,0:T(8,128)}), f32[32,8,128]{2,1,0:T(8,128)}, u32[]{:S(2)}, u32[]{:S(2)}) async-start(f32[32,8,128]{2,1,0:T(8,128)} %get-tuple-element.20.refs_1_), calls=%async_computation.1 | async-start | bytes 262144 | tf_op jit(solution)/shard_map/all_to_all | solution.py:553
  53.1 1.3 copy-start
  57.1 71.6 %copy-start.1 = (bf16[4,144,288]{2,1,0:T(8,128)(2,1)S(1)}, bf16[4,144,288]{2,1,0:T(8,128)(2,1)}, u32[]{:S(2)}) copy-start(bf16[4,144,288]{2,1,0:T(8,128)(2,1)} %constant.36.clone.table) | copy-start | bytes 995332
  119.4 12.2 %collective-permute-start.1 = (bf16[4,480,128]{2,1,0:T(8,128)(2,1)S(1)}, bf16[4,480,128]{2,1,0:T(8,128)(2,1)S(1)}, u32[]{:S(2)}, u32[]{:S(2)}) collective-permute-start(bf16[4,480,128]{2,1,0:T(8,128)(2,1)S(1)} %bitcast.11), channel_id=1, source_target_pairs={{0,256},{256,0},{1,257},{257,1},{2,258},{258,2},{3,259},{259,3},{4... | collective-permute-start | bytes 1474568 | tf_op jit(solution)/shard_map/ppermute | solution.py:421
